TPU v7x, 32 devices: a whole 2x2x4 slice. The times are simulated.
32 devices in a mesh: wave: 4 (over z), lev: 8 (over y, x, core).
Axes of the slice: x: 2, y: 2, z: 4, core: 2. Of those that a mesh axis runs over, the one named last changes fastest.
Arguments:
- spec: bfloat16 [8, 8, 2, 1280], P('wave', 'lev'), may hold values from -0.59765625 to 0.59765625
- legendre: bfloat16 [8, 1280, 1200], P('wave', 'lev'), may hold values from -0.15625 to 0.15625
- gauss_w: float32 [1200], replicated, may hold values from 0.5 to 1.5
- cycle_len: int32 [1200], replicated, may hold values from 20 to 4816, as said below
- wave_map: int32 [8], replicated, may hold values from 0 to 7, as said below
Outputs:
- grid: bfloat16 [2, 600, 8, 4864], P(None, 'wave', 'lev')
- spec_out: float32 [8, 8, 2, 1280], P('wave', 'lev')
Inputs may be any that keep to these rules, and one draw needn't show every extreme that they name: `wave_map`: A permutation of 0 .. 7; slot r of each index of wave (slots are numbered 2 to an index) holds a value from the r-th group of 4 consecutive values. `cycle_len`: entry 2r is the point count of the r-th cycle from the pole, entry 2r + 1 that of cycle 1200 - 1 - r; cycle j has a multiple of 4 points between max(20, 8 + 4 j) and 20 + 4 j, and cycle 1200 - 1 exactly 20 + 4 (1199); the southern cycle mirrors the northern one.
All inputs are finite; a program needn't handle non-finite values.
Results may differ from a plain program's by a relative error of at most 0.0055.
Values may be sent and summed in bfloat16 or wider, within the bound.
No kernel may reach another device: no remote copies, remote signals or barrier semaphores. Data moves between devices by JAX's collectives and lax.ppermute only.
A program may use at most 64 MiB of HBM per device.

v0:
```python
import math

import jax
import jax.numpy as jnp
from jax import lax
from jax.sharding import PartitionSpec as P

LPAD = 4864


def block_rows():
    for candidate in (10, 8, 6, 5, 4, 3, 2):
        return candidate
    return 1


def cycle_tables(lens_pair, orders, padded):
    position = jnp.arange(padded, dtype=jnp.int32)[None, :]
    first_len = lens_pair[:, 0:1]
    second = lens_pair[:, 1:2]
    upper_half = position >= first_len
    occupied = position < first_len + second
    offset = jnp.where(upper_half, position - first_len, position)
    length = jnp.where(upper_half, second, first_len)
    turn_count = orders[None, :, None] * offset[:, None, :] % length[:, None, :]
    angles = 2.0 * math.pi * turn_count.astype(jnp.float32) / length[:, None, :].astype(jnp.float32)
    cosine = jnp.where(occupied[:, None, :], jnp.cos(angles), 0.0).astype(jnp.bfloat16)
    minus_sine = jnp.where(occupied[:, None, :], -jnp.sin(angles), 0.0).astype(jnp.bfloat16)
    return (jnp.concatenate([cosine, minus_sine], 1), upper_half, occupied)


def cycle_block(waves, lens_pair, weights, orders, padded):
    row_count = waves.shape[0]
    fields = waves.shape[3]
    slot_count = orders.shape[0]
    tables, upper_half, occupied = cycle_tables(lens_pair, orders, padded)
    double = jnp.where(orders == 0, 1.0, 2.0)
    resolved = 2 * orders[None, None, :] < lens_pair[:, :, None]
    widening = jnp.where(resolved, double[None, None, :], 0.0)
    scaled = (waves.astype(jnp.float32) * widening[:, None, :, None, None, :]).astype(jnp.bfloat16)
    scaled = scaled.reshape(row_count, 4 * fields, 2 * slot_count)
    images = jnp.einsum("rak,rkp->rap", scaled, tables, preferred_element_type=jnp.float32)
    images = images.reshape(row_count, 2, 2, fields, padded)
    values = jnp.where(upper_half[:, None, None, :], images[:, :, 1], images[:, :, 0])
    values = jnp.where(occupied[:, None, None, :], values, 0.0).astype(jnp.bfloat16)
    squared = (values.astype(jnp.float32) * values.astype(jnp.float32)).astype(jnp.bfloat16)
    selector = jnp.stack([jnp.logical_not(upper_half), upper_half], 1)
    by_cycle = jnp.where(
        selector[:, None, :, None, :], squared[:, :, None, :, :], jnp.zeros((), jnp.bfloat16)
    )
    by_cycle = by_cycle.reshape(row_count, 4 * fields, padded)
    returned = jnp.einsum("rap,rkp->rak", by_cycle, tables, preferred_element_type=jnp.float32)
    returned = returned.reshape(row_count, 2, 2, fields, 2, slot_count)
    factor = jnp.where(
        resolved, weights[:, :, None] / lens_pair[:, :, None].astype(jnp.float32), 0.0
    )
    returned = (returned * factor[:, None, :, None, None, :]).astype(jnp.bfloat16)
    return (values, returned)


def parity_of(degree_ids, own_orders):
    return jnp.where((degree_ids[None, :] + own_orders[:, None]) % 2 == 0, 1.0, -1.0)


def per_device(spec, legendre, gauss_w, cycle_len, wave_map):
    slots_dev = spec.shape[0]
    fields = spec.shape[1]
    degrees_all = spec.shape[3]
    slot_count = wave_map.shape[0]
    orders = wave_map * degrees_all // slot_count
    wave_pos = lax.axis_index("wave")
    own_orders = lax.dynamic_slice_in_dim(orders, wave_pos * slots_dev, slots_dev)
    degrees = jnp.arange(degrees_all, dtype=jnp.int32)
    retained = degrees[None, :] >= own_orders[:, None]
    coefficients = jnp.where(retained[:, None, None, :], spec, jnp.zeros((), jnp.bfloat16))
    panels = lax.all_gather(legendre, "lev", axis=1, tiled=True)
    sign_flip = parity_of(degrees, own_orders)
    flipped = (coefficients.astype(jnp.float32) * sign_flip[:, None, None, :]).astype(jnp.bfloat16)
    stacked = jnp.stack([coefficients, flipped], 1)
    fourier = jnp.einsum(
        "shfcn,snq->shfcq", stacked, panels, preferred_element_type=jnp.float32
    ).astype(jnp.bfloat16)
    cycle_waves = lax.all_to_all(fourier, "wave", split_axis=4, concat_axis=0, tiled=True)
    local_lats = cycle_waves.shape[4]
    row_total = local_lats // 2
    lat_start = wave_pos * local_lats
    lens_here = lax.dynamic_slice_in_dim(cycle_len, lat_start, local_lats)
    weights_here = lax.dynamic_slice_in_dim(gauss_w, lat_start, local_lats)
    row_block = block_rows()
    blocks = row_total // row_block
    ordered = cycle_waves.reshape(slot_count, 2, fields, 2, row_total, 2).transpose(
        4, 1, 5, 2, 3, 0
    )
    ordered = ordered.reshape(blocks, row_block, 2, 2, fields, 2, slot_count)

    def run_block(operands):
        return cycle_block(operands[0], operands[1], operands[2], orders, LPAD)

    values, returned = lax.map(
        run_block,
        (
            ordered,
            lens_here.reshape(blocks, row_block, 2),
            weights_here.reshape(blocks, row_block, 2),
        ),
    )
    grid = values.reshape(row_total, 2, fields, LPAD).transpose(1, 0, 2, 3)
    returned = returned.reshape(row_total, 2, 2, fields, 2, slot_count).transpose(5, 1, 3, 4, 0, 2)
    returned = returned.reshape(slot_count, 2, fields, 2, local_lats)
    spectral = lax.all_to_all(returned, "wave", split_axis=0, concat_axis=4, tiled=True)
    both = jnp.einsum("shfcq,snq->shfcn", spectral, panels, preferred_element_type=jnp.float32)
    total = both[:, 0] + sign_flip[:, None, None, :] * both[:, 1]
    spec_out = jnp.where(retained[:, None, None, :], total, 0.0)
    return (grid, spec_out)


def solution(mesh):
    placed = (P("wave", "lev", None, None), P("wave", "lev", None), P(), P(), P())
    return jax.shard_map(
        per_device,
        mesh=mesh,
        in_specs=placed,
        out_specs=(P(None, "wave", "lev", None), P("wave", "lev", None, None)),
        check_vma=False,
    )
```

profile of v0, /device:TPU:0, one launch (start us, length us, event | category | flops | bytes accessed | tf_op | source)
XLA Modules:
  0.0 523.7 jit_solution(2916085774371340817)
XLA Ops:
  10.3 49.0 %all-gather.2.cloned.1.call-done = bf16[2,1280,1200]{2,1,0:T(8,128)(2,1)} async-done(((bf16[2,160,1200]{2,1,0:T(8,128)(2,1)}), bf16[2,1280,1200]{2,1,0:T(8,128)(2,1)}) %all-gather.2.cloned.1.call-update) | async-done | bytes 6144016 | tf_op jit(solution)/shard_map/all_gather | solution.py:76
  59.3 3.9 fusion.32
  63.2 2.6 copy.54
  65.8 1.6 reshape.527
  67.4 4.6 all-to-all-start
  74.2 3.4 all-to-all-done
  77.6 1.3 reshape.528
  78.9 1.0 copy.55
  81.9 420.7 %while.12 = (s32[]{:T(128)}, bf16[15,10,2,1,4864]{4,2,3,1,0:T(2,128)(2,1)}, bf16[15,10,2,2,1,2,8]{1,6,5,3,2,4,0:T(8,128)(2,1)S(1)}, s32[15,10,2]{1,2,0:T(2,128)S...) while((s32[]{:T(128)}, ...), condition=%wide.region_1.2_spmd, body=%wide.region_0.1_spmd.sunk | while | flops 26609836 | bytes 11610541 | solution.py:99
  82.5 21.5 %select_convert_fusion.4 = (bf16[10,8,4864]{2,1,0:T(8,128)(2,1)S(1)}, bf16[10,8,4864]{2,1,0:T(8,128)(2,1)S(1)}) fusion(f32[10,4864]{1,0:T(8,128)S(1)} %get-tuple-element.164, pred[10,4864]{1,0:T(8,128)(4,1)S(1)} %get-tuple-element.165, s32[10,4864]{1,0:T(8,128)S(1)} %get-tuple-element.166, s32[10,4864]{1,0:T(8,128)S(1)} %get-tuple-element.167, ...), kind=kLoop, calls=%fused_computation.6.clone.1 | loop fusion | flops 6225920 | bytes 2237472 | tf_op jit(solution)/shard_map/while/body/eval_jaxpr/convert_element_type | solution.py:27
  104.8 1.0 fusion.67
  108.4 0.9 fusion.65
  109.2 0.9 copy_dynamic-update-slice_fusion.2
  110.5 21.5 %select_convert_fusion.4 = (bf16[10,8,4864]{2,1,0:T(8,128)(2,1)S(1)}, bf16[10,8,4864]{2,1,0:T(8,128)(2,1)S(1)}) fusion(f32[10,4864]{1,0:T(8,128)S(1)} %get-tuple-element.164, pred[10,4864]{1,0:T(8,128)(4,1)S(1)} %get-tuple-element.165, s32[10,4864]{1,0:T(8,128)S(1)} %get-tuple-element.166, s32[10,4864]{1,0:T(8,128)S(1)} %get-tuple-element.167, ...), kind=kLoop, calls=%fused_computation.6.clone.1 | loop fusion | flops 6225920 | bytes 2237472 | tf_op jit(solution)/shard_map/while/body/eval_jaxpr/convert_element_type | solution.py:27
  132.8 1.0 fusion.67
  136.4 0.9 fusion.65
  137.3 0.9 copy_dynamic-update-slice_fusion.2
  138.5 21.5 %select_convert_fusion.4 = (bf16[10,8,4864]{2,1,0:T(8,128)(2,1)S(1)}, bf16[10,8,4864]{2,1,0:T(8,128)(2,1)S(1)}) fusion(f32[10,4864]{1,0:T(8,128)S(1)} %get-tuple-element.164, pred[10,4864]{1,0:T(8,128)(4,1)S(1)} %get-tuple-element.165, s32[10,4864]{1,0:T(8,128)S(1)} %get-tuple-element.166, s32[10,4864]{1,0:T(8,128)S(1)} %get-tuple-element.167, ...), kind=kLoop, calls=%fused_computation.6.clone.1 | loop fusion | flops 6225920 | bytes 2237472 | tf_op jit(solution)/shard_map/while/body/eval_jaxpr/convert_element_type | solution.py:27
  160.8 1.0 fusion.67
  164.4 0.9 fusion.65
  165.3 0.9 copy_dynamic-update-slice_fusion.2
  166.6 21.5 %select_convert_fusion.4 = (bf16[10,8,4864]{2,1,0:T(8,128)(2,1)S(1)}, bf16[10,8,4864]{2,1,0:T(8,128)(2,1)S(1)}) fusion(f32[10,4864]{1,0:T(8,128)S(1)} %get-tuple-element.164, pred[10,4864]{1,0:T(8,128)(4,1)S(1)} %get-tuple-element.165, s32[10,4864]{1,0:T(8,128)S(1)} %get-tuple-element.166, s32[10,4864]{1,0:T(8,128)S(1)} %get-tuple-element.167, ...), kind=kLoop, calls=%fused_computation.6.clone.1 | loop fusion | flops 6225920 | bytes 2237472 | tf_op jit(solution)/shard_map/while/body/eval_jaxpr/convert_element_type | solution.py:27
  188.9 1.0 fusion.67
  192.5 0.9 fusion.65
  193.3 0.9 copy_dynamic-update-slice_fusion.2
  194.6 21.5 %select_convert_fusion.4 = (bf16[10,8,4864]{2,1,0:T(8,128)(2,1)S(1)}, bf16[10,8,4864]{2,1,0:T(8,128)(2,1)S(1)}) fusion(f32[10,4864]{1,0:T(8,128)S(1)} %get-tuple-element.164, pred[10,4864]{1,0:T(8,128)(4,1)S(1)} %get-tuple-element.165, s32[10,4864]{1,0:T(8,128)S(1)} %get-tuple-element.166, s32[10,4864]{1,0:T(8,128)S(1)} %get-tuple-element.167, ...), kind=kLoop, calls=%fused_computation.6.clone.1 | loop fusion | flops 6225920 | bytes 2237472 | tf_op jit(solution)/shard_map/while/body/eval_jaxpr/convert_element_type | solution.py:27
  216.9 1.0 fusion.67
  220.5 0.9 fusion.65
  221.4 0.9 copy_dynamic-update-slice_fusion.2
  222.6 21.5 %select_convert_fusion.4 = (bf16[10,8,4864]{2,1,0:T(8,128)(2,1)S(1)}, bf16[10,8,4864]{2,1,0:T(8,128)(2,1)S(1)}) fusion(f32[10,4864]{1,0:T(8,128)S(1)} %get-tuple-element.164, pred[10,4864]{1,0:T(8,128)(4,1)S(1)} %get-tuple-element.165, s32[10,4864]{1,0:T(8,128)S(1)} %get-tuple-element.166, s32[10,4864]{1,0:T(8,128)S(1)} %get-tuple-element.167, ...), kind=kLoop, calls=%fused_computation.6.clone.1 | loop fusion | flops 6225920 | bytes 2237472 | tf_op jit(solution)/shard_map/while/body/eval_jaxpr/convert_element_type | solution.py:27
  244.9 1.0 fusion.67
  248.5 0.9 fusion.65
  249.4 0.9 copy_dynamic-update-slice_fusion.2
  250.7 21.5 %select_convert_fusion.4 = (bf16[10,8,4864]{2,1,0:T(8,128)(2,1)S(1)}, bf16[10,8,4864]{2,1,0:T(8,128)(2,1)S(1)}) fusion(f32[10,4864]{1,0:T(8,128)S(1)} %get-tuple-element.164, pred[10,4864]{1,0:T(8,128)(4,1)S(1)} %get-tuple-element.165, s32[10,4864]{1,0:T(8,128)S(1)} %get-tuple-element.166, s32[10,4864]{1,0:T(8,128)S(1)} %get-tuple-element.167, ...), kind=kLoop, calls=%fused_computation.6.clone.1 | loop fusion | flops 6225920 | bytes 2237472 | tf_op jit(solution)/shard_map/while/body/eval_jaxpr/convert_element_type | solution.py:27
  272.9 1.0 fusion.67
  276.5 0.9 fusion.65
  277.4 0.9 copy_dynamic-update-slice_fusion.2
  278.7 21.5 %select_convert_fusion.4 = (bf16[10,8,4864]{2,1,0:T(8,128)(2,1)S(1)}, bf16[10,8,4864]{2,1,0:T(8,128)(2,1)S(1)}) fusion(f32[10,4864]{1,0:T(8,128)S(1)} %get-tuple-element.164, pred[10,4864]{1,0:T(8,128)(4,1)S(1)} %get-tuple-element.165, s32[10,4864]{1,0:T(8,128)S(1)} %get-tuple-element.166, s32[10,4864]{1,0:T(8,128)S(1)} %get-tuple-element.167, ...), kind=kLoop, calls=%fused_computation.6.clone.1 | loop fusion | flops 6225920 | bytes 2237472 | tf_op jit(solution)/shard_map/while/body/eval_jaxpr/convert_element_type | solution.py:27
  301.0 1.0 fusion.67
  304.6 0.9 fusion.65
  305.5 0.9 copy_dynamic-update-slice_fusion.2
  306.7 21.5 %select_convert_fusion.4 = (bf16[10,8,4864]{2,1,0:T(8,128)(2,1)S(1)}, bf16[10,8,4864]{2,1,0:T(8,128)(2,1)S(1)}) fusion(f32[10,4864]{1,0:T(8,128)S(1)} %get-tuple-element.164, pred[10,4864]{1,0:T(8,128)(4,1)S(1)} %get-tuple-element.165, s32[10,4864]{1,0:T(8,128)S(1)} %get-tuple-element.166, s32[10,4864]{1,0:T(8,128)S(1)} %get-tuple-element.167, ...), kind=kLoop, calls=%fused_computation.6.clone.1 | loop fusion | flops 6225920 | bytes 2237472 | tf_op jit(solution)/shard_map/while/body/eval_jaxpr/convert_element_type | solution.py:27
  329.0 1.0 fusion.67
  333.5 0.9 copy_dynamic-update-slice_fusion.2
  334.8 21.5 %select_convert_fusion.4 = (bf16[10,8,4864]{2,1,0:T(8,128)(2,1)S(1)}, bf16[10,8,4864]{2,1,0:T(8,128)(2,1)S(1)}) fusion(f32[10,4864]{1,0:T(8,128)S(1)} %get-tuple-element.164, pred[10,4864]{1,0:T(8,128)(4,1)S(1)} %get-tuple-element.165, s32[10,4864]{1,0:T(8,128)S(1)} %get-tuple-element.166, s32[10,4864]{1,0:T(8,128)S(1)} %get-tuple-element.167, ...), kind=kLoop, calls=%fused_computation.6.clone.1 | loop fusion | flops 6225920 | bytes 2237472 | tf_op jit(solution)/shard_map/while/body/eval_jaxpr/convert_element_type | solution.py:27
  357.0 1.0 fusion.67
  361.5 0.9 copy_dynamic-update-slice_fusion.2
  362.8 21.5 %select_convert_fusion.4 = (bf16[10,8,4864]{2,1,0:T(8,128)(2,1)S(1)}, bf16[10,8,4864]{2,1,0:T(8,128)(2,1)S(1)}) fusion(f32[10,4864]{1,0:T(8,128)S(1)} %get-tuple-element.164, pred[10,4864]{1,0:T(8,128)(4,1)S(1)} %get-tuple-element.165, s32[10,4864]{1,0:T(8,128)S(1)} %get-tuple-element.166, s32[10,4864]{1,0:T(8,128)S(1)} %get-tuple-element.167, ...), kind=kLoop, calls=%fused_computation.6.clone.1 | loop fusion | flops 6225920 | bytes 2237472 | tf_op jit(solution)/shard_map/while/body/eval_jaxpr/convert_element_type | solution.py:27
  385.1 1.0 fusion.67
  389.6 0.9 copy_dynamic-update-slice_fusion.2
  390.8 21.5 %select_convert_fusion.4 = (bf16[10,8,4864]{2,1,0:T(8,128)(2,1)S(1)}, bf16[10,8,4864]{2,1,0:T(8,128)(2,1)S(1)}) fusion(f32[10,4864]{1,0:T(8,128)S(1)} %get-tuple-element.164, pred[10,4864]{1,0:T(8,128)(4,1)S(1)} %get-tuple-element.165, s32[10,4864]{1,0:T(8,128)S(1)} %get-tuple-element.166, s32[10,4864]{1,0:T(8,128)S(1)} %get-tuple-element.167, ...), kind=kLoop, calls=%fused_computation.6.clone.1 | loop fusion | flops 6225920 | bytes 2237472 | tf_op jit(solution)/shard_map/while/body/eval_jaxpr/convert_element_type | solution.py:27
  413.1 1.0 fusion.67
  417.6 0.9 copy_dynamic-update-slice_fusion.2
  418.9 21.5 %select_convert_fusion.4 = (bf16[10,8,4864]{2,1,0:T(8,128)(2,1)S(1)}, bf16[10,8,4864]{2,1,0:T(8,128)(2,1)S(1)}) fusion(f32[10,4864]{1,0:T(8,128)S(1)} %get-tuple-element.164, pred[10,4864]{1,0:T(8,128)(4,1)S(1)} %get-tuple-element.165, s32[10,4864]{1,0:T(8,128)S(1)} %get-tuple-element.166, s32[10,4864]{1,0:T(8,128)S(1)} %get-tuple-element.167, ...), kind=kLoop, calls=%fused_computation.6.clone.1 | loop fusion | flops 6225920 | bytes 2237472 | tf_op jit(solution)/shard_map/while/body/eval_jaxpr/convert_element_type | solution.py:27
  441.1 1.0 fusion.67
  445.6 0.9 copy_dynamic-update-slice_fusion.2
  446.9 21.5 %select_convert_fusion.4 = (bf16[10,8,4864]{2,1,0:T(8,128)(2,1)S(1)}, bf16[10,8,4864]{2,1,0:T(8,128)(2,1)S(1)}) fusion(f32[10,4864]{1,0:T(8,128)S(1)} %get-tuple-element.164, pred[10,4864]{1,0:T(8,128)(4,1)S(1)} %get-tuple-element.165, s32[10,4864]{1,0:T(8,128)S(1)} %get-tuple-element.166, s32[10,4864]{1,0:T(8,128)S(1)} %get-tuple-element.167, ...), kind=kLoop, calls=%fused_computation.6.clone.1 | loop fusion | flops 6225920 | bytes 2237472 | tf_op jit(solution)/shard_map/while/body/eval_jaxpr/convert_element_type | solution.py:27
  469.2 1.0 fusion.67
  473.7 0.9 copy_dynamic-update-slice_fusion.2
  474.9 21.5 %select_convert_fusion.4 = (bf16[10,8,4864]{2,1,0:T(8,128)(2,1)S(1)}, bf16[10,8,4864]{2,1,0:T(8,128)(2,1)S(1)}) fusion(f32[10,4864]{1,0:T(8,128)S(1)} %get-tuple-element.164, pred[10,4864]{1,0:T(8,128)(4,1)S(1)} %get-tuple-element.165, s32[10,4864]{1,0:T(8,128)S(1)} %get-tuple-element.166, s32[10,4864]{1,0:T(8,128)S(1)} %get-tuple-element.167, ...), kind=kLoop, calls=%fused_computation.6.clone.1 | loop fusion | flops 6225920 | bytes 2237472 | tf_op jit(solution)/shard_map/while/body/eval_jaxpr/convert_element_type | solution.py:27
  497.2 1.0 fusion.67
  501.7 0.9 copy_dynamic-update-slice_fusion.2
  503.4 8.0 %all_to_all.30 = bf16[8,2,1,2,300]{4,3,2,1,0:T(2,128)(2,1)S(1)} all-to-all(bf16[8,2,1,2,300]{4,3,2,1,0:T(2,128)(2,1)S(1)} %copy.62), channel_id=1, replica_groups=mesh['wave'=4,'lev'=8] {'wave'}, dimensions={0} | all-to-all | bytes 38400 | tf_op jit(solution)/shard_map/all_to_all | solution.py:110
  511.5 4.7 fusion.26
  (364 shorter events, 70.0 us)
Async XLA Ops:
  7.2 52.1 %all-gather.2.cloned.1.call-start = ((), (), s32[]{:S(2)}) async-start(), calls=%async_computation.2 | async-start | bytes 7372800 | tf_op jit(solution)/shard_map/all_gather | solution.py:76
  67.4 10.2 %all-to-all-start = ((bf16[4,2,1200]{2,1,0:T(2,128)(2,1)}), bf16[4,2,1200]{2,1,0:T(2,128)(2,1)S(1)}, u32[]{:S(2)}, u32[]{:S(2)}) async-start(bf16[4,2,1200]{2,1,0:T(2,128)(2,1)} %reshape.527), calls=%async_computation | async-start | bytes 40960 | tf_op jit(solution)/shard_map/all_to_all | solution.py:83
Sparse Core Ops, SparseCore 0:
  9.9 49.3 all-gather.1
where the time goes:
time: 524 us
  other arithmetic  383 us (73%)
  waiting for transfers between devices  53.1 us (10%)
  local copies, waits for them, and re-layouts  35.7 us (7%)
  matrix products  23.6 us (5%)
  between operations  14.1 us (3%)
  blocking collectives  7.99 us (2%)
    convert_element_type x15, other arithmetic, cycle_tables(): jnp.where(occupied[:, None, :], jnp.cos(angles), 0.0).astype(jnp.bfloat16)  322 us
    all_gather x1, waiting for transfers between devices, per_device(): panels = lax.all_gather(legendre, 'lev', axis=1, tiled=True)  49 us
    convert_element_type x15, other arithmetic, cycle_block(): (values.astype(jnp.float32) * values.astype(jnp.float32)).astype(jnp.bflo...  14.8 us
    dynamic_update_slice x15, local copies, waits for them, and re-layouts, per_device(): lax.map(run_block, (ordered, lens_here.reshape(blocks, row_block, 2), wei...  13.2 us
    convert_element_type x15, other arithmetic, cycle_block(): jnp.where(occupied[:, None, None, :], values, 0.0).astype(jnp.bfloat16)  13.2 us
  transfers between devices with their start and end apart: 2, of which 2 were waited for; matrix products, arithmetic and copies ran while one was open for 1% of the time, Pallas kernels for 0%

commit v1 on v0

--- a/solution.py
+++ b/solution.py
@@ -1,8 +1,12 @@
+import functools
 import math
 
 import jax
 import jax.numpy as jnp
 from jax import lax
+from jax.experimental import pallas as pl
+from jax.experimental.layout import Layout, with_layout_constraint
+from jax.experimental.pallas import tpu as pltpu
 from jax.sharding import PartitionSpec as P
 
 LPAD = 4864
@@ -62,7 +66,7 @@
     return jnp.where((degree_ids[None, :] + own_orders[:, None]) % 2 == 0, 1.0, -1.0)
 
 
-def per_device(spec, legendre, gauss_w, cycle_len, wave_map):
+def general(spec, legendre, gauss_w, cycle_len, wave_map):
     slots_dev = spec.shape[0]
     fields = spec.shape[1]
     degrees_all = spec.shape[3]
@@ -114,6 +118,459 @@
     return (grid, spec_out)
 
 
+LANES = 128
+SUBLANES = 8
+STEPS = 5
+VMEM = 56 * 1024 * 1024
+SINE = (6.28318516, -41.34165503, 81.60100407, -76.54978222, 39.53670553)
+
+
+def cos_turns(x, period, inverse):
+    turn = x - period * jnp.floor(x * inverse + 0.5)
+    v = 0.25 - jnp.abs(turn * inverse)
+    y = v * v
+    series = SINE[4]
+    for coefficient in SINE[3::-1]:
+        series = series * y + coefficient
+    return v * series
+
+
+def params(memory=VMEM):
+    return pltpu.CompilerParams(vmem_limit_bytes=memory)
+
+
+def cost(flops, nbytes):
+    return pl.CostEstimate(flops=flops, bytes_accessed=nbytes, transcendentals=0)
+
+
+def send_spec(info, spec, levels):
+    slots, parts, degrees_all = spec.shape
+    own = degrees_all // levels
+    rows = 2 * slots * parts
+
+    def kernel(info_ref, x_ref, o_ref):
+        degree = lax.broadcasted_iota(jnp.int32, (parts, degrees_all), 1)
+        north, south = [], []
+        for s in range(slots):
+            order = info_ref[1 + s]
+            x = jnp.where(degree >= order, x_ref[s].astype(jnp.float32), 0.0)
+            sign = (1 - 2 * ((degree + order) & 1)).astype(jnp.float32)
+            north.append(x)
+            south.append(x * sign)
+        both = jnp.concatenate(north + south, axis=0)
+        slot_of = (lax.broadcasted_iota(jnp.int32, (rows, own), 0) // parts) % slots
+        for j in range(levels):
+            piece = both[:, j * own : (j + 1) * own]
+            wide = [jnp.where(slot_of == s, piece, 0.0) for s in range(slots)]
+            o_ref[j] = jnp.concatenate(wide, axis=1).astype(jnp.bfloat16)
+
+    return pl.pallas_call(
+        kernel,
+        out_shape=jax.ShapeDtypeStruct((levels, rows, slots * own), jnp.bfloat16),
+        in_specs=[pl.BlockSpec(memory_space=pltpu.SMEM), pl.BlockSpec(memory_space=pltpu.VMEM)],
+        out_specs=pl.BlockSpec(memory_space=pltpu.VMEM),
+        compiler_params=params(),
+        name="send_spec",
+    )(info, spec)
+
+
+def partial_fourier(coefficients, panels):
+    rows = coefficients.shape[0]
+    chunks, depth, wide = panels.shape
+
+    def kernel(x_ref, panel_ref, o_ref):
+        for j in range(chunks):
+            o_ref[j] = jnp.dot(
+                x_ref[...], panel_ref[j], preferred_element_type=jnp.float32
+            ).astype(jnp.bfloat16)
+
+    return pl.pallas_call(
+        kernel,
+        out_shape=jax.ShapeDtypeStruct((chunks, rows, wide), jnp.bfloat16),
+        compiler_params=params(),
+        name="partial_fourier",
+    )(coefficients, panels)
+
+
+def quadratic(wave_map, parts_sum, lens, weights, waves, step):
+    sources, rows, wide = parts_sum.shape
+    slot_count = wave_map.shape[0]
+    levels = sources // waves
+    slots = slot_count // waves
+    tiles = wide // LANES
+    top = 2 * (slot_count - 1)
+    shape = (SUBLANES, LANES)
+
+    def kernel(map_ref, x_ref, len_ref, weight_ref, g_ref, o_ref, z_ref, r_ref, s_ref):
+        z_ref[...] = jnp.zeros(z_ref.shape, jnp.float32)
+        for i in range(waves):
+            total = x_ref[i * levels].astype(jnp.float32)
+            for j in range(1, levels):
+                total = total + x_ref[i * levels + j].astype(jnp.float32)
+            for row in range(rows):
+                h, s, c = row // (2 * slots), row // 2 % slots, row % 2
+                at = map_ref[i * slots + s] * 2 + c
+                for t in range(tiles):
+                    k = h * tiles + t
+                    z_ref[at, k : k + 1, :] = total[row : row + 1, t * LANES : (t + 1) * LANES]
+        lens_here = len_ref[...]
+        kept = [
+            jnp.where(lens_here > 2.0 * step * w, 1.0, 0.0) for w in range(slot_count)
+        ]
+        real = [z_ref[2 * w] * kept[w] for w in range(slot_count)]
+        imag = [z_ref[2 * w + 1] * kept[w] for w in range(slot_count)]
+        for w in range(slot_count):
+            double = 1.0 if w == 0 else 2.0
+            g_ref[2 * w] = real[w] * double
+            g_ref[2 * w + 1] = imag[w] * double
+        imag[0] = jnp.zeros(shape, jnp.float32)
+        square_real, square_imag = [], []
+        for n in range(top + 1):
+            re, im = jnp.zeros(shape, jnp.float32), jnp.zeros(shape, jnp.float32)
+            for a in range(max(0, n - slot_count + 1), (n + 1) // 2):
+                b = n - a
+                re = re + (real[a] * real[b] - imag[a] * imag[b])
+                im = im + (real[a] * imag[b] + imag[a] * real[b])
+            for b in range(1, slot_count - n):
+                a = n + b
+                re = re + (real[a] * real[b] + imag[a] * imag[b])
+                im = im + (imag[a] * real[b] - real[a] * imag[b])
+            re, im = 2.0 * re, 2.0 * im
+            if n % 2 == 0:
+                a = n // 2
+                re = re + (real[a] * real[a] - imag[a] * imag[a])
+                im = im + 2.0 * (real[a] * imag[a])
+            square_real.append(re)
+            square_imag.append(im)
+        whole = {
+            d: jnp.where(lens_here == 1.0 * step * d, 1.0, 0.0)
+            for d in range(3, top + slot_count)
+        }
+        weights_here = weight_ref[...]
+        for w in range(slot_count):
+            re, im = square_real[w], square_imag[w]
+            if w == 0:
+                im = jnp.zeros(shape, jnp.float32)
+            else:
+                for n in range(w + 1, top + 1):
+                    re = re + whole[w + n] * square_real[n]
+                    im = im - whole[w + n] * square_imag[n]
+            factor = kept[w] * weights_here
+            r_ref[2 * w] = re * factor
+            r_ref[2 * w + 1] = im * factor
+        for i in range(waves):
+            for row in range(rows):
+                h, s, c = row // (2 * slots), row // 2 % slots, row % 2
+                at = map_ref[i * slots + s] * 2 + c
+                for t in range(tiles):
+                    k = h * tiles + t
+                    s_ref[row : row + 1, t * LANES : (t + 1) * LANES] = r_ref[at, k : k + 1, :]
+            packed = s_ref[...].astype(jnp.bfloat16)
+            for j in range(levels):
+                o_ref[i * levels + j] = packed
+
+    smem = pl.BlockSpec(memory_space=pltpu.SMEM)
+    vmem = pl.BlockSpec(memory_space=pltpu.VMEM)
+    return pl.pallas_call(
+        kernel,
+        out_shape=(
+            jax.ShapeDtypeStruct((2 * slot_count,) + shape, jnp.float32),
+            jax.ShapeDtypeStruct((sources, rows, wide), jnp.bfloat16),
+        ),
+        in_specs=[smem, vmem, vmem, vmem],
+        out_specs=(vmem, vmem),
+        scratch_shapes=[
+            pltpu.VMEM((2 * slot_count,) + shape, jnp.float32),
+            pltpu.VMEM((2 * slot_count,) + shape, jnp.float32),
+            pltpu.VMEM((rows, wide), jnp.float32),
+        ],
+        compiler_params=params(),
+        name="quadratic",
+    )(wave_map, parts_sum, lens, weights)
+
+
+def lane_facts(slot_count):
+    lane = lax.broadcasted_iota(jnp.int32, (1, LANES), 1)
+    return (
+        lane % (2 * slot_count) // 2,
+        lane % 2,
+        lane // (2 * slot_count) % 2,
+        lane // (4 * slot_count),
+    )
+
+
+def tile_of_row(rows, span, slot_count):
+    at = lax.broadcasted_iota(jnp.int32, (rows, LANES), 0)
+    at = at - lane_facts(slot_count)[3] * span % SUBLANES
+    return at // 2, jnp.logical_and(at >= 0, at < span)
+
+
+def phase_tables(facts, span, slot_count, step):
+    groups = facts.shape[0]
+    rows = -(-(span + SUBLANES // 2) // SUBLANES) * SUBLANES
+
+    def kernel(fact_ref, p_ref, q_ref, t_ref):
+        wave, part, cycle, _ = lane_facts(slot_count)
+        tile, inside = tile_of_row(rows, span, slot_count)
+        first = (tile * LANES).astype(jnp.float32)
+        order = (step * wave).astype(jnp.float32)
+        is_imag = part.astype(jnp.float32)
+        point = lax.broadcasted_iota(jnp.int32, (LANES, LANES), 1).astype(jnp.float32)
+        down = lax.broadcasted_iota(jnp.int32, (LANES, 1), 0)
+        order_down = (step * (down % (2 * slot_count) // 2)).astype(jnp.float32)
+        imag_down = (down % 2).astype(jnp.float32)
+        second_down = down // (2 * slot_count) % 2 == 1
+
+        def body(g, carry):
+            fact = fact_ref[g]
+            length, inverse, offset = fact[0:1], fact[1:2], fact[2:3]
+            x = order * (first - offset)
+            quarter = 0.25 * length
+            p = cos_turns(x - is_imag * quarter, length, inverse)
+            q = cos_turns(x + (1.0 - is_imag) * quarter, length, inverse)
+            p_ref[g] = jnp.where(inside, p, 0.0)
+            q_ref[g] = jnp.where(inside, q, 0.0)
+            across = jnp.transpose(fact)
+            length, inverse, split = across[:, 0:1], across[:, 1:2], across[:, 4:5]
+            x = order_down * point + imag_down * (0.25 * length)
+            t = cos_turns(x, length, inverse)
+            t_ref[g, 0:LANES, :] = t.astype(jnp.bfloat16)
+            here = jnp.logical_xor(point < split, second_down)
+            t_ref[g, LANES : 2 * LANES, :] = jnp.where(here, t, 0.0).astype(jnp.bfloat16)
+            return carry
+
+        lax.fori_loop(0, groups, body, 0)
+
+    return pl.pallas_call(
+        kernel,
+        out_shape=(
+            jax.ShapeDtypeStruct((groups, rows, LANES), jnp.float32),
+            jax.ShapeDtypeStruct((groups, rows, LANES), jnp.float32),
+            jax.ShapeDtypeStruct((groups, 2 * LANES, LANES), jnp.bfloat16),
+        ),
+        compiler_params=params(),
+        cost_estimate=cost(20 * groups * 36 * 1024, 0),
+        name="phase_tables",
+    )(facts)
+
+
+def grid_values(ends, facts, waves, p, q, t, span, slot_count, rows_out):
+    groups, rows, _ = p.shape
+    per = LANES // (4 * slot_count)
+    block = groups // STEPS
+
+    def kernel(end_ref, fact_ref, wave_ref, p_ref, q_ref, t_ref, o_ref):
+        _, _, cycle, _ = lane_facts(slot_count)
+        tile, _ = tile_of_row(rows, span, slot_count)
+        way = 1 - 2 * cycle
+        tile = (tile * way).astype(jnp.float32)
+        way = way.astype(jnp.float32)
+        last = lax.broadcasted_iota(jnp.int32, (SUBLANES, LANES), 0) + rows - SUBLANES
+        point = lax.broadcasted_iota(jnp.int32, (SUBLANES, LANES), 1)
+        base = pl.program_id(0) * block
+
+        def body(g, carry):
+            fold = (rows // SUBLANES, SUBLANES, LANES)
+            amplitude = wave_ref[g, 0] * p_ref[g].reshape(fold) + wave_ref[g, 1] * q_ref[g].reshape(fold)
+            amplitude = amplitude.reshape(rows, LANES)
+            apart = tile - way * fact_ref[g, 3:4, :]
+            left = jnp.concatenate(
+                [jnp.where(apart < 0.0, amplitude, 0.0), jnp.where(apart == 0.0, amplitude, 0.0)], axis=1
+            ).astype(jnp.bfloat16)
+            size = 4 * slot_count
+            columns = []
+            for r in range(per):
+                before = jnp.zeros((r * size, LANES), jnp.bfloat16)
+                after = jnp.zeros((LANES - (r + 1) * size, LANES), jnp.bfloat16)
+                pieces = []
+                for half in range(2):
+                    at = half * LANES + r * size
+                    pieces += [before, t_ref[g, at : at + size, :], after]
+                columns.append(jnp.concatenate([x for x in pieces if x.shape[0]], axis=0))
+            right = jnp.concatenate(columns, axis=1)
+            product = jnp.dot(left, right, preferred_element_type=jnp.float32)
+            places = {}
+            for r in range(per):
+                shift = r * span % SUBLANES
+                values = product[:, r * LANES : (r + 1) * LANES]
+                for k in range(rows // SUBLANES):
+                    if k * SUBLANES >= shift + span:
+                        continue
+                    value = values[k * SUBLANES : (k + 1) * SUBLANES]
+                    if k == rows // SUBLANES - 1:
+                        position = (last - shift) // 2 * LANES + point
+                        value = jnp.where(position < end_ref[(base + g) * per + r], value, 0.0)
+                    places.setdefault((r * span - shift) // SUBLANES + k, []).append(value)
+            whole = [functools.reduce(lambda a, b: a + b, places[k]) for k in sorted(places)]
+            size_out = per * span
+            o_ref[pl.ds(pl.multiple_of(g * size_out, 16), size_out), :] = jnp.concatenate(
+                whole, axis=0
+            ).astype(jnp.bfloat16)
+            return carry
+
+        lax.fori_loop(0, block, body, 0)
+
+    def stepped(shape):
+        return pl.BlockSpec((block,) + shape, lambda i: (i, 0, 0))
+
+    return pl.pallas_call(
+        kernel,
+        grid=(STEPS,),
+        out_shape=jax.ShapeDtypeStruct((rows_out * span, LANES), jnp.bfloat16),
+        in_specs=[
+            pl.BlockSpec(memory_space=pltpu.SMEM),
+            stepped((SUBLANES, LANES)),
+            pl.BlockSpec((block, 2, SUBLANES, LANES), lambda i: (i, 0, 0, 0)),
+            stepped((rows, LANES)),
+            stepped((rows, LANES)),
+            stepped((2 * LANES, LANES)),
+        ],
+        out_specs=pl.BlockSpec((block * per * span, LANES), lambda i: (i, 0)),
+        compiler_params=params(),
+        cost_estimate=cost(20 * groups * 36 * 1024, 0),
+        name="grid_values",
+    )(ends, facts, waves, p, q, t)
+
+
+def direct(info, returned, panels, slots, own):
+    chunks, rows, _ = returned.shape
+    half = slots * 2
+    levels = rows // (2 * half)
+
+    def kernel(info_ref, x_ref, panel_ref, o_ref):
+        total = jnp.zeros((rows, slots * own), jnp.float32)
+        for j in range(chunks):
+            total = total + lax.dot_general(
+                x_ref[j], panel_ref[j], (((1,), (1,)), ((), ())), preferred_element_type=jnp.float32
+            )
+        total = total.reshape(levels, 2 * half, slots * own)
+        slot_of = lax.broadcasted_iota(jnp.int32, (levels, half, own), 1) // 2
+        degree = lax.broadcasted_iota(jnp.int32, (levels, half, own), 2) + info_ref[0] * own
+        result = jnp.zeros((levels, half, own), jnp.float32)
+        for s in range(slots):
+            order = info_ref[1 + s]
+            mine = total[:, :, s * own : (s + 1) * own]
+            sign = (1 - 2 * ((degree + order) & 1)).astype(jnp.float32)
+            value = mine[:, :half] + sign * mine[:, half:]
+            keep = jnp.logical_and(slot_of == s, degree >= order)
+            result = jnp.where(keep, value, result)
+        o_ref[...] = result
+
+    return pl.pallas_call(
+        kernel,
+        out_shape=jax.ShapeDtypeStruct((levels, half, own), jnp.float32),
+        in_specs=[pl.BlockSpec(memory_space=pltpu.SMEM)] + [pl.BlockSpec(memory_space=pltpu.VMEM)] * 2,
+        out_specs=pl.BlockSpec(memory_space=pltpu.VMEM),
+        compiler_params=params(),
+        name="direct",
+    )(info, returned, panels)
+
+
+def evenly_spaced(spec, legendre, gauss_w, cycle_len, wave_map):
+    slots = spec.shape[0]
+    degrees_all = spec.shape[3]
+    own = legendre.shape[1]
+    lats = legendre.shape[2]
+    slot_count = wave_map.shape[0]
+    step = degrees_all // slot_count
+    waves = slot_count // slots
+    levels = degrees_all // own
+    wave_pos = lax.axis_index("wave")
+    lev_pos = lax.axis_index("lev")
+    orders = lax.dynamic_slice_in_dim(wave_map * step, wave_pos * slots, slots)
+    info = jnp.concatenate([lev_pos.reshape(1), orders]).astype(jnp.int32)
+    rows_here = 2 * slots * 2
+
+    sent = send_spec(info, spec.reshape(slots, 2, degrees_all), levels)
+    coefficients = lax.all_to_all(sent, "lev", 0, 0, tiled=True)
+
+    here = lats // waves
+    wide = -(-here // LANES) * LANES
+    tiles = wide // LANES
+    panel = legendre.reshape(slots * own, lats)
+    panels = jnp.stack(
+        [
+            jnp.pad(panel[:, i * here : (i + 1) * here], ((0, 0), (0, wide - here)))
+            for i in range(waves)
+        ]
+    )
+
+    lens = lax.dynamic_slice_in_dim(cycle_len, wave_pos * here, here)
+    weights = lax.dynamic_slice_in_dim(gauss_w, wave_pos * here, here)
+    lens = jnp.pad(lens, (0, wide - here), constant_values=4)
+    weights = jnp.pad(weights, (0, wide - here))
+
+    def both_halves(x):
+        x = jnp.tile(x.reshape(tiles, LANES), (2, 1))
+        return jnp.pad(x, ((0, SUBLANES - 2 * tiles), (0, 0)), constant_values=1)
+
+    per = LANES // (4 * slot_count)
+    rows_out = here // 2
+    groups = -(-rows_out // (per * STEPS)) * STEPS
+    span = 2 * (LPAD // LANES)
+    grouped = lens[: groups * 2 * per].reshape(groups, per, 2)
+    first = jnp.broadcast_to(grouped[:, :, :1], grouped.shape)
+    offset = first * jnp.array([0, 1], jnp.int32)
+    facts = jnp.stack(
+        [
+            grouped.astype(jnp.float32),
+            1.0 / grouped.astype(jnp.float32),
+            offset.astype(jnp.float32),
+            (first // LANES).astype(jnp.float32),
+            (first % LANES).astype(jnp.float32),
+        ]
+        + [jnp.zeros(grouped.shape, jnp.float32)] * 3,
+        axis=1,
+    ).reshape(groups, SUBLANES, 2 * per)
+    facts = jnp.repeat(facts, 2 * slot_count, axis=2)
+    ends = (grouped[:, :, 0] + grouped[:, :, 1]).reshape(groups * per)
+    p, q, t = phase_tables(facts, span, slot_count, step)
+
+    part = partial_fourier(coefficients.reshape(levels * rows_here, slots * own), panels)
+    part = part.reshape(waves * levels, rows_here, wide)
+    part = lax.all_to_all(part, ("wave", "lev"), 0, 0, tiled=True)
+    fourier, returned = quadratic(
+        wave_map,
+        part,
+        both_halves(lens.astype(jnp.float32)),
+        both_halves(weights),
+        waves,
+        step,
+    )
+    returned = lax.all_to_all(returned, ("wave", "lev"), 0, 0, tiled=True)
+
+    amplitudes = fourier[:, : 2 * tiles].reshape(slot_count, 2, 2, wide)[..., : groups * 2 * per]
+    amplitudes = amplitudes.reshape(slot_count, 2, 2, groups, 2 * per).transpose(3, 1, 2, 4, 0)
+    amplitudes = jnp.repeat(amplitudes, 2, axis=4).reshape(groups, 2, 2, LANES)
+    amplitudes = jnp.tile(amplitudes, (1, 1, SUBLANES // 2, 1))
+    values = grid_values(ends, facts, amplitudes, p, q, t, span, slot_count, rows_out)
+    values = values.reshape(rows_out, span // 2, 2, LANES)
+    values = with_layout_constraint(values, Layout(major_to_minor=(0, 1, 2, 3)))
+    values = values.transpose(0, 2, 1, 3)
+    values = with_layout_constraint(values, Layout(major_to_minor=(0, 2, 1, 3)))
+    values = values.reshape(rows_out, 2, LPAD)
+    values = with_layout_constraint(values, Layout(major_to_minor=(0, 1, 2)))
+    grid = values.transpose(1, 0, 2).reshape(2, rows_out, 1, LPAD)
+
+    returned = returned.reshape(waves, levels * rows_here, wide)
+    spectral = direct(info, returned, panels, slots, own)
+    spectral = lax.all_to_all(spectral, "lev", 0, 0, tiled=True)
+    spec_out = spectral.transpose(1, 0, 2).reshape(slots, 1, 2, degrees_all)
+    return (grid, spec_out)
+
+
+def per_device(spec, legendre, gauss_w, cycle_len, wave_map):
+    slot_count = wave_map.shape[0]
+    fits = (
+        spec.shape[3] % slot_count == 0
+        and LANES % (4 * slot_count) == 0
+        and spec.shape[1] == 1
+        and 4 * spec.shape[0] == SUBLANES
+    )
+    form = evenly_spaced if fits else general
+    return form(spec, legendre, gauss_w, cycle_len, wave_map)
+
+
 def solution(mesh):
     placed = (P("wave", "lev", None, None), P("wave", "lev", None), P(), P(), P())
     return jax.shard_map(

time: 524 us -> 82.7 us (0.16)
  other arithmetic: 383 us -> 4.32 us
  waiting for transfers between devices: 53.1 us -> 16.3 us
  Pallas kernels: 0 us -> 32.1 us
  local copies, waits for them, and re-layouts: 35.7 us -> 10.8 us
  matrix products: 23.6 us -> 0 us
  between operations: 14.1 us -> 0.83 us
  starting transfers between devices: 4.64 us -> 17.5 us
  blocking collectives: 7.99 us -> 0 us
    convert_element_type x60 -> x2, other arithmetic: 351 us -> 0.02 us  [the longest x1 0.01 us: evenly_spaced(): (first % LANES).astype(jnp.float32)]
    all_gather x1 -> x0, waiting for transfers between devices: 49 us -> none  [per_device(): panels = lax.all_gather(legendre, 'lev', axis=1, tiled=True)]
    pallas_call x0 -> x6, Pallas kernels: none -> 32.1 us  [the longest x1 14.3 us: phase_tables(): pl.pallas_call(kernel, out_shape=(jax.ShapeDtypeStruct((groups, rows, LAN...]
    dot_general x32 -> x0, matrix products: 23.6 us -> none  [the longest x15 9.74 us: cycle_block(): jnp.einsum('rap,rkp->rak', by_cycle, tables, preferred_element_type=jnp.f...]
    dynamic_update_slice x15 -> x0, local copies, waits for them, and re-layouts: 13.2 us -> none  [per_device(): lax.map(run_block, (ordered, lens_here.reshape(blocks, row_block, 2), wei...]
    all_to_all x1 -> x4, starting transfers between devices: 4.6 us -> 17.5 us  [the longest x1 6.33 us: evenly_spaced(): part = lax.all_to_all(part, ('wave', 'lev'), 0, 0, tiled=True)]
    all_to_all x1 -> x4, waiting for transfers between devices: 3.41 us -> 16.3 us  [the longest x1 8.8 us: evenly_spaced(): returned = lax.all_to_all(returned, ('wave', 'lev'), 0, 0, tiled=True)]
    select_n x62 -> x0, other arithmetic: 12.6 us -> none  [the longest x15 8.5 us: cycle_block(): jnp.where(selector[:, None, :, None, :], squared[:, :, None, :, :], jnp.z...]
  transfers between devices with their start and end apart: 2 -> 4, of which waited for: 2 -> 2; matrix products, arithmetic and copies ran while one was open for 1% -> 14% of each run, Pallas kernels for 0% -> 29%
where the time goes in v1:
time: 82.7 us; the launch traced here: 81.8 us
  Pallas kernels  32.1 us (39%)
  starting transfers between devices  17.5 us (21%)
  waiting for transfers between devices  16.3 us (20%)
  local copies, waits for them, and re-layouts  10.8 us (13%)
  other arithmetic  4.32 us (5%)
  between operations  0.83 us (1%)
    pallas_call x1, Pallas kernels, phase_tables(): pl.pallas_call(kernel, out_shape=(jax.ShapeDtypeStruct((groups, rows, LAN...  14.3 us
    pallas_call x1, Pallas kernels, grid_values(): pl.pallas_call(kernel, grid=(STEPS,), out_shape=jax.ShapeDtypeStruct((row...  9.69 us
    all_to_all x1, waiting for transfers between devices, evenly_spaced(): returned = lax.all_to_all(returned, ('wave', 'lev'), 0, 0, tiled=True)  8.8 us
    all_to_all x1, waiting for transfers between devices, evenly_spaced(): part = lax.all_to_all(part, ('wave', 'lev'), 0, 0, tiled=True)  7.46 us
    all_to_all x1, starting transfers between devices, evenly_spaced(): part = lax.all_to_all(part, ('wave', 'lev'), 0, 0, tiled=True)  6.33 us
    all_to_all x1, starting transfers between devices, evenly_spaced(): coefficients = lax.all_to_all(sent, 'lev', 0, 0, tiled=True)  5.17 us
    all_to_all x1, starting transfers between devices, evenly_spaced(): spectral = lax.all_to_all(spectral, 'lev', 0, 0, tiled=True)  3.33 us
    all_to_all x1, starting transfers between devices, evenly_spaced(): returned = lax.all_to_all(returned, ('wave', 'lev'), 0, 0, tiled=True)  2.72 us
  transfers between devices with their start and end apart: 4, of which 2 were waited for; matrix products, arithmetic and copies ran while one was open for 14% of the time, Pallas kernels for 29%

profile of v1, /device:TPU:0, one launch (start us, length us, event | category | flops | bytes accessed | tf_op | source)
XLA Modules:
  0.0 81.8 jit_solution(4045979670507367334)
XLA Ops:
  0.6 0.7 broadcast_multiply_fusion
  1.3 0.1 dynamic_slice.10
  1.4 0.6 pad_add_fusion.info_ref
  2.0 1.4 %send_spec.1 = bf16[8,8,320]{2,1,0:T(8,128)(2,1)} custom-call(s32[3]{0:T(128)} %pad_add_fusion.info_ref, bf16[2,2,1280]{2,1,0:T(2,128)(2,1)} %bitcast.84), custom_call_target="tpu_custom_call" | custom-call | tf_op jit(solution)/shard_map/send_spec/pallas_call | solution.py:167
  3.4 5.2 %all-to-all-start = ((bf16[8,8,320]{2,1,0:T(8,128)(2,1)}), bf16[8,8,320]{2,1,0:T(8,128)(2,1)S(1)}, u32[]{:S(2)}, u32[]{:S(2)}) async-start(bf16[8,8,320]{2,1,0:T(8,128)(2,1)} %send_spec.1), calls=%async_computation | async-start | bytes 98304 | tf_op jit(solution)/shard_map/all_to_all | solution.py:485
  8.6 0.8 dynamic_slice.9
  9.4 0.1 convert_element_type.73
  9.5 0.1 copy.28
  9.5 0.2 reshape.243
  9.7 0.8 %fusion.6 = (s32[40,4,1]{2,1,0:T(4,128)S(1)}, s32[40,4]{1,0:T(8,128)S(1)}) fusion(s32[40,4,2]{2,1,0:T(4,128)S(1)} %reshape.243), kind=kLoop, calls=%fused_computation.36 | loop fusion | flops 160 | bytes 2560 | tf_op jit(solution)/shard_map/slice | solution.py:526
  10.5 0.1 copy.27
  10.7 1.5 %fusion.5 = (bf16[320,300]{1,0:T(8,128)(2,1)S(1)}, bf16[320,300]{1,0:T(8,128)(2,1)S(1)}, bf16[320,300]{1,0:T(8,128)(2,1)S(1)}) fusion(bf16[320,1200]{1,0:T(8,128)(2,1)} %bitcast.70), kind=kLoop, calls=%fused_computation.35 | loop fusion | bytes 1152000 | tf_op jit(solution)/shard_map/slice | solution.py:493
  12.2 1.0 %fusion = (bf16[1,320,384]{2,1,0:T(8,128)(2,1)S(1)}, bf16[1,320,384]{2,1,0:T(8,128)(2,1)S(1)}) fusion(bf16[320,1200]{1,0:T(8,128)(2,1)} %bitcast.71, pred[384]{0:T(512)(128)(4,1)} %constant.61.clone.1, bf16[320,300]{1,0:T(8,128)(2,1)S(1)} %get-tuple-element.18), kind=kLoop, calls=%fused_computation.2 | loop fusion | flops 122880 | bytes 929664 | tf_op jit(solution)/shard_map/stack | solution.py:491
  13.3 0.1 pad_bitcast_fusion
  13.3 1.1 %pad_maximum_fusion.panel_ref = bf16[4,320,384]{2,1,0:T(8,128)(2,1)} fusion(bf16[1,320,384]{2,1,0:T(8,128)(2,1)S(1)} %get-tuple-element.33, bf16[1,320,384]{2,1,0:T(8,128)(2,1)S(1)} %get-tuple-element.34, bf16[1,320,384]{2,1,0:T(8,128)(2,1)S(1)} %get-tuple-element.36, bf16[1,320,384]{2,1,0:T(8,128)(2,1)S(1)} %get-tuple-element.35), kind=kLoop, calls=%fused_computation | loop fusion | flops 1474560 | bytes 1966080 | tf_op jit(solution)/shard_map/stack | solution.py:491
  14.4 0.8 dynamic_slice.11
  15.2 0.0 all-to-all-done
  15.2 0.0 copy-start.2
  15.2 0.6 copy-done.2
  15.8 2.2 %partial_fourier.1 = bf16[4,64,384]{2,1,0:T(8,128)(2,1)} custom-call(bf16[64,320]{1,0:T(8,128)(2,1)} %bitcast.75, bf16[4,320,384]{2,1,0:T(8,128)(2,1)} %pad_maximum_fusion.panel_ref), custom_call_target="tpu_custom_call" | custom-call | tf_op jit(solution)/shard_map/partial_fourier/pallas_call | solution.py:187
  18.0 6.3 %all-to-all-start.1 = ((bf16[32,8,384]{2,1,0:T(8,128)(2,1)}), bf16[32,8,384]{2,1,0:T(8,128)(2,1)S(1)}, u32[]{:S(2)}, u32[]{:S(2)}) async-start(bf16[32,8,384]{2,1,0:T(8,128)(2,1)} %bitcast.73), calls=%async_computation.1 | async-start | bytes 393216 | tf_op jit(solution)/shard_map/all_to_all | solution.py:531
  24.4 0.6 pad.35.weight_ref
  25.0 0.6 pad.33.len_ref
  25.6 0.1 mul.32
  25.7 0.1 copy.29
  25.8 7.5 %all-to-all-done.1.x_ref = bf16[32,8,384]{2,1,0:T(8,128)(2,1)S(1)} async-done(((bf16[32,8,384]{2,1,0:T(8,128)(2,1)}), bf16[32,8,384]{2,1,0:T(8,128)(2,1)S(1)}, u32[]{:S(2)}, u32[]{:S(2)}) %all-to-all-start.1) | async-done | bytes 196640 | tf_op jit(solution)/shard_map/all_to_all | solution.py:531
  33.2 0.0 copy-start
  33.3 0.7 copy-done
  33.9 1.8 %quadratic.1 = (f32[16,8,128]{2,1,0:T(8,128)}, bf16[32,8,384]{2,1,0:T(8,128)(2,1)}) custom-call(s32[8]{0:T(128)} %map_ref.1, bf16[32,8,384]{2,1,0:T(8,128)(2,1)} %copy-done, f32[8,128]{1,0:T(8,128)} %pad.33.len_ref, f32[8,128]{1,0:T(8,128)} %pad.35.weight_ref), custom_call_target="tpu_custom_call" | custom-call | tf_op jit(solution)/shard_map/quadratic/pallas_call | solution.py:274
  35.8 0.0 copy-start.3
  35.8 2.7 %all-to-all-start.2 = ((bf16[32,8,384]{2,1,0:T(8,128)(2,1)}), bf16[32,8,384]{2,1,0:T(8,128)(2,1)S(1)}, u32[]{:S(2)}, u32[]{:S(2)}) async-start(bf16[32,8,384]{2,1,0:T(8,128)(2,1)} %get-tuple-element.11), calls=%async_computation.2 | async-start | bytes 393216 | tf_op jit(solution)/shard_map/all_to_all | solution.py:540
  38.5 0.1 constant_dynamic-update-slice_fusion.4
  38.6 8.8 %all-to-all-done.2 = bf16[32,8,384]{2,1,0:T(8,128)(2,1)S(1)} async-done(((bf16[32,8,384]{2,1,0:T(8,128)(2,1)}), bf16[32,8,384]{2,1,0:T(8,128)(2,1)S(1)}, u32[]{:S(2)}, u32[]{:S(2)}) %all-to-all-start.2) | async-done | bytes 196640 | tf_op jit(solution)/shard_map/all_to_all | solution.py:540
  47.4 0.0 copy-start.1
  47.4 0.7 copy-done.1
  48.0 2.6 %direct.1 = f32[8,4,160]{2,1,0:T(4,128)} custom-call(s32[3]{0:T(128)} %pad_add_fusion.info_ref, bf16[4,64,384]{2,1,0:T(8,128)(2,1)} %bitcast.74, bf16[4,320,384]{2,1,0:T(8,128)(2,1)} %pad_maximum_fusion.panel_ref), custom_call_target="tpu_custom_call" | custom-call | tf_op jit(solution)/shard_map/direct/pallas_call | solution.py:459
  50.6 3.3 %all-to-all-start.3 = ((f32[8,4,160]{2,1,0:T(4,128)}), f32[8,4,160]{2,1,0:T(4,128)S(1)}, u32[]{:S(2)}, u32[]{:S(2)}) async-start(f32[8,4,160]{2,1,0:T(4,128)} %direct.1), calls=%async_computation.3 | async-start | bytes 65536 | tf_op jit(solution)/shard_map/all_to_all | solution.py:557
  54.0 0.7 add.39.end_ref
  54.7 0.8 %copy.34.fact_ref = f32[40,8,128]{2,1,0:T(8,128)} copy(f32[40,8,128]{0,2,1:T(8,128)S(1)} %bitcast.68) | data formatting | bytes 327680 | tf_op jit(solution)/shard_map/reshape | solution.py:525
  55.5 14.3 %phase_tables.1 = (f32[40,80,128]{2,1,0:T(8,128)}, f32[40,80,128]{2,1,0:T(8,128)}, bf16[40,256,128]{2,1,0:T(8,128)(2,1)}) custom-call(f32[40,8,128]{2,1,0:T(8,128)} %copy.34.fact_ref), custom_call_target="tpu_custom_call" | custom-call | flops 29491200 | tf_op jit(solution)/shard_map/phase_tables/pallas_call | solution.py:344
  69.8 0.0 copy-done.3
  69.9 0.2 reshape.251
  70.1 0.2 copy.31
  70.4 0.1 broadcast_in_dim.38
  70.5 0.1 copy.32
  70.6 0.8 tile.37
  71.4 9.7 %grid_values.1 = bf16[11400,128]{1,0:T(8,128)(2,1)} custom-call(s32[160]{0:T(256)} %add.39.end_ref, f32[40,8,128]{2,1,0:T(8,128)} %copy.34.fact_ref, f32[40,2,8,128]{3,2,1,0:T(8,128)} %bitcast.69, f32[40,80,128]{2,1,0:T(8,128)} %get-tuple-element.8.p_ref, f32[40,80,128]{2,1,0:T(8,128)} %get-tuple-element.9.q_ref, bf16[40,256,128]{2,1,0:T(8,128)(2,1)} %get-tuple-element.10.t_ref), custom_call_target="tpu_custom_call" | custom-call | flops 29491200 | tf_op jit(solution)/shard_map/grid_values/pallas_call | solution.py:416
  81.1 0.0 all-to-all-done.3
  81.1 0.7 reshape.256
  (23 shorter events, 0.2 us)
Async XLA Ops:
  3.4 11.8 %all-to-all-start = ((bf16[8,8,320]{2,1,0:T(8,128)(2,1)}), bf16[8,8,320]{2,1,0:T(8,128)(2,1)S(1)}, u32[]{:S(2)}, u32[]{:S(2)}) async-start(bf16[8,8,320]{2,1,0:T(8,128)(2,1)} %send_spec.1), calls=%async_computation | async-start | bytes 98304 | tf_op jit(solution)/shard_map/all_to_all | solution.py:485
  15.2 0.6 copy-start.2
  18.0 15.2 %all-to-all-start.1 = ((bf16[32,8,384]{2,1,0:T(8,128)(2,1)}), bf16[32,8,384]{2,1,0:T(8,128)(2,1)S(1)}, u32[]{:S(2)}, u32[]{:S(2)}) async-start(bf16[32,8,384]{2,1,0:T(8,128)(2,1)} %bitcast.73), calls=%async_computation.1 | async-start | bytes 393216 | tf_op jit(solution)/shard_map/all_to_all | solution.py:531
  33.2 0.7 copy-start
  35.8 34.1 %copy-start.3 = (f32[16,8,128]{2,1,0:T(8,128)S(1)}, f32[16,8,128]{2,1,0:T(8,128)}, u32[]{:S(2)}) copy-start(f32[16,8,128]{2,1,0:T(8,128)} %get-tuple-element.7) | copy-start | bytes 196612
  35.8 11.6 %all-to-all-start.2 = ((bf16[32,8,384]{2,1,0:T(8,128)(2,1)}), bf16[32,8,384]{2,1,0:T(8,128)(2,1)S(1)}, u32[]{:S(2)}, u32[]{:S(2)}) async-start(bf16[32,8,384]{2,1,0:T(8,128)(2,1)} %get-tuple-element.11), calls=%async_computation.2 | async-start | bytes 393216 | tf_op jit(solution)/shard_map/all_to_all | solution.py:540
  47.4 0.7 copy-start.1
  50.6 30.5 %all-to-all-start.3 = ((f32[8,4,160]{2,1,0:T(4,128)}), f32[8,4,160]{2,1,0:T(4,128)S(1)}, u32[]{:S(2)}, u32[]{:S(2)}) async-start(f32[8,4,160]{2,1,0:T(4,128)} %direct.1), calls=%async_computation.3 | async-start | bytes 65536 | tf_op jit(solution)/shard_map/all_to_all | solution.py:557

commit v2 on v0

--- a/solution.py
+++ b/solution.py
@@ -1,8 +1,12 @@
+import functools
 import math
 
 import jax
 import jax.numpy as jnp
 from jax import lax
+from jax.experimental import pallas as pl
+from jax.experimental.layout import Layout, with_layout_constraint
+from jax.experimental.pallas import tpu as pltpu
 from jax.sharding import PartitionSpec as P
 
 LPAD = 4864
@@ -62,7 +66,7 @@
     return jnp.where((degree_ids[None, :] + own_orders[:, None]) % 2 == 0, 1.0, -1.0)
 
 
-def per_device(spec, legendre, gauss_w, cycle_len, wave_map):
+def general(spec, legendre, gauss_w, cycle_len, wave_map):
     slots_dev = spec.shape[0]
     fields = spec.shape[1]
     degrees_all = spec.shape[3]
@@ -114,10 +118,607 @@
     return (grid, spec_out)
 
 
+LANES = 128
+SUBLANES = 8
+STEPS = 5
+VMEM = 8 * 1024 * 1024
+SINE = (6.28318516, -41.34165503, 81.60100407, -76.54978222, 39.53670553)
+
+
+def cos_turns(x, period, inverse):
+    turn = x - period * jnp.floor(x * inverse + 0.5)
+    v = 0.25 - jnp.abs(turn * inverse)
+    y = v * v
+    series = SINE[4]
+    for coefficient in SINE[3::-1]:
+        series = series * y + coefficient
+    return v * series
+
+
+def params(memory=VMEM):
+    return pltpu.CompilerParams(vmem_limit_bytes=memory)
+
+
+def cost(flops, nbytes):
+    return pl.CostEstimate(flops=flops, bytes_accessed=nbytes, transcendentals=0)
+
+
+def at_wave():
+    return lax.axis_index("wave")
+
+
+def at_level():
+    return lax.axis_index("lev")
+
+
+def smem():
+    return pl.BlockSpec(memory_space=pltpu.SMEM)
+
+
+def vmem():
+    return pl.BlockSpec(memory_space=pltpu.VMEM)
+
+
+def own_rows(wave_map, spec, panel, step):
+    slots, parts, degrees_all = spec.shape
+    rows = 2 * slots * parts
+
+    def kernel(map_hbm, x_hbm, panel_hbm, o_ref, factor_ref, near_ref, map_ref, x_ref, sems):
+        copies = [
+            pltpu.make_async_copy(a, b, sems.at[i])
+            for i, (a, b) in enumerate(((map_hbm, map_ref), (x_hbm, x_ref), (panel_hbm, near_ref)))
+        ]
+        for copy in copies:
+            copy.start()
+        copies[0].wait()
+        row = lax.broadcasted_iota(jnp.int32, (rows, degrees_all), 0)
+        degree = lax.broadcasted_iota(jnp.int32, (rows, degrees_all), 1)
+        order = jnp.zeros((rows, degrees_all), jnp.int32)
+        for s in range(slots):
+            mine = row // parts % slots == s
+            order = jnp.where(mine, map_ref[at_wave() * slots + s] * step, order)
+        odd = jnp.logical_and(row >= rows // 2, ((degree + order) & 1) == 1)
+        factor = jnp.where(degree >= order, jnp.where(odd, -1.0, 1.0), 0.0)
+        factor_ref[...] = factor
+        copies[1].wait()
+        x = [x_ref[s].astype(jnp.float32) for s in range(slots)]
+        o_ref[...] = jnp.concatenate(x + x, axis=0) * factor
+        copies[2].wait()
+
+    flat = jax.ShapeDtypeStruct((rows, degrees_all), jnp.float32)
+    return pl.pallas_call(
+        kernel,
+        out_shape=(flat, flat, jax.ShapeDtypeStruct(panel.shape, panel.dtype)),
+        in_specs=[pl.BlockSpec(memory_space=pltpu.HBM)] * 3,
+        out_specs=(vmem(),) * 3,
+        scratch_shapes=[
+            pltpu.SMEM(wave_map.shape, wave_map.dtype),
+            pltpu.VMEM(spec.shape, spec.dtype),
+            pltpu.SemaphoreType.DMA((3,)),
+        ],
+        compiler_params=params(),
+        cost_estimate=cost(10**9, 2 * 10**6),
+        name="own_rows",
+    )(wave_map, spec, panel)
+
+
+def partial_fourier(first, factor, others, panels, slots, waves, wide):
+    chips = len(others) + 1
+    rows, degrees_all = first.shape
+    parts = rows // (2 * slots)
+    depth, lats = panels[0].shape
+    own, here = depth // slots, lats // waves
+
+    def kernel(first_ref, factor_ref, *refs):
+        spec_refs, panel_refs = refs[: chips - 1], refs[chips - 1 : chips + 1]
+        o_ref, left_ref = refs[chips + 1 :]
+        factor = factor_ref[...]
+        whole = [first_ref[...]]
+        for ref in spec_refs:
+            x = [ref[s].astype(jnp.float32) for s in range(slots)]
+            whole.append(jnp.concatenate(x + x, axis=0) * factor)
+        whole = jnp.concatenate(whole, axis=0)
+        slot_of = lax.broadcasted_iota(jnp.int32, (chips * rows, own), 0) // parts % slots
+        for level in range(2 * chips):
+
+            @pl.when(at_level() == level)
+            def _(level=level):
+                for e in range(2):
+                    start = (level ^ e) * own
+                    piece = whole[:, start : start + own]
+                    left = [jnp.where(slot_of == s, piece, 0.0) for s in range(slots)]
+                    left_ref[e] = jnp.concatenate(left, axis=1).astype(jnp.bfloat16)
+
+        total = jnp.dot(left_ref[0], panel_refs[0][...], preferred_element_type=jnp.float32)
+        total += jnp.dot(left_ref[1], panel_refs[1][...], preferred_element_type=jnp.float32)
+        chip = at_level() // 2
+        fill = jnp.zeros((rows, wide - here), jnp.float32)
+        for i in range(chips):
+            mine = total[i * rows : (i + 1) * rows]
+            for j in range(waves):
+                value = mine[:, j * here : (j + 1) * here]
+                o_ref[j, chip ^ i] = jnp.concatenate([value, fill], axis=1)
+
+    return pl.pallas_call(
+        kernel,
+        out_shape=jax.ShapeDtypeStruct((waves, chips, rows, wide), jnp.float32),
+        in_specs=[vmem()] * (chips + 3),
+        out_specs=vmem(),
+        scratch_shapes=[pltpu.VMEM((2, chips * rows, depth), jnp.bfloat16)],
+        compiler_params=params(),
+        cost_estimate=cost(10**9, 2 * 10**6),
+        name="partial_fourier",
+    )(first, factor, *others, *panels)
+
+
+def quadratic(wave_map, parts_sum, lens, weights, waves, step):
+    sources, rows, wide = parts_sum.shape
+    slot_count = wave_map.shape[0]
+    levels = sources // waves
+    slots = slot_count // waves
+    tiles = wide // LANES
+    top = 2 * (slot_count - 1)
+    shape = (SUBLANES, LANES)
+
+    def kernel(map_ref, x_ref, len_ref, weight_ref, g_ref, o_ref, z_ref, r_ref, s_ref):
+        z_ref[...] = jnp.zeros(z_ref.shape, jnp.float32)
+        for i in range(waves):
+            total = x_ref[i * levels].astype(jnp.float32)
+            for j in range(1, levels):
+                total = total + x_ref[i * levels + j].astype(jnp.float32)
+            total = total.astype(jnp.bfloat16).astype(jnp.float32)
+            for row in range(rows):
+                h, s, c = row // (2 * slots), row // 2 % slots, row % 2
+                at = map_ref[i * slots + s] * 2 + c
+                for t in range(tiles):
+                    k = h * tiles + t
+                    z_ref[at, k : k + 1, :] = total[row : row + 1, t * LANES : (t + 1) * LANES]
+        lens_here = len_ref[...]
+        kept = [
+            jnp.where(lens_here > 2.0 * step * w, 1.0, 0.0) for w in range(slot_count)
+        ]
+        real = [z_ref[2 * w] * kept[w] for w in range(slot_count)]
+        imag = [z_ref[2 * w + 1] * kept[w] for w in range(slot_count)]
+        for w in range(slot_count):
+            double = 1.0 if w == 0 else 2.0
+            g_ref[2 * w] = real[w] * double
+            g_ref[2 * w + 1] = imag[w] * double
+        imag[0] = jnp.zeros(shape, jnp.float32)
+        square_real, square_imag = [], []
+        for n in range(top + 1):
+            re, im = jnp.zeros(shape, jnp.float32), jnp.zeros(shape, jnp.float32)
+            for a in range(max(0, n - slot_count + 1), (n + 1) // 2):
+                b = n - a
+                re = re + (real[a] * real[b] - imag[a] * imag[b])
+                im = im + (real[a] * imag[b] + imag[a] * real[b])
+            for b in range(1, slot_count - n):
+                a = n + b
+                re = re + (real[a] * real[b] + imag[a] * imag[b])
+                im = im + (imag[a] * real[b] - real[a] * imag[b])
+            re, im = 2.0 * re, 2.0 * im
+            if n % 2 == 0:
+                a = n // 2
+                re = re + (real[a] * real[a] - imag[a] * imag[a])
+                im = im + 2.0 * (real[a] * imag[a])
+            square_real.append(re)
+            square_imag.append(im)
+        whole = {
+            d: jnp.where(lens_here == 1.0 * step * d, 1.0, 0.0)
+            for d in range(3, top + slot_count)
+        }
+        weights_here = weight_ref[...]
+        for w in range(slot_count):
+            re, im = square_real[w], square_imag[w]
+            if w == 0:
+                im = jnp.zeros(shape, jnp.float32)
+            else:
+                for n in range(w + 1, top + 1):
+                    re = re + whole[w + n] * square_real[n]
+                    im = im - whole[w + n] * square_imag[n]
+            factor = kept[w] * weights_here
+            r_ref[2 * w] = re * factor
+            r_ref[2 * w + 1] = im * factor
+        for i in range(waves):
+            for row in range(rows):
+                h, s, c = row // (2 * slots), row // 2 % slots, row % 2
+                at = map_ref[i * slots + s] * 2 + c
+                for t in range(tiles):
+                    k = h * tiles + t
+                    s_ref[row : row + 1, t * LANES : (t + 1) * LANES] = r_ref[at, k : k + 1, :]
+            packed = s_ref[...].astype(jnp.bfloat16)
+            for j in range(levels):
+                o_ref[i * levels + j] = packed
+
+    return pl.pallas_call(
+        kernel,
+        out_shape=(
+            jax.ShapeDtypeStruct((2 * slot_count,) + shape, jnp.float32),
+            jax.ShapeDtypeStruct((sources, rows, wide), jnp.bfloat16),
+        ),
+        in_specs=[smem(), vmem(), vmem(), vmem()],
+        out_specs=(vmem(), vmem()),
+        scratch_shapes=[
+            pltpu.VMEM((2 * slot_count,) + shape, jnp.float32),
+            pltpu.VMEM((2 * slot_count,) + shape, jnp.float32),
+            pltpu.VMEM((rows, wide), jnp.float32),
+        ],
+        compiler_params=params(),
+        name="quadratic",
+    )(wave_map, parts_sum, lens, weights)
+
+
+def lane_facts(slot_count):
+    lane = lax.broadcasted_iota(jnp.int32, (SUBLANES, LANES), 1)
+    return (lane % (4 * slot_count) // 4, lane % 4 // 2, lane // (4 * slot_count), lane % 2)
+
+
+def tile_of_row(block, span, slot_count):
+    at = lax.broadcasted_iota(jnp.int32, (SUBLANES, LANES), 0) + block * SUBLANES
+    at = at - lane_facts(slot_count)[2] * span % SUBLANES
+    return at // 2, jnp.logical_and(at >= 0, at < span)
+
+
+def prepare(cycle_len, gauss_w, span, slot_count, step, waves, groups, wide):
+    here = cycle_len.shape[0] // waves
+    tiles = wide // LANES
+    per = SUBLANES // 2
+
+    def kernel(len_ref, len_row_ref, weight_row_ref, o_ref, lens_ref, weights_ref):
+        wave, part, row, cycle = lane_facts(slot_count)
+        tile, _ = tile_of_row(0, span, slot_count)
+        first = (tile * LANES).astype(jnp.float32)
+        order = (step * wave).astype(jnp.float32)
+        stride = order * (LANES * SUBLANES / 2.0)
+        is_imag = part.astype(jnp.float32)
+        way = (1 - 2 * cycle).astype(jnp.float32)
+        point = lax.broadcasted_iota(jnp.int32, (SUBLANES, LANES), 1).astype(jnp.float32)
+        down = lax.broadcasted_iota(jnp.int32, (SUBLANES, LANES), 0)
+        start = at_wave() * here
+
+        def body(g, carry):
+            lens = [
+                len_ref[start + jnp.minimum(g * SUBLANES + i, here - 1)] for i in range(SUBLANES)
+            ]
+            length = jnp.full((SUBLANES, LANES), lens[0], jnp.int32)
+            length_down = length
+            offset = jnp.zeros((SUBLANES, LANES), jnp.int32)
+            split = offset
+            for i in range(1, SUBLANES):
+                mine = row == i // 2 if i % 2 == 0 else jnp.logical_and(row == i // 2, cycle == 1)
+                length = jnp.where(mine, lens[i], length)
+                length_down = jnp.where(down == i, lens[i], length_down)
+            for r in range(per):
+                offset = jnp.where(jnp.logical_and(row == r, cycle == 1), lens[2 * r], offset)
+                split = jnp.where(row == r, lens[2 * r] // LANES, split)
+            length = length.astype(jnp.float32)
+            inverse = 1.0 / length
+            quarter = 0.25 * length
+            x = order * (first - offset.astype(jnp.float32))
+            o_ref[g, 0] = cos_turns(x - is_imag * quarter, length, inverse)
+            o_ref[g, 1] = cos_turns(x + (1.0 - is_imag) * quarter, length, inverse)
+            turns = cos_turns(jnp.where(down == 1, stride - quarter, stride), length, inverse)
+            o_ref[g, 2] = jnp.where(down < 2, turns, way * split.astype(jnp.float32))
+            length = length_down.astype(jnp.float32)
+            inverse = 1.0 / length
+            quarter = 0.25 * length
+            for i in range(2):
+                turn = (i + 1.0) * step * point
+                o_ref[g, 3 + 2 * i] = cos_turns(turn, length, inverse)
+                o_ref[g, 4 + 2 * i] = cos_turns(turn + quarter, length, inverse)
+            return carry
+
+        lax.fori_loop(0, groups, body, 0, unroll=4)
+        lens_ref[...] = jnp.full((SUBLANES, LANES), 4.0, jnp.float32)
+        weights_ref[...] = jnp.zeros((SUBLANES, LANES), jnp.float32)
+        for v in range(waves):
+
+            @pl.when(at_wave() == v)
+            def _(v=v):
+                for t in range(tiles):
+                    size = min(LANES, here - t * LANES)
+                    at = v * here + t * LANES
+                    lens = len_row_ref[:, at : at + size].astype(jnp.float32)
+                    weights = weight_row_ref[:, at : at + size]
+                    for h in range(2):
+                        k = h * tiles + t
+                        lens_ref[k : k + 1, 0:size] = lens
+                        weights_ref[k : k + 1, 0:size] = weights
+
+    flat = jax.ShapeDtypeStruct((SUBLANES, LANES), jnp.float32)
+    return pl.pallas_call(
+        kernel,
+        out_shape=(jax.ShapeDtypeStruct((groups, 7, SUBLANES, LANES), jnp.float32), flat, flat),
+        in_specs=[smem(), vmem(), vmem()],
+        out_specs=(vmem(),) * 3,
+        compiler_params=params(),
+        cost_estimate=cost(3 * 10**9, 10**6),
+        name="prepare",
+    )(cycle_len, cycle_len.reshape(1, -1), gauss_w.reshape(1, -1))
+
+
+def grid_values(cycle_len, fourier, tables, span, slot_count, rows_out, tiles):
+    groups = tables.shape[0]
+    per = SUBLANES // 2
+    block = groups // STEPS
+    blocks = -(-(span + SUBLANES // 2) // SUBLANES)
+    size = 4 * slot_count
+    kinds = 4 * slot_count
+    around = LANES // SUBLANES
+
+    def kernel(len_ref, fourier_ref, table_ref, o_ref, rows_ref, wave_ref):
+        wave, _, row, cycle = lane_facts(slot_count)
+        way = (1 - 2 * cycle).astype(jnp.float32)
+        point = lax.broadcasted_iota(jnp.int32, (SUBLANES, LANES), 1)
+        down = lax.broadcasted_iota(jnp.int32, (SUBLANES, LANES), 0)
+        second = down % 2 == 1
+        unit = jnp.where(down < 2, 1.0, 0.0)
+        beside = jnp.where(down < 6, -1.0, 1.0)
+        base = pl.program_id(0) * block
+        start = at_wave() * 2 * rows_out
+
+        @pl.when(pl.program_id(0) == 0)
+        def _():
+            for c in range(2):
+                for h in range(2):
+                    for w in range(slot_count):
+                        for t in range(tiles):
+                            at = (c * 2 + h) * slot_count + w
+                            k = h * tiles + t
+                            rows_ref[t, at : at + 1, :] = fourier_ref[2 * w + c, k : k + 1, :]
+
+        pick = lax.broadcasted_iota(jnp.int32, (LANES, LANES), 0)
+        lane = lax.broadcasted_iota(jnp.int32, (LANES, LANES), 1)
+        pick = jnp.where(pick == lane // size * 2 + lane % 2, 1.0, 0.0).astype(jnp.bfloat16)
+        turned = []
+        for g in range(block):
+            at = base + g
+            shift = (around - at % around) % around * SUBLANES
+            turned.append(pltpu.roll(rows_ref[at // around], shift, 1))
+        spread = jnp.dot(
+            jnp.concatenate(turned, axis=0).astype(jnp.bfloat16), pick, preferred_element_type=jnp.float32
+        )
+        for g in range(block):
+            sums = []
+            for k in range(4):
+                at = g * kinds + k * slot_count
+                value = jnp.where(down == wave, spread[at : at + SUBLANES], 0.0)
+                sums.append(jnp.sum(value, axis=0, keepdims=True))
+            for c in range(2):
+                wave_ref[g, c] = jnp.where(down % 2 == 0, sums[2 * c], sums[2 * c + 1])
+
+        def body(g, carry):
+            real, imag = wave_ref[g, 0], wave_ref[g, 1]
+            x = real * table_ref[g, 0] + imag * table_ref[g, 1]
+            y = real * table_ref[g, 1] - imag * table_ref[g, 0]
+            turn_cos, turn_sin = table_ref[g, 2, 0:1], table_ref[g, 2, 1:2]
+            split = table_ref[g, 2, 2:3]
+            main, mixed = [], []
+            for k in range(blocks):
+                if k:
+                    x, y = x * turn_cos + y * turn_sin, y * turn_cos - x * turn_sin
+                tile, inside = tile_of_row(k, span, slot_count)
+                apart = tile.astype(jnp.float32) * way - split
+                value = jnp.where(inside, x, 0.0) if k in (0, blocks - 1) else x
+                main.append(jnp.where(apart < 0.0, value, 0.0))
+                mixed.append(jnp.where(apart == 0.0, value, 0.0))
+            main, mixed = jnp.concatenate(main, axis=0), jnp.concatenate(mixed, axis=0)
+            left = jnp.concatenate([main, mixed], axis=1).astype(jnp.bfloat16)
+
+            columns, ends = [], []
+            for r in range(per):
+                at = 2 * jnp.minimum((base + g) * per + r, rows_out - 1) + start
+                first_end, end = len_ref[at], len_ref[at] + len_ref[at + 1]
+                ends.append(end)
+                cos1, sin1, cos2, sin2 = [
+                    jnp.where(
+                        second,
+                        table_ref[g, i, 2 * r + 1 : 2 * r + 2],
+                        table_ref[g, i, 2 * r : 2 * r + 1],
+                    )
+                    for i in range(3, 7)
+                ]
+                twice = 2.0 * cos2
+                series = [jnp.where(down < 4, unit, jnp.where(down < 6, cos1, sin1))]
+                third = series[0] * (twice + beside)
+                series.append(jnp.where(down < 2, cos2, jnp.where(down < 4, sin2, third)))
+                here = jnp.logical_xor(point < first_end % LANES, second)
+                for _ in range(2, size // SUBLANES):
+                    series.append(twice * series[-1] - series[-2])
+                full = jnp.concatenate(series, axis=0).astype(jnp.bfloat16)
+                part = jnp.concatenate([jnp.where(here, v, 0.0) for v in series], axis=0).astype(jnp.bfloat16)
+                before = [jnp.zeros((r * size, LANES), jnp.bfloat16)] if r else []
+                after = [jnp.zeros((LANES - (r + 1) * size, LANES), jnp.bfloat16)] if r < per - 1 else []
+                columns.append(jnp.concatenate(before + [full] + after + before + [part] + after, axis=0))
+            right = jnp.concatenate(columns, axis=1)
+            product = jnp.dot(left, right, preferred_element_type=jnp.float32)
+            places = {}
+            for r in range(per):
+                shift = r * span % SUBLANES
+                for k in range(blocks):
+                    if k * SUBLANES >= shift + span:
+                        continue
+                    value = product[k * SUBLANES : (k + 1) * SUBLANES, r * LANES : (r + 1) * LANES]
+                    if k == blocks - 1:
+                        position = (down + k * SUBLANES - shift) // 2 * LANES + point
+                        value = jnp.where(position < ends[r], value, 0.0)
+                    places.setdefault((r * span - shift) // SUBLANES + k, []).append(value)
+            whole = [functools.reduce(lambda a, b: a + b, places[k]) for k in sorted(places)]
+            size_out = per * span
+            o_ref[pl.ds(pl.multiple_of(g * size_out, 16), size_out), :] = jnp.concatenate(
+                whole, axis=0
+            ).astype(jnp.bfloat16)
+            return carry
+
+        lax.fori_loop(0, block, body, 0, unroll=8)
+
+    return pl.pallas_call(
+        kernel,
+        grid=(STEPS,),
+        out_shape=jax.ShapeDtypeStruct((rows_out * span, LANES), jnp.bfloat16),
+        in_specs=[
+            smem(),
+            pl.BlockSpec(fourier.shape, lambda i: (0, 0, 0)),
+            pl.BlockSpec((block,) + tables.shape[1:], lambda i: (i, 0, 0, 0)),
+        ],
+        out_specs=pl.BlockSpec((block * per * span, LANES), lambda i: (i, 0)),
+        scratch_shapes=[
+            pltpu.VMEM((tiles, kinds, LANES), jnp.float32),
+            pltpu.VMEM((block, 2, SUBLANES, LANES), jnp.float32),
+        ],
+        compiler_params=params(16 * 1024 * 1024),
+        cost_estimate=cost(8 * 10**9, 3 * 10**6),
+        name="grid_values",
+    )(cycle_len, fourier, tables)
+
+
+def direct(wave_map, returned, panels, step, slots):
+    waves, tall, _ = returned.shape
+    depth, lats = panels[0].shape
+    own, here = depth // slots, lats // waves
+    half = 2 * slots
+    chips = tall // (2 * half)
+
+    def kernel(map_ref, x_ref, own_ref, other_ref, *refs):
+        o_refs, left_ref, all_ref = refs[:chips], refs[chips], refs[chips + 1]
+        for j in range(waves):
+            left_ref[:, j * here : (j + 1) * here] = x_ref[j, :, 0:here].astype(jnp.float32)
+        left = left_ref[...].astype(jnp.bfloat16)
+        shape = (chips, half, own)
+        slot_of = lax.broadcasted_iota(jnp.int32, shape, 1) // 2
+        lane = lax.broadcasted_iota(jnp.int32, shape, 2)
+        for e, panel_ref in enumerate((own_ref, other_ref)):
+            total = lax.dot_general(
+                left, panel_ref[...], (((1,), (1,)), ((), ())), preferred_element_type=jnp.float32
+            ).reshape(chips, 2 * half, depth)
+            degree = lane + (at_level() ^ e) * own
+            result = jnp.zeros(shape, jnp.float32)
+            for s in range(slots):
+                order = map_ref[at_wave() * slots + s] * step
+                mine = total[:, :, s * own : (s + 1) * own]
+                sign = (1 - 2 * ((degree + order) & 1)).astype(jnp.float32)
+                value = mine[:, :half] + sign * mine[:, half:]
+                keep = jnp.logical_and(slot_of == s, degree >= order)
+                result = jnp.where(keep, value, result)
+            all_ref[:, e * half : (e + 1) * half, :] = result
+        for i in range(chips):
+            o_refs[i][...] = all_ref[(at_level() // 2) ^ i]
+
+    return pl.pallas_call(
+        kernel,
+        out_shape=(jax.ShapeDtypeStruct((2 * half, own), jnp.float32),) * chips,
+        in_specs=[smem()] + [vmem()] * 3,
+        out_specs=(vmem(),) * chips,
+        scratch_shapes=[
+            pltpu.VMEM((tall, lats), jnp.float32),
+            pltpu.VMEM((chips, 2 * half, own), jnp.float32),
+        ],
+        compiler_params=params(),
+        cost_estimate=cost(10**9, 2 * 10**6),
+        name="direct",
+    )(wave_map, returned, *panels)
+
+
+def join_degrees(pieces, slots):
+    chips = len(pieces)
+    rows, own = pieces[0].shape
+    half = rows // 2
+
+    def kernel(*refs):
+        piece_refs, o_ref, all_ref = refs[:chips], refs[chips], refs[chips + 1]
+        for i in range(chips):
+            for e in range(2):
+                all_ref[at_level() ^ (2 * i + e)] = piece_refs[i][e * half : (e + 1) * half, :]
+        whole = jnp.concatenate([all_ref[v] for v in range(2 * chips)], axis=1)
+        for s in range(slots):
+            o_ref[s] = whole[2 * s : 2 * s + 2]
+
+    return pl.pallas_call(
+        kernel,
+        out_shape=jax.ShapeDtypeStruct((slots, 2, 2 * chips * own), jnp.float32),
+        in_specs=[vmem()] * chips,
+        out_specs=vmem(),
+        scratch_shapes=[pltpu.VMEM((2 * chips, half, own), jnp.float32)],
+        compiler_params=params(),
+        name="join_degrees",
+    )(*pieces)
+
+
+def evenly_spaced(levels, spec, legendre, gauss_w, cycle_len, wave_map):
+    slots = spec.shape[0]
+    degrees_all = spec.shape[3]
+    own = legendre.shape[1]
+    lats = legendre.shape[2]
+    slot_count = wave_map.shape[0]
+    step = degrees_all // slot_count
+    waves = slot_count // slots
+    chips = levels // 2
+
+    def across(x, bits):
+        return lax.ppermute(x, "lev", [(j, j ^ bits) for j in range(levels)])
+
+    def same_core(x):
+        groups = [[j for j in range(waves * levels) if j % 2 == core] for core in range(2)]
+        return lax.all_to_all(x, ("wave", "lev"), 0, 0, tiled=True, axis_index_groups=groups)
+
+    mine = spec.reshape(slots, 2, degrees_all)
+    others = [across(mine, 2 * i) for i in range(1, chips)]
+    panel = legendre.reshape(slots * own, lats)
+    first, factor, near = own_rows(wave_map, mine, panel, step)
+    panels = (near, across(panel, 1))
+
+    here = lats // waves
+    wide = -(-here // LANES) * LANES
+    tiles = wide // LANES
+    per = SUBLANES // 2
+    rows_out = here // 2
+    groups = -(-rows_out // (per * STEPS)) * STEPS
+    span = 2 * (LPAD // LANES)
+    rows_here = 2 * slots * 2
+
+    part = partial_fourier(first, factor, others, panels, slots, waves, wide)
+    part = same_core(part.reshape(waves * chips, rows_here, wide))
+    tables, lens, weights = prepare(
+        cycle_len, gauss_w, span, slot_count, step, waves, groups, wide
+    )
+    fourier, returned = quadratic(wave_map, part, lens, weights, waves, step)
+    returned = same_core(returned)
+
+    values = grid_values(cycle_len, fourier, tables, span, slot_count, rows_out, tiles)
+    returned, values = lax.optimization_barrier((returned, values))
+    values = values.reshape(rows_out, span // 2, 2, LANES)
+    values = with_layout_constraint(values, Layout(major_to_minor=(0, 1, 2, 3)))
+    values = values.transpose(0, 2, 1, 3)
+    values = with_layout_constraint(values, Layout(major_to_minor=(0, 2, 1, 3)))
+    values = values.reshape(rows_out, 2, LPAD)
+    values = with_layout_constraint(values, Layout(major_to_minor=(0, 1, 2)))
+    grid = values.transpose(1, 0, 2).reshape(2, rows_out, 1, LPAD)
+
+    returned = returned.reshape(waves, chips * rows_here, wide)
+    pieces = direct(wave_map, returned, (panel, panels[1]), step, slots)
+    pieces = [pieces[0]] + [across(pieces[i], 2 * i) for i in range(1, chips)]
+    spec_out = join_degrees(pieces, slots).reshape(slots, 1, 2, degrees_all)
+    return (grid, spec_out)
+
+
+def per_device(levels, spec, legendre, gauss_w, cycle_len, wave_map):
+    slot_count = wave_map.shape[0]
+    fits = (
+        spec.shape[3] % slot_count == 0
+        and 2 * slot_count * SUBLANES == LANES
+        and spec.shape[1] == 1
+        and 4 * spec.shape[0] == SUBLANES
+        and levels > 1
+        and levels & (levels - 1) == 0
+    )
+    if fits:
+        return evenly_spaced(levels, spec, legendre, gauss_w, cycle_len, wave_map)
+    return general(spec, legendre, gauss_w, cycle_len, wave_map)
+
+
 def solution(mesh):
     placed = (P("wave", "lev", None, None), P("wave", "lev", None), P(), P(), P())
     return jax.shard_map(
-        per_device,
+        functools.partial(per_device, mesh.shape["lev"]),
         mesh=mesh,
         in_specs=placed,
         out_specs=(P(None, "wave", "lev", None), P("wave", "lev", None, None)),

time: 524 us -> 46.5 us (0.09)
  other arithmetic: 383 us -> 0 us
  waiting for transfers between devices: 53.1 us -> 11.9 us
  local copies, waits for them, and re-layouts: 35.7 us -> 2.54 us
  matrix products: 23.6 us -> 0 us
  starting transfers between devices: 4.64 us -> 18.5 us
  between operations: 14.1 us -> 0.75 us
  Pallas kernels: 0 us -> 12.4 us
  blocking collectives: 7.99 us -> 0 us
    convert_element_type x60 -> x0, other arithmetic: 351 us -> none  [the longest x15 322 us: cycle_tables(): jnp.where(occupied[:, None, :], jnp.cos(angles), 0.0).astype(jnp.bfloat16)]
    all_gather x1 -> x0, waiting for transfers between devices: 49 us -> none  [per_device(): panels = lax.all_gather(legendre, 'lev', axis=1, tiled=True)]
    dot_general x32 -> x0, matrix products: 23.6 us -> none  [the longest x15 9.74 us: cycle_block(): jnp.einsum('rap,rkp->rak', by_cycle, tables, preferred_element_type=jnp.f...]
    dynamic_update_slice x15 -> x0, local copies, waits for them, and re-layouts: 13.2 us -> none  [per_device(): lax.map(run_block, (ordered, lens_here.reshape(blocks, row_block, 2), wei...]
    select_n x62 -> x0, other arithmetic: 12.6 us -> none  [the longest x15 8.5 us: cycle_block(): jnp.where(selector[:, None, :, None, :], squared[:, :, None, :, :], jnp.z...]
    pallas_call x0 -> x7, Pallas kernels: none -> 12.4 us  [the longest x1 4.97 us: grid_values(): pl.pallas_call(kernel, grid=(STEPS,), out_shape=jax.ShapeDtypeStruct((row...]
    another operation x17 -> x0, other arithmetic: 8.32 us -> none  [the longest x15 6.87 us: cycle_block(): selector = jnp.stack([jnp.logical_not(upper_half), upper_half], 1)]
    ppermute x0 -> x7, starting transfers between devices: none -> 8.23 us  [across(): return lax.ppermute(x, 'lev', [(j, j ^ bits) for j in range(levels)])]
  transfers between devices with their start and end apart: 2 -> 9, of which waited for: 2 -> 7; matrix products, arithmetic and copies ran while one was open for 1% -> 0% of each run, Pallas kernels for 0% -> 17%
where the time goes in v2:
time: 46.5 us; the launch traced here: 46.1 us
  starting transfers between devices  18.5 us (40%)
  Pallas kernels  12.4 us (27%)
  waiting for transfers between devices  11.9 us (26%)
  local copies, waits for them, and re-layouts  2.54 us (5%)
  between operations  0.75 us (2%)
    all_to_all x2, starting transfers between devices, same_core(): lax.all_to_all(x, ('wave', 'lev'), 0, 0, tiled=True, axis_index_groups=gr...  10.2 us
    all_to_all x2, waiting for transfers between devices, same_core(): lax.all_to_all(x, ('wave', 'lev'), 0, 0, tiled=True, axis_index_groups=gr...  9 us
    ppermute x7, starting transfers between devices, across(): return lax.ppermute(x, 'lev', [(j, j ^ bits) for j in range(levels)])  8.23 us
    pallas_call x1, Pallas kernels, grid_values(): pl.pallas_call(kernel, grid=(STEPS,), out_shape=jax.ShapeDtypeStruct((row...  4.97 us
    ppermute x7, waiting for transfers between devices, across(): return lax.ppermute(x, 'lev', [(j, j ^ bits) for j in range(levels)])  2.9 us
    unnamed x14, local copies, waits for them, and re-layouts  2.53 us
    pallas_call x1, Pallas kernels, prepare(): pl.pallas_call(kernel, out_shape=(jax.ShapeDtypeStruct((groups, 7, SUBLAN...  2.1 us
    pallas_call x1, Pallas kernels, quadratic(): pl.pallas_call(kernel, out_shape=(jax.ShapeDtypeStruct((2 * slot_count,)...  1.38 us
  transfers between devices with their start and end apart: 9, of which 7 were waited for; matrix products, arithmetic and copies ran while one was open for 0% of the time, Pallas kernels for 17%

profile of v2, /device:TPU:0, one launch (start us, length us, event | category | flops | bytes accessed | tf_op | source)
XLA Modules:
  0.0 46.1 jit_solution(11778851184374176258)
XLA Ops:
  0.6 0.5 %collective-permute-start.3 = (bf16[320,1200]{1,0:T(8,128)(2,1)}, bf16[320,1200]{1,0:T(8,128)(2,1)S(1)}, u32[]{:S(2)}, u32[]{:S(2)}) collective-permute-start(bf16[320,1200]{1,0:T(8,128)(2,1)} %bitcast.19), channel_id=1, source_target_pairs={{0,1},{1,0},{2,3},{3,2},{4,5},{5,4},{6,7},{7,6},{8,9},{9,8},{10,11... | collective-permute-start | bytes 2304008 | tf_op jit(solution)/shard_map/ppermute | solution.py:657
  1.1 3.5 %collective-permute-start.2 = (bf16[2,2,1280]{2,1,0:T(2,128)(2,1)}, bf16[2,2,1280]{2,1,0:T(2,128)(2,1)S(1)}, u32[]{:S(2)}, u32[]{:S(2)}) collective-permute-start(bf16[2,2,1280]{2,1,0:T(2,128)(2,1)} %bitcast.22), channel_id=1, source_target_pairs={{0,6},{1,7},{2,4},{3,5},{4,2},{5,3},{6,0},{7,1},{8,14},{9,15},{10,... | collective-permute-start | bytes 30728 | tf_op jit(solution)/shard_map/ppermute | solution.py:657
  4.7 0.5 %collective-permute-start.1 = (bf16[2,2,1280]{2,1,0:T(2,128)(2,1)}, bf16[2,2,1280]{2,1,0:T(2,128)(2,1)S(1)}, u32[]{:S(2)}, u32[]{:S(2)}) collective-permute-start(bf16[2,2,1280]{2,1,0:T(2,128)(2,1)} %bitcast.23), channel_id=1, source_target_pairs={{0,4},{1,5},{2,6},{3,7},{4,0},{5,1},{6,2},{7,3},{8,12},{9,13},{10,... | collective-permute-start | bytes 30728 | tf_op jit(solution)/shard_map/ppermute | solution.py:657
  5.2 0.1 collective-permute-start
  5.3 0.0 copy-start.1
  5.3 0.7 %copy-done.1 = s32[8]{0:T(128)S(1)} copy-done((s32[8]{0:T(128)S(1)}, s32[8]{0:T(128)}, u32[]{:S(2)}) %copy-start.1) | copy-done | bytes 56
  6.0 0.0 copy-start.3
  6.0 1.1 %copy-done.3 = bf16[2,160,1200]{2,1,0:T(8,128)(2,1)S(1)} copy-done((bf16[2,160,1200]{2,1,0:T(8,128)(2,1)S(1)}, bf16[2,160,1200]{2,1,0:T(8,128)(2,1)}, u32[]{:S(2)}) %copy-start.3) | copy-done | bytes 768024
  7.1 0.0 copy-start.5
  7.1 0.7 %copy-done.5 = bf16[2,1,2,1280]{3,2,1,0:T(2,128)(2,1)S(1)} copy-done((bf16[2,1,2,1280]{3,2,1,0:T(2,128)(2,1)S(1)}, bf16[2,1,2,1280]{3,2,1,0:T(2,128)(2,1)}, u32[]{:S(2)}) %copy-start.5) | copy-done | bytes 10264
  7.8 0.6 %own_rows.1 = (f32[8,1280]{1,0:T(8,128)S(1)}, f32[8,1280]{1,0:T(8,128)S(1)}, bf16[320,1200]{1,0:T(8,128)(2,1)S(1)}) custom-call(s32[8]{0:T(128)S(1)} %copy-done.1, bf16[2,2,1280]{2,1,0:T(2,128)(2,1)S(1)} %bitcast.25, bf16[320,1200]{1,0:T(8,128)(2,1)S(1)} %bitcast.20), custom_call_target="tpu_custom_call" | custom-call | flops 1000000000 | bytes 2000000 | tf_op jit(solution)/shard_map/own_rows/pallas_call | solution.py:189
  8.4 0.0 copy-start.6
  8.4 0.0 copy-start
  8.5 0.0 collective-permute-done.2.refs_2_
  8.5 0.1 collective-permute-done.1.refs_1_
  8.6 0.5 %collective-permute-done.refs_0_ = bf16[2,2,1280]{2,1,0:T(2,128)(2,1)S(1)} collective-permute-done((bf16[2,2,1280]{2,1,0:T(2,128)(2,1)}, bf16[2,2,1280]{2,1,0:T(2,128)(2,1)S(1)}, u32[]{:S(2)}, u32[]{:S(2)}) %collective-permute-start) | collective-permute-done | bytes 10272 | tf_op jit(solution)/shard_map/ppermute | solution.py:657
  9.1 0.0 collective-permute-done.3.refs_4_.other_ref
  9.1 1.3 %partial_fourier.1 = f32[4,4,8,384]{3,2,1,0:T(8,128)} custom-call(f32[8,1280]{1,0:T(8,128)S(1)} %get-tuple-element.16.first_ref, f32[8,1280]{1,0:T(8,128)S(1)} %get-tuple-element.17.factor_ref, bf16[2,2,1280]{2,1,0:T(2,128)(2,1)S(1)} %collective-permute-done.refs_0_, bf16[2,2,1280]{2,1,0:T(2,128)(2,1)S(1)} %collective-permute-done.1.refs_1_, ...), custom_call_target="tpu_custom_call" | custom-call | flops 1000000000 | bytes 2000000 | tf_op jit(solution)/shard_map/partial_fourier/pallas_call | solution.py:242
  10.4 6.7 %all-to-all-start = ((f32[16,8,384]{2,1,0:T(8,128)}), f32[16,8,384]{2,1,0:T(8,128)S(1)}, u32[]{:S(2)}, u32[]{:S(2)}) async-start(f32[16,8,384]{2,1,0:T(8,128)} %bitcast.2), calls=%async_computation | async-start | bytes 393216 | tf_op jit(solution)/shard_map/all_to_all | solution.py:661
  17.1 0.0 copy-done.6
  17.1 0.0 copy-done
  17.1 0.0 copy-start.2
  17.1 2.1 %prepare.1 = (f32[40,7,8,128]{3,2,1,0:T(8,128)S(1)}, f32[8,128]{1,0:T(8,128)S(1)}, f32[8,128]{1,0:T(8,128)S(1)}) custom-call(s32[1200]{0:T(1024)S(1)} %copy-done, s32[1,1200]{1,0:T(1,128)S(1)} %reshape.37.len_row_ref, f32[1,1200]{1,0:T(1,128)S(1)} %reshape.38.weight_row_ref), custom_call_target="tpu_custom_call" | custom-call | flops 3000000000 | bytes 1000000 | tf_op jit(solution)/shard_map/prepare/pallas_call | solution.py:428
  19.3 6.4 %all-to-all-done.x_ref = f32[16,8,384]{2,1,0:T(8,128)S(1)} async-done(((f32[16,8,384]{2,1,0:T(8,128)}), f32[16,8,384]{2,1,0:T(8,128)S(1)}, u32[]{:S(2)}, u32[]{:S(2)}) %all-to-all-start) | async-done | bytes 196640 | tf_op jit(solution)/shard_map/all_to_all | solution.py:661
  25.6 0.0 copy-done.2
  25.6 1.4 %quadratic.1 = (f32[16,8,128]{2,1,0:T(8,128)S(1)}, bf16[16,8,384]{2,1,0:T(8,128)(2,1)}) custom-call(s32[8]{0:T(128)S(1)} %copy-done.2, f32[16,8,384]{2,1,0:T(8,128)S(1)} %all-to-all-done.x_ref, f32[8,128]{1,0:T(8,128)S(1)} %get-tuple-element.19.len_ref, f32[8,128]{1,0:T(8,128)S(1)} %get-tuple-element.20.weight_ref), custom_call_target="tpu_custom_call" | custom-call | tf_op jit(solution)/shard_map/quadratic/pallas_call | solution.py:332
  27.0 3.5 %all-to-all-start.1 = ((bf16[16,8,384]{2,1,0:T(8,128)(2,1)}), bf16[16,8,384]{2,1,0:T(8,128)(2,1)S(1)}, u32[]{:S(2)}, u32[]{:S(2)}) async-start(bf16[16,8,384]{2,1,0:T(8,128)(2,1)} %get-tuple-element.21), calls=%async_computation.1 | async-start | bytes 196608 | tf_op jit(solution)/shard_map/all_to_all | solution.py:661
  30.5 0.0 copy-start.4
  30.5 5.0 %grid_values.1 = bf16[11400,128]{1,0:T(8,128)(2,1)} custom-call(s32[1200]{0:T(1024)S(1)} %copy-done, f32[16,8,128]{2,1,0:T(8,128)S(1)} %get-tuple-element.22.fourier_ref, f32[40,7,8,128]{3,2,1,0:T(8,128)S(1)} %get-tuple-element.23.table_ref), custom_call_target="tpu_custom_call" | custom-call | flops 8000000000 | bytes 3000000 | tf_op jit(solution)/shard_map/grid_values/pallas_call | solution.py:554
  35.5 2.6 %all-to-all-done.1 = bf16[16,8,384]{2,1,0:T(8,128)(2,1)S(1)} async-done(((bf16[16,8,384]{2,1,0:T(8,128)(2,1)}), bf16[16,8,384]{2,1,0:T(8,128)(2,1)S(1)}, u32[]{:S(2)}, u32[]{:S(2)}) %all-to-all-start.1) | async-done | bytes 98336 | tf_op jit(solution)/shard_map/all_to_all | solution.py:661
  38.1 0.0 copy-done.4
  38.1 1.4 %direct.1 = (f32[8,160]{1,0:T(8,128)S(1)}, f32[8,160]{1,0:T(8,128)S(1)}, f32[8,160]{1,0:T(8,128)S(1)}, f32[8,160]{1,0:T(8,128)S(1)}) custom-call(s32[8]{0:T(128)S(1)} %copy-done.2, bf16[4,32,384]{2,1,0:T(8,128)(2,1)S(1)} %bitcast.18, bf16[320,1200]{1,0:T(8,128)(2,1)S(1)} %bitcast.21, bf16[320,1200]{1,0:T(8,128)(2,1)S(1)} %collective-permute-done.3.refs_4_.other_ref), custom_call_target="tpu_custom_call" | custom-call | flops 1000000000 | bytes 2000000 | tf_op jit(solution)/shard_map/direct/pallas_call | solution.py:606
  39.5 1.0 %collective-permute-start.4 = (f32[8,160]{1,0:T(8,128)S(1)}, f32[8,160]{1,0:T(8,128)S(1)}, u32[]{:S(2)}, u32[]{:S(2)}) collective-permute-start(f32[8,160]{1,0:T(8,128)S(1)} %get-tuple-element.27), channel_id=1, source_target_pairs={{0,2},{1,3},{2,0},{3,1},{4,6},{5,7},{6,4},{7,5},{8,10},{9,11},{10,... | collective-permute-start | bytes 15368 | tf_op jit(solution)/shard_map/ppermute | solution.py:657
  40.5 0.3 collective-permute-start.5
  40.8 2.2 %collective-permute-start.6 = (f32[8,160]{1,0:T(8,128)S(1)}, f32[8,160]{1,0:T(8,128)S(1)}, u32[]{:S(2)}, u32[]{:S(2)}) collective-permute-start(f32[8,160]{1,0:T(8,128)S(1)} %get-tuple-element.29), channel_id=1, source_target_pairs={{0,6},{1,7},{2,4},{3,5},{4,2},{5,3},{6,0},{7,1},{8,14},{9,15},{10,... | collective-permute-start | bytes 15368 | tf_op jit(solution)/shard_map/ppermute | solution.py:657
  43.1 0.2 collective-permute-done.4.refs_1_
  43.2 1.0 %collective-permute-done.5.refs_2_ = f32[8,160]{1,0:T(8,128)S(1)} collective-permute-done((f32[8,160]{1,0:T(8,128)S(1)}, f32[8,160]{1,0:T(8,128)S(1)}, u32[]{:S(2)}, u32[]{:S(2)}) %collective-permute-start.5) | collective-permute-done | bytes 5152 | tf_op jit(solution)/shard_map/ppermute | solution.py:657
  44.2 1.2 %collective-permute-done.6.refs_3_ = f32[8,160]{1,0:T(8,128)S(1)} collective-permute-done((f32[8,160]{1,0:T(8,128)S(1)}, f32[8,160]{1,0:T(8,128)S(1)}, u32[]{:S(2)}, u32[]{:S(2)}) %collective-permute-start.6) | collective-permute-done | bytes 5152 | tf_op jit(solution)/shard_map/ppermute | solution.py:657
  45.4 0.7 %join_degrees.1 = f32[2,2,1280]{2,1,0:T(2,128)} custom-call(f32[8,160]{1,0:T(8,128)S(1)} %get-tuple-element.26.refs_0_, f32[8,160]{1,0:T(8,128)S(1)} %collective-permute-done.4.refs_1_, f32[8,160]{1,0:T(8,128)S(1)} %collective-permute-done.5.refs_2_, f32[8,160]{1,0:T(8,128)S(1)} %collective-permute-done.6.refs_3_), custom_call_target="tpu_custom_call" | custom-call | tf_op jit(solution)/shard_map/join_degrees/pallas_call | solution.py:635
  (2 shorter events, 0.0 us)
Async XLA Ops:
  0.6 8.4 %collective-permute-start.3 = (bf16[320,1200]{1,0:T(8,128)(2,1)}, bf16[320,1200]{1,0:T(8,128)(2,1)S(1)}, u32[]{:S(2)}, u32[]{:S(2)}) collective-permute-start(bf16[320,1200]{1,0:T(8,128)(2,1)} %bitcast.19), channel_id=1, source_target_pairs={{0,1},{1,0},{2,3},{3,2},{4,5},{5,4},{6,7},{7,6},{8,9},{9,8},{10,11... | collective-permute-start | bytes 2304008 | tf_op jit(solution)/shard_map/ppermute | solution.py:657
  1.1 7.3 %collective-permute-start.2 = (bf16[2,2,1280]{2,1,0:T(2,128)(2,1)}, bf16[2,2,1280]{2,1,0:T(2,128)(2,1)S(1)}, u32[]{:S(2)}, u32[]{:S(2)}) collective-permute-start(bf16[2,2,1280]{2,1,0:T(2,128)(2,1)} %bitcast.22), channel_id=1, source_target_pairs={{0,6},{1,7},{2,4},{3,5},{4,2},{5,3},{6,0},{7,1},{8,14},{9,15},{10,... | collective-permute-start | bytes 30728 | tf_op jit(solution)/shard_map/ppermute | solution.py:657
  4.7 3.9 %collective-permute-start.1 = (bf16[2,2,1280]{2,1,0:T(2,128)(2,1)}, bf16[2,2,1280]{2,1,0:T(2,128)(2,1)S(1)}, u32[]{:S(2)}, u32[]{:S(2)}) collective-permute-start(bf16[2,2,1280]{2,1,0:T(2,128)(2,1)} %bitcast.23), channel_id=1, source_target_pairs={{0,4},{1,5},{2,6},{3,7},{4,0},{5,1},{6,2},{7,3},{8,12},{9,13},{10,... | collective-permute-start | bytes 30728 | tf_op jit(solution)/shard_map/ppermute | solution.py:657
  5.2 3.9 %collective-permute-start = (bf16[2,2,1280]{2,1,0:T(2,128)(2,1)}, bf16[2,2,1280]{2,1,0:T(2,128)(2,1)S(1)}, u32[]{:S(2)}, u32[]{:S(2)}) collective-permute-start(bf16[2,2,1280]{2,1,0:T(2,128)(2,1)} %bitcast.24), channel_id=1, source_target_pairs={{0,2},{1,3},{2,0},{3,1},{4,6},{5,7},{6,4},{7,5},{8,10},{9,11},{10,... | collective-permute-start | bytes 30728 | tf_op jit(solution)/shard_map/ppermute | solution.py:657
  5.3 0.7 %copy-start.1 = (s32[8]{0:T(128)S(1)}, s32[8]{0:T(128)}, u32[]{:S(2)}) copy-start(s32[8]{0:T(128)} %map_ref.3) | copy-start | bytes 100
  6.0 1.1 %copy-start.3 = (bf16[2,160,1200]{2,1,0:T(8,128)(2,1)S(1)}, bf16[2,160,1200]{2,1,0:T(8,128)(2,1)}, u32[]{:S(2)}) copy-start(bf16[2,160,1200]{2,1,0:T(8,128)(2,1)} %param.6) | copy-start | bytes 2304004
  7.1 0.7 %copy-start.5 = (bf16[2,1,2,1280]{3,2,1,0:T(2,128)(2,1)S(1)}, bf16[2,1,2,1280]{3,2,1,0:T(2,128)(2,1)}, u32[]{:S(2)}) copy-start(bf16[2,1,2,1280]{3,2,1,0:T(2,128)(2,1)} %param.5) | copy-start | bytes 30724
  8.4 8.7 %copy-start.6 = (f32[1200]{0:T(1024)S(1)}, f32[1200]{0:T(1024)}, u32[]{:S(2)}) copy-start(f32[1200]{0:T(1024)} %param.7) | copy-start | bytes 14404
  8.4 8.7 %copy-start = (s32[1200]{0:T(1024)S(1)}, s32[1200]{0:T(1024)}, u32[]{:S(2)}) copy-start(s32[1200]{0:T(1024)} %len_ref.3) | copy-start | bytes 14404
  10.4 15.2 %all-to-all-start = ((f32[16,8,384]{2,1,0:T(8,128)}), f32[16,8,384]{2,1,0:T(8,128)S(1)}, u32[]{:S(2)}, u32[]{:S(2)}) async-start(f32[16,8,384]{2,1,0:T(8,128)} %bitcast.2), calls=%async_computation | async-start | bytes 393216 | tf_op jit(solution)/shard_map/all_to_all | solution.py:661
  17.1 8.5 %copy-start.2 = (s32[8]{0:T(128)S(1)}, s32[8]{0:T(128)}, u32[]{:S(2)}) copy-start(s32[8]{0:T(128)} %map_ref.3) | copy-start | bytes 100
  27.0 11.1 %all-to-all-start.1 = ((bf16[16,8,384]{2,1,0:T(8,128)(2,1)}), bf16[16,8,384]{2,1,0:T(8,128)(2,1)S(1)}, u32[]{:S(2)}, u32[]{:S(2)}) async-start(bf16[16,8,384]{2,1,0:T(8,128)(2,1)} %get-tuple-element.21), calls=%async_computation.1 | async-start | bytes 196608 | tf_op jit(solution)/shard_map/all_to_all | solution.py:661
  30.5 7.6 %copy-start.4 = (bf16[2,160,1200]{2,1,0:T(8,128)(2,1)S(1)}, bf16[2,160,1200]{2,1,0:T(8,128)(2,1)}, u32[]{:S(2)}) copy-start(bf16[2,160,1200]{2,1,0:T(8,128)(2,1)} %param.6) | copy-start | bytes 2304004
  39.5 3.7 %collective-permute-start.4 = (f32[8,160]{1,0:T(8,128)S(1)}, f32[8,160]{1,0:T(8,128)S(1)}, u32[]{:S(2)}, u32[]{:S(2)}) collective-permute-start(f32[8,160]{1,0:T(8,128)S(1)} %get-tuple-element.27), channel_id=1, source_target_pairs={{0,2},{1,3},{2,0},{3,1},{4,6},{5,7},{6,4},{7,5},{8,10},{9,11},{10,... | collective-permute-start | bytes 15368 | tf_op jit(solution)/shard_map/ppermute | solution.py:657
  40.5 3.7 %collective-permute-start.5 = (f32[8,160]{1,0:T(8,128)S(1)}, f32[8,160]{1,0:T(8,128)S(1)}, u32[]{:S(2)}, u32[]{:S(2)}) collective-permute-start(f32[8,160]{1,0:T(8,128)S(1)} %get-tuple-element.28), channel_id=1, source_target_pairs={{0,4},{1,5},{2,6},{3,7},{4,0},{5,1},{6,2},{7,3},{8,12},{9,13},{10,... | collective-permute-start | bytes 15368 | tf_op jit(solution)/shard_map/ppermute | solution.py:657
  40.8 4.5 %collective-permute-start.6 = (f32[8,160]{1,0:T(8,128)S(1)}, f32[8,160]{1,0:T(8,128)S(1)}, u32[]{:S(2)}, u32[]{:S(2)}) collective-permute-start(f32[8,160]{1,0:T(8,128)S(1)} %get-tuple-element.29), channel_id=1, source_target_pairs={{0,6},{1,7},{2,4},{3,5},{4,2},{5,3},{6,0},{7,1},{8,14},{9,15},{10,... | collective-permute-start | bytes 15368 | tf_op jit(solution)/shard_map/ppermute | solution.py:657

commit v3 on v2

--- a/solution.py
+++ b/solution.py
@@ -159,47 +159,55 @@
     return pl.BlockSpec(memory_space=pltpu.VMEM)
 
 
-def own_rows(wave_map, spec, panel, step):
+def parity_signs(rows, degrees_all):
+    def kernel(o_ref):
+        row = lax.broadcasted_iota(jnp.int32, (rows, degrees_all), 0)
+        degree = lax.broadcasted_iota(jnp.int32, (rows, degrees_all), 1)
+        odd = jnp.logical_and(row >= rows // 2, (degree & 1) == 1)
+        o_ref[...] = jnp.where(odd, -1.0, 1.0)
+
+    return pl.pallas_call(
+        kernel,
+        out_shape=jax.ShapeDtypeStruct((rows, degrees_all), jnp.float32),
+        out_specs=vmem(),
+        compiler_params=params(),
+        cost_estimate=cost(4 * 10**9, 10**6),
+        name="parity_signs",
+    )()
+
+
+def own_rows(wave_map, spec, panel, signs, step):
     slots, parts, degrees_all = spec.shape
     rows = 2 * slots * parts
 
-    def kernel(map_hbm, x_hbm, panel_hbm, o_ref, factor_ref, near_ref, map_ref, x_ref, sems):
-        copies = [
-            pltpu.make_async_copy(a, b, sems.at[i])
-            for i, (a, b) in enumerate(((map_hbm, map_ref), (x_hbm, x_ref), (panel_hbm, near_ref)))
-        ]
-        for copy in copies:
-            copy.start()
-        copies[0].wait()
+    def kernel(map_ref, x_ref, panel_ref, sign_ref, o_ref, factor_ref, near_ref, sem):
+        copy = pltpu.make_async_copy(panel_ref, near_ref, sem)
+        copy.start()
         row = lax.broadcasted_iota(jnp.int32, (rows, degrees_all), 0)
         degree = lax.broadcasted_iota(jnp.int32, (rows, degrees_all), 1)
         order = jnp.zeros((rows, degrees_all), jnp.int32)
         for s in range(slots):
             mine = row // parts % slots == s
             order = jnp.where(mine, map_ref[at_wave() * slots + s] * step, order)
-        odd = jnp.logical_and(row >= rows // 2, ((degree + order) & 1) == 1)
-        factor = jnp.where(degree >= order, jnp.where(odd, -1.0, 1.0), 0.0)
+        turned = jnp.logical_and(row >= rows // 2, (order & 1) == 1)
+        sign = sign_ref[...]
+        factor = jnp.where(degree >= order, jnp.where(turned, -sign, sign), 0.0)
         factor_ref[...] = factor
-        copies[1].wait()
         x = [x_ref[s].astype(jnp.float32) for s in range(slots)]
         o_ref[...] = jnp.concatenate(x + x, axis=0) * factor
-        copies[2].wait()
+        copy.wait()
 
     flat = jax.ShapeDtypeStruct((rows, degrees_all), jnp.float32)
     return pl.pallas_call(
         kernel,
         out_shape=(flat, flat, jax.ShapeDtypeStruct(panel.shape, panel.dtype)),
-        in_specs=[pl.BlockSpec(memory_space=pltpu.HBM)] * 3,
+        in_specs=[smem(), vmem(), pl.BlockSpec(memory_space=pl.ANY), vmem()],
         out_specs=(vmem(),) * 3,
-        scratch_shapes=[
-            pltpu.SMEM(wave_map.shape, wave_map.dtype),
-            pltpu.VMEM(spec.shape, spec.dtype),
-            pltpu.SemaphoreType.DMA((3,)),
-        ],
+        scratch_shapes=[pltpu.SemaphoreType.DMA],
         compiler_params=params(),
         cost_estimate=cost(10**9, 2 * 10**6),
         name="own_rows",
-    )(wave_map, spec, panel)
+    )(wave_map, spec, panel, signs)
 
 
 def partial_fourier(first, factor, others, panels, slots, waves, wide):
@@ -251,34 +259,45 @@
     )(first, factor, *others, *panels)
 
 
-def quadratic(wave_map, parts_sum, lens, weights, waves, step):
+def quadratic(held, parts_sum, lens, weights, waves, step):
     sources, rows, wide = parts_sum.shape
-    slot_count = wave_map.shape[0]
+    slot_count = held.shape[0]
     levels = sources // waves
     slots = slot_count // waves
     tiles = wide // LANES
     top = 2 * (slot_count - 1)
     shape = (SUBLANES, LANES)
 
-    def kernel(map_ref, x_ref, len_ref, weight_ref, g_ref, o_ref, z_ref, r_ref, s_ref):
+    def kernel(held_ref, x_ref, len_ref, weight_ref, g_ref, o_ref, z_ref, r_ref, s_ref):
+        half = rows // 2
         z_ref[...] = jnp.zeros(z_ref.shape, jnp.float32)
         for i in range(waves):
             total = x_ref[i * levels].astype(jnp.float32)
             for j in range(1, levels):
                 total = total + x_ref[i * levels + j].astype(jnp.float32)
             total = total.astype(jnp.bfloat16).astype(jnp.float32)
-            for row in range(rows):
-                h, s, c = row // (2 * slots), row // 2 % slots, row % 2
-                at = map_ref[i * slots + s] * 2 + c
+            for h in range(2):
                 for t in range(tiles):
-                    k = h * tiles + t
-                    z_ref[at, k : k + 1, :] = total[row : row + 1, t * LANES : (t + 1) * LANES]
+                    at = i * half * SUBLANES + h * (SUBLANES // 2) + t
+                    z_ref[pl.ds(at, half, stride=SUBLANES), :] = total[
+                        h * half : (h + 1) * half, t * LANES : (t + 1) * LANES
+                    ]
         lens_here = len_ref[...]
         kept = [
             jnp.where(lens_here > 2.0 * step * w, 1.0, 0.0) for w in range(slot_count)
         ]
-        real = [z_ref[2 * w] * kept[w] for w in range(slot_count)]
-        imag = [z_ref[2 * w + 1] * kept[w] for w in range(slot_count)]
+        held = [
+            [held_ref[w, i : i + 1, :] > 0.5 for i in range(slot_count)] for w in range(slot_count)
+        ]
+        real, imag = [], []
+        for w in range(slot_count):
+            re, im = jnp.zeros(shape, jnp.float32), jnp.zeros(shape, jnp.float32)
+            for i in range(slot_count):
+                at = i * 2 * SUBLANES
+                re = jnp.where(held[w][i], z_ref[at : at + SUBLANES, :], re)
+                im = jnp.where(held[w][i], z_ref[at + SUBLANES : at + 2 * SUBLANES, :], im)
+            real.append(re * kept[w])
+            imag.append(im * kept[w])
         for w in range(slot_count):
             double = 1.0 if w == 0 else 2.0
             g_ref[2 * w] = real[w] * double
@@ -307,6 +326,7 @@
             for d in range(3, top + slot_count)
         }
         weights_here = weight_ref[...]
+        result = []
         for w in range(slot_count):
             re, im = square_real[w], square_imag[w]
             if w == 0:
@@ -316,15 +336,22 @@
                     re = re + whole[w + n] * square_real[n]
                     im = im - whole[w + n] * square_imag[n]
             factor = kept[w] * weights_here
-            r_ref[2 * w] = re * factor
-            r_ref[2 * w + 1] = im * factor
+            result.append((re * factor, im * factor))
+        for i in range(slot_count):
+            re, im = result[0]
+            for w in range(1, slot_count):
+                re = jnp.where(held[w][i], result[w][0], re)
+                im = jnp.where(held[w][i], result[w][1], im)
+            at = i * 2 * SUBLANES
+            r_ref[at : at + SUBLANES, :] = re
+            r_ref[at + SUBLANES : at + 2 * SUBLANES, :] = im
         for i in range(waves):
-            for row in range(rows):
-                h, s, c = row // (2 * slots), row // 2 % slots, row % 2
-                at = map_ref[i * slots + s] * 2 + c
+            for h in range(2):
                 for t in range(tiles):
-                    k = h * tiles + t
-                    s_ref[row : row + 1, t * LANES : (t + 1) * LANES] = r_ref[at, k : k + 1, :]
+                    start = i * half * SUBLANES + h * (SUBLANES // 2) + t
+                    s_ref[h * half : (h + 1) * half, t * LANES : (t + 1) * LANES] = r_ref[
+                        pl.ds(start, half, stride=SUBLANES), :
+                    ]
             packed = s_ref[...].astype(jnp.bfloat16)
             for j in range(levels):
                 o_ref[i * levels + j] = packed
@@ -335,16 +362,16 @@
             jax.ShapeDtypeStruct((2 * slot_count,) + shape, jnp.float32),
             jax.ShapeDtypeStruct((sources, rows, wide), jnp.bfloat16),
         ),
-        in_specs=[smem(), vmem(), vmem(), vmem()],
+        in_specs=[vmem()] * 4,
         out_specs=(vmem(), vmem()),
         scratch_shapes=[
-            pltpu.VMEM((2 * slot_count,) + shape, jnp.float32),
-            pltpu.VMEM((2 * slot_count,) + shape, jnp.float32),
+            pltpu.VMEM((2 * slot_count * SUBLANES, LANES), jnp.float32),
+            pltpu.VMEM((2 * slot_count * SUBLANES, LANES), jnp.float32),
             pltpu.VMEM((rows, wide), jnp.float32),
         ],
         compiler_params=params(),
         name="quadratic",
-    )(wave_map, parts_sum, lens, weights)
+    )(held, parts_sum, lens, weights)
 
 
 def lane_facts(slot_count):
@@ -358,12 +385,31 @@
     return at // 2, jnp.logical_and(at >= 0, at < span)
 
 
-def prepare(cycle_len, gauss_w, span, slot_count, step, waves, groups, wide):
+def prepare(cycle_len, gauss_w, wave_map, factor, span, step, waves, groups, wide, own):
+    slot_count = wave_map.shape[0]
+    slots = slot_count // waves
+    rows, degrees_all = factor.shape
+    levels = degrees_all // own
     here = cycle_len.shape[0] // waves
     tiles = wide // LANES
     per = SUBLANES // 2
 
-    def kernel(len_ref, len_row_ref, weight_row_ref, o_ref, lens_ref, weights_ref):
+    def kernel(
+        len_ref, map_ref, len_row_ref, weight_row_ref, factor_ref, o_ref, lens_ref, weights_ref, held_ref, near_ref
+    ):
+        for i in range(slot_count):
+            where = map_ref[i]
+            for w in range(slot_count):
+                held = jnp.where(where == w, 1.0, 0.0)
+                held_ref[w, i : i + 1, :] = jnp.full((1, LANES), held, jnp.float32)
+        for level in range(levels):
+
+            @pl.when(at_level() == level)
+            def _(level=level):
+                for e in range(2):
+                    start = (level ^ e) * own
+                    near_ref[e] = factor_ref[:, start : start + own]
+
         wave, part, row, cycle = lane_facts(slot_count)
         tile, _ = tile_of_row(0, span, slot_count)
         first = (tile * LANES).astype(jnp.float32)
@@ -420,20 +466,26 @@
                     lens = len_row_ref[:, at : at + size].astype(jnp.float32)
                     weights = weight_row_ref[:, at : at + size]
                     for h in range(2):
-                        k = h * tiles + t
+                        k = h * (SUBLANES // 2) + t
                         lens_ref[k : k + 1, 0:size] = lens
                         weights_ref[k : k + 1, 0:size] = weights
 
     flat = jax.ShapeDtypeStruct((SUBLANES, LANES), jnp.float32)
     return pl.pallas_call(
         kernel,
-        out_shape=(jax.ShapeDtypeStruct((groups, 7, SUBLANES, LANES), jnp.float32), flat, flat),
-        in_specs=[smem(), vmem(), vmem()],
-        out_specs=(vmem(),) * 3,
+        out_shape=(
+            jax.ShapeDtypeStruct((groups, 7, SUBLANES, LANES), jnp.float32),
+            flat,
+            flat,
+            jax.ShapeDtypeStruct((slot_count, slot_count, LANES), jnp.float32),
+            jax.ShapeDtypeStruct((2, rows, own), jnp.float32),
+        ),
+        in_specs=[smem()] * 2 + [vmem()] * 3,
+        out_specs=(vmem(),) * 5,
         compiler_params=params(),
         cost_estimate=cost(3 * 10**9, 10**6),
         name="prepare",
-    )(cycle_len, cycle_len.reshape(1, -1), gauss_w.reshape(1, -1))
+    )(cycle_len, wave_map, cycle_len.reshape(1, -1), gauss_w.reshape(1, -1), factor)
 
 
 def grid_values(cycle_len, fourier, tables, span, slot_count, rows_out, tiles):
@@ -463,7 +515,7 @@
                     for w in range(slot_count):
                         for t in range(tiles):
                             at = (c * 2 + h) * slot_count + w
-                            k = h * tiles + t
+                            k = h * (SUBLANES // 2) + t
                             rows_ref[t, at : at + 1, :] = fourier_ref[2 * w + c, k : k + 1, :]
 
         pick = lax.broadcasted_iota(jnp.int32, (LANES, LANES), 0)
@@ -571,34 +623,28 @@
     )(cycle_len, fourier, tables)
 
 
-def direct(wave_map, returned, panels, step, slots):
+def direct(returned, factors, panels):
     waves, tall, _ = returned.shape
     depth, lats = panels[0].shape
-    own, here = depth // slots, lats // waves
-    half = 2 * slots
+    own, here = factors.shape[2], lats // waves
+    slots, half = depth // own, factors.shape[1] // 2
     chips = tall // (2 * half)
 
-    def kernel(map_ref, x_ref, own_ref, other_ref, *refs):
+    def kernel(x_ref, factor_ref, own_ref, other_ref, *refs):
         o_refs, left_ref, all_ref = refs[:chips], refs[chips], refs[chips + 1]
         for j in range(waves):
             left_ref[:, j * here : (j + 1) * here] = x_ref[j, :, 0:here].astype(jnp.float32)
         left = left_ref[...].astype(jnp.bfloat16)
         shape = (chips, half, own)
         slot_of = lax.broadcasted_iota(jnp.int32, shape, 1) // 2
-        lane = lax.broadcasted_iota(jnp.int32, shape, 2)
         for e, panel_ref in enumerate((own_ref, other_ref)):
             total = lax.dot_general(
                 left, panel_ref[...], (((1,), (1,)), ((), ())), preferred_element_type=jnp.float32
             ).reshape(chips, 2 * half, depth)
-            degree = lane + (at_level() ^ e) * own
             result = jnp.zeros(shape, jnp.float32)
             for s in range(slots):
-                order = map_ref[at_wave() * slots + s] * step
-                mine = total[:, :, s * own : (s + 1) * own]
-                sign = (1 - 2 * ((degree + order) & 1)).astype(jnp.float32)
-                value = mine[:, :half] + sign * mine[:, half:]
-                keep = jnp.logical_and(slot_of == s, degree >= order)
-                result = jnp.where(keep, value, result)
+                mine = total[:, :, s * own : (s + 1) * own] * factor_ref[e][None]
+                result = jnp.where(slot_of == s, mine[:, :half] + mine[:, half:], result)
             all_ref[:, e * half : (e + 1) * half, :] = result
         for i in range(chips):
             o_refs[i][...] = all_ref[(at_level() // 2) ^ i]
@@ -606,7 +652,7 @@
     return pl.pallas_call(
         kernel,
         out_shape=(jax.ShapeDtypeStruct((2 * half, own), jnp.float32),) * chips,
-        in_specs=[smem()] + [vmem()] * 3,
+        in_specs=[vmem()] * 4,
         out_specs=(vmem(),) * chips,
         scratch_shapes=[
             pltpu.VMEM((tall, lats), jnp.float32),
@@ -615,7 +661,7 @@
         compiler_params=params(),
         cost_estimate=cost(10**9, 2 * 10**6),
         name="direct",
-    )(wave_map, returned, *panels)
+    )(returned, factors, *panels)
 
 
 def join_degrees(pieces, slots):
@@ -663,7 +709,8 @@
     mine = spec.reshape(slots, 2, degrees_all)
     others = [across(mine, 2 * i) for i in range(1, chips)]
     panel = legendre.reshape(slots * own, lats)
-    first, factor, near = own_rows(wave_map, mine, panel, step)
+    signs = parity_signs(2 * slots * 2, degrees_all)
+    first, factor, near = own_rows(wave_map, mine, panel, signs, step)
     panels = (near, across(panel, 1))
 
     here = lats // waves
@@ -677,10 +724,10 @@
 
     part = partial_fourier(first, factor, others, panels, slots, waves, wide)
     part = same_core(part.reshape(waves * chips, rows_here, wide))
-    tables, lens, weights = prepare(
-        cycle_len, gauss_w, span, slot_count, step, waves, groups, wide
+    tables, lens, weights, held, factors = prepare(
+        cycle_len, gauss_w, wave_map, factor, span, step, waves, groups, wide, own
     )
-    fourier, returned = quadratic(wave_map, part, lens, weights, waves, step)
+    fourier, returned = quadratic(held, part, lens, weights, waves, step)
     returned = same_core(returned)
 
     values = grid_values(cycle_len, fourier, tables, span, slot_count, rows_out, tiles)
@@ -694,7 +741,7 @@
     grid = values.transpose(1, 0, 2).reshape(2, rows_out, 1, LPAD)
 
     returned = returned.reshape(waves, chips * rows_here, wide)
-    pieces = direct(wave_map, returned, (panel, panels[1]), step, slots)
+    pieces = direct(returned, factors, (panel, panels[1]))
     pieces = [pieces[0]] + [across(pieces[i], 2 * i) for i in range(1, chips)]
     spec_out = join_degrees(pieces, slots).reshape(slots, 1, 2, degrees_all)
     return (grid, spec_out)

time: 46.5 us -> 44.1 us (0.948)
  local copies, waits for them, and re-layouts: 2.54 us -> 0.03 us
  waiting for transfers between devices: 11.9 us -> 13.8 us
  Pallas kernels: 12.4 us -> 11.5 us
  starting transfers between devices: 18.5 us -> 17.7 us
    unnamed x14 -> x10, local copies, waits for them, and re-layouts: 2.53 us -> 0.02 us
    ppermute x7, waiting for transfers between devices: 2.9 us -> 5.3 us  [across(): return lax.ppermute(x, 'lev', [(j, j ^ bits) for j in range(levels)])]
    all_to_all x2, starting transfers between devices: 10.2 us -> 9.44 us  [same_core(): lax.all_to_all(x, ('wave', 'lev'), 0, 0, tiled=True, axis_index_groups=gr...]
    pallas_call x1, Pallas kernels: 1.36 us -> 0.76 us  [direct(): pl.pallas_call(kernel, out_shape=(jax.ShapeDtypeStruct((2 * half, own), j...]
    all_to_all x2, waiting for transfers between devices: 9 us -> 8.47 us  [same_core(): lax.all_to_all(x, ('wave', 'lev'), 0, 0, tiled=True, axis_index_groups=gr...]
    pallas_call x1, Pallas kernels: 1.38 us -> 0.88 us  [quadratic(): pl.pallas_call(kernel, out_shape=(jax.ShapeDtypeStruct((2 * slot_count,)...]
  transfers between devices with their start and end apart: 9 -> 9, of which waited for: 7 -> 8; matrix products, arithmetic and copies ran while one was open for 0% -> 0% of each run, Pallas kernels for 17% -> 18%
where the time goes in v3:
time: 44.1 us; the launch traced here: 43.8 us
  starting transfers between devices  17.7 us (40%)
  waiting for transfers between devices  13.8 us (31%)
  Pallas kernels  11.5 us (26%)
  between operations  0.75 us (2%)
    all_to_all x2, starting transfers between devices, same_core(): lax.all_to_all(x, ('wave', 'lev'), 0, 0, tiled=True, axis_index_groups=gr...  9.44 us
    all_to_all x2, waiting for transfers between devices, same_core(): lax.all_to_all(x, ('wave', 'lev'), 0, 0, tiled=True, axis_index_groups=gr...  8.47 us
    ppermute x7, starting transfers between devices, across(): return lax.ppermute(x, 'lev', [(j, j ^ bits) for j in range(levels)])  8.26 us
    ppermute x7, waiting for transfers between devices, across(): return lax.ppermute(x, 'lev', [(j, j ^ bits) for j in range(levels)])  5.3 us
    pallas_call x1, Pallas kernels, grid_values(): pl.pallas_call(kernel, grid=(STEPS,), out_shape=jax.ShapeDtypeStruct((row...  4.96 us
    pallas_call x1, Pallas kernels, prepare(): pl.pallas_call(kernel, out_shape=(jax.ShapeDtypeStruct((groups, 7, SUBLAN...  2.23 us
    pallas_call x1, Pallas kernels, partial_fourier(): pl.pallas_call(kernel, out_shape=jax.ShapeDtypeStruct((waves, chips, rows...  1.3 us
  transfers between devices with their start and end apart: 9, of which 8 were waited for; matrix products, arithmetic and copies ran while one was open for 0% of the time, Pallas kernels for 18%

profile of v3, /device:TPU:0, one launch (start us, length us, event | category | flops | bytes accessed | tf_op | source)
XLA Modules:
  0.0 43.8 jit_solution(4296043952789967856)
XLA Ops:
  0.6 0.5 %collective-permute-start.3 = (bf16[320,1200]{1,0:T(8,128)(2,1)}, bf16[320,1200]{1,0:T(8,128)(2,1)S(1)}, u32[]{:S(2)}, u32[]{:S(2)}) collective-permute-start(bf16[320,1200]{1,0:T(8,128)(2,1)} %bitcast.19), channel_id=1, source_target_pairs={{0,1},{1,0},{2,3},{3,2},{4,5},{5,4},{6,7},{7,6},{8,9},{9,8},{10,11... | collective-permute-start | bytes 2304008 | tf_op jit(solution)/shard_map/ppermute | solution.py:703
  1.1 0.0 copy-start.1
  1.1 0.0 copy-start.2
  1.2 0.0 copy-start.3
  1.2 3.5 %collective-permute-start.2 = (bf16[2,2,1280]{2,1,0:T(2,128)(2,1)}, bf16[2,2,1280]{2,1,0:T(2,128)(2,1)S(1)}, u32[]{:S(2)}, u32[]{:S(2)}) collective-permute-start(bf16[2,2,1280]{2,1,0:T(2,128)(2,1)} %bitcast.22), channel_id=1, source_target_pairs={{0,6},{1,7},{2,4},{3,5},{4,2},{5,3},{6,0},{7,1},{8,14},{9,15},{10,... | collective-permute-start | bytes 30728 | tf_op jit(solution)/shard_map/ppermute | solution.py:703
  4.7 0.5 %collective-permute-start.1 = (bf16[2,2,1280]{2,1,0:T(2,128)(2,1)}, bf16[2,2,1280]{2,1,0:T(2,128)(2,1)S(1)}, u32[]{:S(2)}, u32[]{:S(2)}) collective-permute-start(bf16[2,2,1280]{2,1,0:T(2,128)(2,1)} %bitcast.23), channel_id=1, source_target_pairs={{0,4},{1,5},{2,6},{3,7},{4,0},{5,1},{6,2},{7,3},{8,12},{9,13},{10,... | collective-permute-start | bytes 30728 | tf_op jit(solution)/shard_map/ppermute | solution.py:703
  5.2 0.1 collective-permute-start
  5.4 0.0 copy-done.1
  5.4 0.0 copy-done.2
  5.4 0.0 copy-done.3
  5.4 0.7 %own_rows.1 = (f32[8,1280]{1,0:T(8,128)S(1)}, f32[8,1280]{1,0:T(8,128)S(1)}, bf16[320,1200]{1,0:T(8,128)(2,1)S(1)}) custom-call(s32[8]{0:T(128)S(1)} %copy-done.3, bf16[2,2,1280]{2,1,0:T(2,128)(2,1)S(1)} %bitcast.25, bf16[320,1200]{1,0:T(8,128)(2,1)S(1)} %bitcast.20, f32[8,1280]{1,0:T(8,128)S(1)} %parity_signs.1.sign_ref), custom_call_target="tpu_custom_call" | custom-call | flops 1000000000 | bytes 2000000 | tf_op jit(solution)/shard_map/own_rows/pallas_call | solution.py:201
  6.1 0.0 copy-start.4
  6.1 0.0 copy-start
  6.1 0.5 %collective-permute-done.2.refs_2_ = bf16[2,2,1280]{2,1,0:T(2,128)(2,1)S(1)} collective-permute-done((bf16[2,2,1280]{2,1,0:T(2,128)(2,1)}, bf16[2,2,1280]{2,1,0:T(2,128)(2,1)S(1)}, u32[]{:S(2)}, u32[]{:S(2)}) %collective-permute-start.2) | collective-permute-done | bytes 10272 | tf_op jit(solution)/shard_map/ppermute | solution.py:703
  6.6 2.0 %collective-permute-done.1.refs_1_ = bf16[2,2,1280]{2,1,0:T(2,128)(2,1)S(1)} collective-permute-done((bf16[2,2,1280]{2,1,0:T(2,128)(2,1)}, bf16[2,2,1280]{2,1,0:T(2,128)(2,1)S(1)}, u32[]{:S(2)}, u32[]{:S(2)}) %collective-permute-start.1) | collective-permute-done | bytes 10272 | tf_op jit(solution)/shard_map/ppermute | solution.py:703
  8.6 0.5 %collective-permute-done.refs_0_ = bf16[2,2,1280]{2,1,0:T(2,128)(2,1)S(1)} collective-permute-done((bf16[2,2,1280]{2,1,0:T(2,128)(2,1)}, bf16[2,2,1280]{2,1,0:T(2,128)(2,1)S(1)}, u32[]{:S(2)}, u32[]{:S(2)}) %collective-permute-start) | collective-permute-done | bytes 10272 | tf_op jit(solution)/shard_map/ppermute | solution.py:703
  9.1 0.0 collective-permute-done.3.refs_4_.other_ref
  9.1 1.3 %partial_fourier.1 = f32[4,4,8,384]{3,2,1,0:T(8,128)} custom-call(f32[8,1280]{1,0:T(8,128)S(1)} %get-tuple-element.20.first_ref, f32[8,1280]{1,0:T(8,128)S(1)} %get-tuple-element.18.factor_ref, bf16[2,2,1280]{2,1,0:T(2,128)(2,1)S(1)} %collective-permute-done.refs_0_, bf16[2,2,1280]{2,1,0:T(2,128)(2,1)S(1)} %collective-permute-done.1.refs_1_, ...), custom_call_target="tpu_custom_call" | custom-call | flops 1000000000 | bytes 2000000 | tf_op jit(solution)/shard_map/partial_fourier/pallas_call | solution.py:250
  10.4 5.9 %all-to-all-start = ((f32[16,8,384]{2,1,0:T(8,128)}), f32[16,8,384]{2,1,0:T(8,128)S(1)}, u32[]{:S(2)}, u32[]{:S(2)}) async-start(f32[16,8,384]{2,1,0:T(8,128)} %bitcast.2), calls=%async_computation | async-start | bytes 393216 | tf_op jit(solution)/shard_map/all_to_all | solution.py:707
  16.3 0.0 copy-done.4
  16.4 0.0 copy-done
  16.4 2.2 %prepare.1 = (f32[40,7,8,128]{3,2,1,0:T(8,128)S(1)}, f32[8,128]{1,0:T(8,128)S(1)}, f32[8,128]{1,0:T(8,128)S(1)}, f32[8,8,128]{2,1,0:T(8,128)S(1)}, f32[2,8,160]{2,1,0:T(8,128)S(1)}) custom-call(s32[1200]{0:T(1024)S(1)} %copy-done, s32[8]{0:T(128)S(1)} %copy-done.3, s32[1,1200]{1,0:T(1,128)S(1)} %reshape.34.len_row_ref, ...), custom_call_target="tpu_custom_call" | custom-call | flops 3000000000 | bytes 1000000 | tf_op jit(solution)/shard_map/prepare/pallas_call | solution.py:474
  18.6 5.8 %all-to-all-done.x_ref = f32[16,8,384]{2,1,0:T(8,128)S(1)} async-done(((f32[16,8,384]{2,1,0:T(8,128)}), f32[16,8,384]{2,1,0:T(8,128)S(1)}, u32[]{:S(2)}, u32[]{:S(2)}) %all-to-all-start) | async-done | bytes 196640 | tf_op jit(solution)/shard_map/all_to_all | solution.py:707
  24.4 0.9 %quadratic.1 = (f32[16,8,128]{2,1,0:T(8,128)S(1)}, bf16[16,8,384]{2,1,0:T(8,128)(2,1)}) custom-call(f32[8,8,128]{2,1,0:T(8,128)S(1)} %get-tuple-element.19.held_ref, f32[16,8,384]{2,1,0:T(8,128)S(1)} %all-to-all-done.x_ref, f32[8,128]{1,0:T(8,128)S(1)} %get-tuple-element.22.len_ref, f32[8,128]{1,0:T(8,128)S(1)} %get-tuple-element.23.weight_ref), custom_call_target="tpu_custom_call" | custom-call | tf_op jit(solution)/shard_map/quadratic/pallas_call | solution.py:359
  25.3 3.5 %all-to-all-start.1 = ((bf16[16,8,384]{2,1,0:T(8,128)(2,1)}), bf16[16,8,384]{2,1,0:T(8,128)(2,1)S(1)}, u32[]{:S(2)}, u32[]{:S(2)}) async-start(bf16[16,8,384]{2,1,0:T(8,128)(2,1)} %get-tuple-element.24), calls=%async_computation.1 | async-start | bytes 196608 | tf_op jit(solution)/shard_map/all_to_all | solution.py:707
  28.8 5.0 %grid_values.1 = bf16[11400,128]{1,0:T(8,128)(2,1)} custom-call(s32[1200]{0:T(1024)S(1)} %copy-done, f32[16,8,128]{2,1,0:T(8,128)S(1)} %get-tuple-element.25.fourier_ref, f32[40,7,8,128]{3,2,1,0:T(8,128)S(1)} %get-tuple-element.26.table_ref), custom_call_target="tpu_custom_call" | custom-call | flops 8000000000 | bytes 3000000 | tf_op jit(solution)/shard_map/grid_values/pallas_call | solution.py:606
  33.8 2.7 %all-to-all-done.1 = bf16[16,8,384]{2,1,0:T(8,128)(2,1)S(1)} async-done(((bf16[16,8,384]{2,1,0:T(8,128)(2,1)}), bf16[16,8,384]{2,1,0:T(8,128)(2,1)S(1)}, u32[]{:S(2)}, u32[]{:S(2)}) %all-to-all-start.1) | async-done | bytes 98336 | tf_op jit(solution)/shard_map/all_to_all | solution.py:707
  36.4 0.8 %direct.1 = (f32[8,160]{1,0:T(8,128)S(1)}, f32[8,160]{1,0:T(8,128)S(1)}, f32[8,160]{1,0:T(8,128)S(1)}, f32[8,160]{1,0:T(8,128)S(1)}) custom-call(bf16[4,32,384]{2,1,0:T(8,128)(2,1)S(1)} %bitcast.18, f32[2,8,160]{2,1,0:T(8,128)S(1)} %get-tuple-element.29.factor_ref, bf16[320,1200]{1,0:T(8,128)(2,1)S(1)} %bitcast.21, ...), custom_call_target="tpu_custom_call" | custom-call | flops 1000000000 | bytes 2000000 | tf_op jit(solution)/shard_map/direct/pallas_call | solution.py:652
  37.2 1.0 %collective-permute-start.4 = (f32[8,160]{1,0:T(8,128)S(1)}, f32[8,160]{1,0:T(8,128)S(1)}, u32[]{:S(2)}, u32[]{:S(2)}) collective-permute-start(f32[8,160]{1,0:T(8,128)S(1)} %get-tuple-element.31), channel_id=1, source_target_pairs={{0,2},{1,3},{2,0},{3,1},{4,6},{5,7},{6,4},{7,5},{8,10},{9,11},{10,... | collective-permute-start | bytes 15368 | tf_op jit(solution)/shard_map/ppermute | solution.py:703
  38.2 0.3 collective-permute-start.5
  38.5 2.2 %collective-permute-start.6 = (f32[8,160]{1,0:T(8,128)S(1)}, f32[8,160]{1,0:T(8,128)S(1)}, u32[]{:S(2)}, u32[]{:S(2)}) collective-permute-start(f32[8,160]{1,0:T(8,128)S(1)} %get-tuple-element.33), channel_id=1, source_target_pairs={{0,6},{1,7},{2,4},{3,5},{4,2},{5,3},{6,0},{7,1},{8,14},{9,15},{10,... | collective-permute-start | bytes 15368 | tf_op jit(solution)/shard_map/ppermute | solution.py:703
  40.8 0.2 collective-permute-done.4.refs_1_
  40.9 1.0 %collective-permute-done.5.refs_2_ = f32[8,160]{1,0:T(8,128)S(1)} collective-permute-done((f32[8,160]{1,0:T(8,128)S(1)}, f32[8,160]{1,0:T(8,128)S(1)}, u32[]{:S(2)}, u32[]{:S(2)}) %collective-permute-start.5) | collective-permute-done | bytes 5152 | tf_op jit(solution)/shard_map/ppermute | solution.py:703
  41.9 1.2 %collective-permute-done.6.refs_3_ = f32[8,160]{1,0:T(8,128)S(1)} collective-permute-done((f32[8,160]{1,0:T(8,128)S(1)}, f32[8,160]{1,0:T(8,128)S(1)}, u32[]{:S(2)}, u32[]{:S(2)}) %collective-permute-start.6) | collective-permute-done | bytes 5152 | tf_op jit(solution)/shard_map/ppermute | solution.py:703
  43.1 0.7 %join_degrees.1 = f32[2,2,1280]{2,1,0:T(2,128)} custom-call(f32[8,160]{1,0:T(8,128)S(1)} %get-tuple-element.30.refs_0_, f32[8,160]{1,0:T(8,128)S(1)} %collective-permute-done.4.refs_1_, f32[8,160]{1,0:T(8,128)S(1)} %collective-permute-done.5.refs_2_, f32[8,160]{1,0:T(8,128)S(1)} %collective-permute-done.6.refs_3_), custom_call_target="tpu_custom_call" | custom-call | tf_op jit(solution)/shard_map/join_degrees/pallas_call | solution.py:681
  (3 shorter events, 0.0 us)
Async XLA Ops:
  0.6 8.5 %collective-permute-start.3 = (bf16[320,1200]{1,0:T(8,128)(2,1)}, bf16[320,1200]{1,0:T(8,128)(2,1)S(1)}, u32[]{:S(2)}, u32[]{:S(2)}) collective-permute-start(bf16[320,1200]{1,0:T(8,128)(2,1)} %bitcast.19), channel_id=1, source_target_pairs={{0,1},{1,0},{2,3},{3,2},{4,5},{5,4},{6,7},{7,6},{8,9},{9,8},{10,11... | collective-permute-start | bytes 2304008 | tf_op jit(solution)/shard_map/ppermute | solution.py:703
  1.1 4.2 %copy-start.1 = (bf16[2,160,1200]{2,1,0:T(8,128)(2,1)S(1)}, bf16[2,160,1200]{2,1,0:T(8,128)(2,1)}, u32[]{:S(2)}) copy-start(bf16[2,160,1200]{2,1,0:T(8,128)(2,1)} %param.6) | copy-start | bytes 2304004
  1.1 4.2 %copy-start.2 = (bf16[2,1,2,1280]{3,2,1,0:T(2,128)(2,1)S(1)}, bf16[2,1,2,1280]{3,2,1,0:T(2,128)(2,1)}, u32[]{:S(2)}) copy-start(bf16[2,1,2,1280]{3,2,1,0:T(2,128)(2,1)} %param.5) | copy-start | bytes 30724
  1.2 4.2 %copy-start.3 = (s32[8]{0:T(128)S(1)}, s32[8]{0:T(128)}, u32[]{:S(2)}) copy-start(s32[8]{0:T(128)} %map_ref.3) | copy-start | bytes 100
  1.2 5.4 %collective-permute-start.2 = (bf16[2,2,1280]{2,1,0:T(2,128)(2,1)}, bf16[2,2,1280]{2,1,0:T(2,128)(2,1)S(1)}, u32[]{:S(2)}, u32[]{:S(2)}) collective-permute-start(bf16[2,2,1280]{2,1,0:T(2,128)(2,1)} %bitcast.22), channel_id=1, source_target_pairs={{0,6},{1,7},{2,4},{3,5},{4,2},{5,3},{6,0},{7,1},{8,14},{9,15},{10,... | collective-permute-start | bytes 30728 | tf_op jit(solution)/shard_map/ppermute | solution.py:703
  4.7 3.9 %collective-permute-start.1 = (bf16[2,2,1280]{2,1,0:T(2,128)(2,1)}, bf16[2,2,1280]{2,1,0:T(2,128)(2,1)S(1)}, u32[]{:S(2)}, u32[]{:S(2)}) collective-permute-start(bf16[2,2,1280]{2,1,0:T(2,128)(2,1)} %bitcast.23), channel_id=1, source_target_pairs={{0,4},{1,5},{2,6},{3,7},{4,0},{5,1},{6,2},{7,3},{8,12},{9,13},{10,... | collective-permute-start | bytes 30728 | tf_op jit(solution)/shard_map/ppermute | solution.py:703
  5.2 3.9 %collective-permute-start = (bf16[2,2,1280]{2,1,0:T(2,128)(2,1)}, bf16[2,2,1280]{2,1,0:T(2,128)(2,1)S(1)}, u32[]{:S(2)}, u32[]{:S(2)}) collective-permute-start(bf16[2,2,1280]{2,1,0:T(2,128)(2,1)} %bitcast.24), channel_id=1, source_target_pairs={{0,2},{1,3},{2,0},{3,1},{4,6},{5,7},{6,4},{7,5},{8,10},{9,11},{10,... | collective-permute-start | bytes 30728 | tf_op jit(solution)/shard_map/ppermute | solution.py:703
  6.1 10.3 %copy-start.4 = (f32[1200]{0:T(1024)S(1)}, f32[1200]{0:T(1024)}, u32[]{:S(2)}) copy-start(f32[1200]{0:T(1024)} %param.7) | copy-start | bytes 14404
  6.1 10.3 %copy-start = (s32[1200]{0:T(1024)S(1)}, s32[1200]{0:T(1024)}, u32[]{:S(2)}) copy-start(s32[1200]{0:T(1024)} %len_ref.3) | copy-start | bytes 14404
  10.4 14.0 %all-to-all-start = ((f32[16,8,384]{2,1,0:T(8,128)}), f32[16,8,384]{2,1,0:T(8,128)S(1)}, u32[]{:S(2)}, u32[]{:S(2)}) async-start(f32[16,8,384]{2,1,0:T(8,128)} %bitcast.2), calls=%async_computation | async-start | bytes 393216 | tf_op jit(solution)/shard_map/all_to_all | solution.py:707
  25.3 11.1 %all-to-all-start.1 = ((bf16[16,8,384]{2,1,0:T(8,128)(2,1)}), bf16[16,8,384]{2,1,0:T(8,128)(2,1)S(1)}, u32[]{:S(2)}, u32[]{:S(2)}) async-start(bf16[16,8,384]{2,1,0:T(8,128)(2,1)} %get-tuple-element.24), calls=%async_computation.1 | async-start | bytes 196608 | tf_op jit(solution)/shard_map/all_to_all | solution.py:707
  37.2 3.7 %collective-permute-start.4 = (f32[8,160]{1,0:T(8,128)S(1)}, f32[8,160]{1,0:T(8,128)S(1)}, u32[]{:S(2)}, u32[]{:S(2)}) collective-permute-start(f32[8,160]{1,0:T(8,128)S(1)} %get-tuple-element.31), channel_id=1, source_target_pairs={{0,2},{1,3},{2,0},{3,1},{4,6},{5,7},{6,4},{7,5},{8,10},{9,11},{10,... | collective-permute-start | bytes 15368 | tf_op jit(solution)/shard_map/ppermute | solution.py:703
  38.2 3.7 %collective-permute-start.5 = (f32[8,160]{1,0:T(8,128)S(1)}, f32[8,160]{1,0:T(8,128)S(1)}, u32[]{:S(2)}, u32[]{:S(2)}) collective-permute-start(f32[8,160]{1,0:T(8,128)S(1)} %get-tuple-element.32), channel_id=1, source_target_pairs={{0,4},{1,5},{2,6},{3,7},{4,0},{5,1},{6,2},{7,3},{8,12},{9,13},{10,... | collective-permute-start | bytes 15368 | tf_op jit(solution)/shard_map/ppermute | solution.py:703
  38.5 4.5 %collective-permute-start.6 = (f32[8,160]{1,0:T(8,128)S(1)}, f32[8,160]{1,0:T(8,128)S(1)}, u32[]{:S(2)}, u32[]{:S(2)}) collective-permute-start(f32[8,160]{1,0:T(8,128)S(1)} %get-tuple-element.33), channel_id=1, source_target_pairs={{0,6},{1,7},{2,4},{3,5},{4,2},{5,3},{6,0},{7,1},{8,14},{9,15},{10,... | collective-permute-start | bytes 15368 | tf_op jit(solution)/shard_map/ppermute | solution.py:703

commit v4 on v3

--- a/solution.py
+++ b/solution.py
@@ -125,14 +125,17 @@
 SINE = (6.28318516, -41.34165503, 81.60100407, -76.54978222, 39.53670553)
 
 
-def cos_turns(x, period, inverse):
-    turn = x - period * jnp.floor(x * inverse + 0.5)
-    v = 0.25 - jnp.abs(turn * inverse)
-    y = v * v
-    series = SINE[4]
-    for coefficient in SINE[3::-1]:
-        series = series * y + coefficient
-    return v * series
+def circle(x, period, inverse):
+    turn = (x - period * jnp.floor(x * inverse + 0.5)) * inverse
+    away = jnp.abs(turn)
+    values = []
+    for v in (0.25 - away, 0.25 - jnp.abs(away - 0.25)):
+        y = v * v
+        series = SINE[4]
+        for coefficient in SINE[3::-1]:
+            series = series * y + coefficient
+        values.append(v * series)
+    return values[0], jnp.where(turn < 0.0, -values[1], values[1])
 
 
 def params(memory=VMEM):
@@ -174,40 +177,6 @@
         cost_estimate=cost(4 * 10**9, 10**6),
         name="parity_signs",
     )()
-
-
-def own_rows(wave_map, spec, panel, signs, step):
-    slots, parts, degrees_all = spec.shape
-    rows = 2 * slots * parts
-
-    def kernel(map_ref, x_ref, panel_ref, sign_ref, o_ref, factor_ref, near_ref, sem):
-        copy = pltpu.make_async_copy(panel_ref, near_ref, sem)
-        copy.start()
-        row = lax.broadcasted_iota(jnp.int32, (rows, degrees_all), 0)
-        degree = lax.broadcasted_iota(jnp.int32, (rows, degrees_all), 1)
-        order = jnp.zeros((rows, degrees_all), jnp.int32)
-        for s in range(slots):
-            mine = row // parts % slots == s
-            order = jnp.where(mine, map_ref[at_wave() * slots + s] * step, order)
-        turned = jnp.logical_and(row >= rows // 2, (order & 1) == 1)
-        sign = sign_ref[...]
-        factor = jnp.where(degree >= order, jnp.where(turned, -sign, sign), 0.0)
-        factor_ref[...] = factor
-        x = [x_ref[s].astype(jnp.float32) for s in range(slots)]
-        o_ref[...] = jnp.concatenate(x + x, axis=0) * factor
-        copy.wait()
-
-    flat = jax.ShapeDtypeStruct((rows, degrees_all), jnp.float32)
-    return pl.pallas_call(
-        kernel,
-        out_shape=(flat, flat, jax.ShapeDtypeStruct(panel.shape, panel.dtype)),
-        in_specs=[smem(), vmem(), pl.BlockSpec(memory_space=pl.ANY), vmem()],
-        out_specs=(vmem(),) * 3,
-        scratch_shapes=[pltpu.SemaphoreType.DMA],
-        compiler_params=params(),
-        cost_estimate=cost(10**9, 2 * 10**6),
-        name="own_rows",
-    )(wave_map, spec, panel, signs)
 
 
 def partial_fourier(first, factor, others, panels, slots, waves, wide):
@@ -245,11 +214,12 @@
             mine = total[i * rows : (i + 1) * rows]
             for j in range(waves):
                 value = mine[:, j * here : (j + 1) * here]
-                o_ref[j, chip ^ i] = jnp.concatenate([value, fill], axis=1)
+                value = jnp.concatenate([value, fill], axis=1)
+                o_ref[j, chip ^ i] = value.astype(jnp.bfloat16)
 
     return pl.pallas_call(
         kernel,
-        out_shape=jax.ShapeDtypeStruct((waves, chips, rows, wide), jnp.float32),
+        out_shape=jax.ShapeDtypeStruct((waves, chips, rows, wide), jnp.bfloat16),
         in_specs=[vmem()] * (chips + 3),
         out_specs=vmem(),
         scratch_shapes=[pltpu.VMEM((2, chips * rows, depth), jnp.bfloat16)],
@@ -300,8 +270,9 @@
             imag.append(im * kept[w])
         for w in range(slot_count):
             double = 1.0 if w == 0 else 2.0
-            g_ref[2 * w] = real[w] * double
-            g_ref[2 * w + 1] = imag[w] * double
+            at = 2 * w * SUBLANES
+            g_ref[at : at + SUBLANES, :] = real[w] * double
+            g_ref[at + SUBLANES : at + 2 * SUBLANES, :] = imag[w] * double
         imag[0] = jnp.zeros(shape, jnp.float32)
         square_real, square_imag = [], []
         for n in range(top + 1):
@@ -359,7 +330,7 @@
     return pl.pallas_call(
         kernel,
         out_shape=(
-            jax.ShapeDtypeStruct((2 * slot_count,) + shape, jnp.float32),
+            jax.ShapeDtypeStruct((2 * slot_count * SUBLANES, LANES), jnp.float32),
             jax.ShapeDtypeStruct((sources, rows, wide), jnp.bfloat16),
         ),
         in_specs=[vmem()] * 4,
@@ -385,110 +356,134 @@
     return at // 2, jnp.logical_and(at >= 0, at < span)
 
 
-def prepare(cycle_len, gauss_w, wave_map, factor, span, step, waves, groups, wide, own):
+def prepare(cycle_len, gauss_w, wave_map, spec, panel, signs, span, step, waves, groups, wide):
     slot_count = wave_map.shape[0]
-    slots = slot_count // waves
-    rows, degrees_all = factor.shape
+    slots, parts, degrees_all = spec.shape
+    own = panel.shape[0] // slots
     levels = degrees_all // own
+    rows = 2 * slots * parts
     here = cycle_len.shape[0] // waves
     tiles = wide // LANES
     per = SUBLANES // 2
 
     def kernel(
-        len_ref, map_ref, len_row_ref, weight_row_ref, factor_ref, o_ref, lens_ref, weights_ref, held_ref, near_ref
+        len_ref, map_ref, len_row_ref, weight_row_ref, x_ref, panel_ref, sign_ref,
+        first_ref, factor_ref, factors_ref, near_ref, o_ref, lens_ref, weights_ref, held_ref, sem,
     ):
-        for i in range(slot_count):
-            where = map_ref[i]
-            for w in range(slot_count):
-                held = jnp.where(where == w, 1.0, 0.0)
-                held_ref[w, i : i + 1, :] = jnp.full((1, LANES), held, jnp.float32)
+        copy = pltpu.make_async_copy(panel_ref, near_ref, sem)
+        copy.start()
+        row_of = lax.broadcasted_iota(jnp.int32, (rows, degrees_all), 0)
+        degree = lax.broadcasted_iota(jnp.int32, (rows, degrees_all), 1)
+        bound = jnp.zeros((rows, degrees_all), jnp.int32)
+        for s in range(slots):
+            mine = row_of // parts % slots == s
+            bound = jnp.where(mine, map_ref[at_wave() * slots + s] * step, bound)
+        turned = jnp.logical_and(row_of >= rows // 2, (bound & 1) == 1)
+        sign = sign_ref[...]
+        factor = jnp.where(degree >= bound, jnp.where(turned, -sign, sign), 0.0)
+        factor_ref[...] = factor
+        x = [x_ref[s].astype(jnp.float32) for s in range(slots)]
+        first_ref[...] = jnp.concatenate(x + x, axis=0) * factor
         for level in range(levels):
 
             @pl.when(at_level() == level)
             def _(level=level):
                 for e in range(2):
                     start = (level ^ e) * own
-                    near_ref[e] = factor_ref[:, start : start + own]
+                    factors_ref[e] = factor[:, start : start + own]
+
+        for i in range(slot_count):
+            for w in range(slot_count):
+                held = jnp.where(map_ref[i] == w, 1.0, 0.0)
+                held_ref[w, i : i + 1, :] = jnp.full((1, LANES), held, jnp.float32)
+
+        lens_ref[...] = jnp.full((SUBLANES, LANES), 4.0, jnp.float32)
+        weights_ref[...] = jnp.zeros((SUBLANES, LANES), jnp.float32)
+        for v in range(waves):
+
+            @pl.when(at_wave() == v)
+            def _(v=v):
+                for t in range(tiles):
+                    size = min(LANES, here - t * LANES)
+                    at = v * here + t * LANES
+                    lens = len_row_ref[at : at + size].astype(jnp.float32).reshape(1, size)
+                    weights = weight_row_ref[at : at + size].reshape(1, size)
+                    for h in range(2):
+                        k = h * (SUBLANES // 2) + t
+                        lens_ref[k : k + 1, 0:size] = lens
+                        weights_ref[k : k + 1, 0:size] = weights
 
         wave, part, row, cycle = lane_facts(slot_count)
         tile, _ = tile_of_row(0, span, slot_count)
         first = (tile * LANES).astype(jnp.float32)
         order = (step * wave).astype(jnp.float32)
         stride = order * (LANES * SUBLANES / 2.0)
-        is_imag = part.astype(jnp.float32)
+        imag = part == 1
         way = (1 - 2 * cycle).astype(jnp.float32)
-        point = lax.broadcasted_iota(jnp.int32, (SUBLANES, LANES), 1).astype(jnp.float32)
         down = lax.broadcasted_iota(jnp.int32, (SUBLANES, LANES), 0)
+        turn = step * lax.broadcasted_iota(jnp.int32, (SUBLANES, LANES), 1).astype(jnp.float32)
+        mine = [row == i // 2 if i % 2 == 0 else jnp.logical_and(row == i // 2, cycle == 1) for i in range(SUBLANES)]
+        after = [jnp.logical_and(row == r, cycle == 1) for r in range(per)]
         start = at_wave() * here
 
         def body(g, carry):
             lens = [
                 len_ref[start + jnp.minimum(g * SUBLANES + i, here - 1)] for i in range(SUBLANES)
             ]
-            length = jnp.full((SUBLANES, LANES), lens[0], jnp.int32)
+            length = jnp.full((SUBLANES, LANES), lens[0].astype(jnp.float32), jnp.float32)
             length_down = length
-            offset = jnp.zeros((SUBLANES, LANES), jnp.int32)
-            split = offset
+            offset = jnp.zeros((SUBLANES, LANES), jnp.float32)
+            split, marks = offset, offset
             for i in range(1, SUBLANES):
-                mine = row == i // 2 if i % 2 == 0 else jnp.logical_and(row == i // 2, cycle == 1)
-                length = jnp.where(mine, lens[i], length)
-                length_down = jnp.where(down == i, lens[i], length_down)
+                value = lens[i].astype(jnp.float32)
+                length = jnp.where(mine[i], value, length)
+                length_down = jnp.where(down == i, value, length_down)
             for r in range(per):
-                offset = jnp.where(jnp.logical_and(row == r, cycle == 1), lens[2 * r], offset)
-                split = jnp.where(row == r, lens[2 * r] // LANES, split)
-            length = length.astype(jnp.float32)
+                offset = jnp.where(after[r], lens[2 * r].astype(jnp.float32), offset)
+                split = jnp.where(row == r, (lens[2 * r] // LANES).astype(jnp.float32), split)
+                marks = jnp.where(down == r, (lens[2 * r] % LANES).astype(jnp.float32), marks)
+                marks = jnp.where(down == per + r, (lens[2 * r] + lens[2 * r + 1]).astype(jnp.float32), marks)
             inverse = 1.0 / length
-            quarter = 0.25 * length
-            x = order * (first - offset.astype(jnp.float32))
-            o_ref[g, 0] = cos_turns(x - is_imag * quarter, length, inverse)
-            o_ref[g, 1] = cos_turns(x + (1.0 - is_imag) * quarter, length, inverse)
-            turns = cos_turns(jnp.where(down == 1, stride - quarter, stride), length, inverse)
-            o_ref[g, 2] = jnp.where(down < 2, turns, way * split.astype(jnp.float32))
-            length = length_down.astype(jnp.float32)
-            inverse = 1.0 / length
-            quarter = 0.25 * length
-            for i in range(2):
-                turn = (i + 1.0) * step * point
-                o_ref[g, 3 + 2 * i] = cos_turns(turn, length, inverse)
-                o_ref[g, 4 + 2 * i] = cos_turns(turn + quarter, length, inverse)
+            cos, sin = circle(order * (first - offset), length, inverse)
+            o_ref[g, 0] = jnp.where(imag, sin, cos)
+            o_ref[g, 1] = jnp.where(imag, cos, -sin)
+            cos, sin = circle(stride, length, inverse)
+            turns = jnp.where(down == 0, cos, sin)
+            o_ref[g, 2] = jnp.where(down < 2, turns, way * split)
+            cos, sin = circle(turn, length_down, 1.0 / length_down)
+            o_ref[g, 3] = cos
+            o_ref[g, 4] = -sin
+            o_ref[g, 5] = 1.0 - 2.0 * sin * sin
+            o_ref[g, 6] = -2.0 * sin * cos
+            o_ref[g, 7] = marks
             return carry
 
         lax.fori_loop(0, groups, body, 0, unroll=4)
-        lens_ref[...] = jnp.full((SUBLANES, LANES), 4.0, jnp.float32)
-        weights_ref[...] = jnp.zeros((SUBLANES, LANES), jnp.float32)
-        for v in range(waves):
-
-            @pl.when(at_wave() == v)
-            def _(v=v):
-                for t in range(tiles):
-                    size = min(LANES, here - t * LANES)
-                    at = v * here + t * LANES
-                    lens = len_row_ref[:, at : at + size].astype(jnp.float32)
-                    weights = weight_row_ref[:, at : at + size]
-                    for h in range(2):
-                        k = h * (SUBLANES // 2) + t
-                        lens_ref[k : k + 1, 0:size] = lens
-                        weights_ref[k : k + 1, 0:size] = weights
+        copy.wait()
 
     flat = jax.ShapeDtypeStruct((SUBLANES, LANES), jnp.float32)
     return pl.pallas_call(
         kernel,
         out_shape=(
-            jax.ShapeDtypeStruct((groups, 7, SUBLANES, LANES), jnp.float32),
+            jax.ShapeDtypeStruct((rows, degrees_all), jnp.float32),
+            jax.ShapeDtypeStruct((rows, degrees_all), jnp.float32),
+            jax.ShapeDtypeStruct((2, rows, own), jnp.float32),
+            jax.ShapeDtypeStruct(panel.shape, panel.dtype),
+            jax.ShapeDtypeStruct((groups, 8, SUBLANES, LANES), jnp.float32),
             flat,
             flat,
             jax.ShapeDtypeStruct((slot_count, slot_count, LANES), jnp.float32),
-            jax.ShapeDtypeStruct((2, rows, own), jnp.float32),
         ),
-        in_specs=[smem()] * 2 + [vmem()] * 3,
-        out_specs=(vmem(),) * 5,
+        in_specs=[smem()] * 2 + [vmem()] * 3 + [pl.BlockSpec(memory_space=pl.ANY), vmem()],
+        out_specs=(vmem(),) * 8,
+        scratch_shapes=[pltpu.SemaphoreType.DMA],
         compiler_params=params(),
         cost_estimate=cost(3 * 10**9, 10**6),
         name="prepare",
-    )(cycle_len, wave_map, cycle_len.reshape(1, -1), gauss_w.reshape(1, -1), factor)
-
-
-def grid_values(cycle_len, fourier, tables, span, slot_count, rows_out, tiles):
+    )(cycle_len, wave_map, cycle_len, gauss_w, spec, panel, signs)
+
+
+def grid_values(fourier, tables, span, slot_count, rows_out, tiles):
     groups = tables.shape[0]
     per = SUBLANES // 2
     block = groups // STEPS
@@ -497,39 +492,35 @@
     kinds = 4 * slot_count
     around = LANES // SUBLANES
 
-    def kernel(len_ref, fourier_ref, table_ref, o_ref, rows_ref, wave_ref):
+    def kernel(fourier_ref, table_ref, o_hbm, rows_ref, wave_ref, part_ref, sems):
         wave, _, row, cycle = lane_facts(slot_count)
         way = (1 - 2 * cycle).astype(jnp.float32)
-        point = lax.broadcasted_iota(jnp.int32, (SUBLANES, LANES), 1)
+        point = lax.broadcasted_iota(jnp.int32, (SUBLANES, LANES), 1).astype(jnp.float32)
         down = lax.broadcasted_iota(jnp.int32, (SUBLANES, LANES), 0)
         second = down % 2 == 1
         unit = jnp.where(down < 2, 1.0, 0.0)
         beside = jnp.where(down < 6, -1.0, 1.0)
-        base = pl.program_id(0) * block
-        start = at_wave() * 2 * rows_out
-
-        @pl.when(pl.program_id(0) == 0)
-        def _():
-            for c in range(2):
-                for h in range(2):
-                    for w in range(slot_count):
-                        for t in range(tiles):
-                            at = (c * 2 + h) * slot_count + w
-                            k = h * (SUBLANES // 2) + t
-                            rows_ref[t, at : at + 1, :] = fourier_ref[2 * w + c, k : k + 1, :]
-
+        for c in range(2):
+            for h in range(2):
+                for t in range(tiles):
+                    at = (c * 2 + h) * slot_count
+                    k = c * SUBLANES + h * (SUBLANES // 2) + t
+                    rows_ref[t, at : at + slot_count, :] = fourier_ref[
+                        pl.ds(k, slot_count, stride=2 * SUBLANES), :
+                    ]
         pick = lax.broadcasted_iota(jnp.int32, (LANES, LANES), 0)
         lane = lax.broadcasted_iota(jnp.int32, (LANES, LANES), 1)
         pick = jnp.where(pick == lane // size * 2 + lane % 2, 1.0, 0.0).astype(jnp.bfloat16)
+
         turned = []
-        for g in range(block):
-            at = base + g
-            shift = (around - at % around) % around * SUBLANES
-            turned.append(pltpu.roll(rows_ref[at // around], shift, 1))
+        for g in range(groups):
+            shift = -g % around * SUBLANES
+            value = rows_ref[g // around]
+            turned.append(pltpu.roll(value, shift, 1) if shift else value)
         spread = jnp.dot(
             jnp.concatenate(turned, axis=0).astype(jnp.bfloat16), pick, preferred_element_type=jnp.float32
         )
-        for g in range(block):
+        for g in range(groups):
             sums = []
             for k in range(4):
                 at = g * kinds + k * slot_count
@@ -538,7 +529,7 @@
             for c in range(2):
                 wave_ref[g, c] = jnp.where(down % 2 == 0, sums[2 * c], sums[2 * c + 1])
 
-        def body(g, carry):
+        def one_group(base, i, g):
             real, imag = wave_ref[g, 0], wave_ref[g, 1]
             x = real * table_ref[g, 0] + imag * table_ref[g, 1]
             y = real * table_ref[g, 1] - imag * table_ref[g, 0]
@@ -558,9 +549,7 @@
 
             columns, ends = [], []
             for r in range(per):
-                at = 2 * jnp.minimum((base + g) * per + r, rows_out - 1) + start
-                first_end, end = len_ref[at], len_ref[at] + len_ref[at + 1]
-                ends.append(end)
+                ends.append(table_ref[g, 7, per + r : per + r + 1])
                 cos1, sin1, cos2, sin2 = [
                     jnp.where(
                         second,
@@ -573,7 +562,7 @@
                 series = [jnp.where(down < 4, unit, jnp.where(down < 6, cos1, sin1))]
                 third = series[0] * (twice + beside)
                 series.append(jnp.where(down < 2, cos2, jnp.where(down < 4, sin2, third)))
-                here = jnp.logical_xor(point < first_end % LANES, second)
+                here = jnp.logical_xor(point < table_ref[g, 7, r : r + 1], second)
                 for _ in range(2, size // SUBLANES):
                     series.append(twice * series[-1] - series[-2])
                 full = jnp.concatenate(series, axis=0).astype(jnp.bfloat16)
@@ -591,36 +580,58 @@
                         continue
                     value = product[k * SUBLANES : (k + 1) * SUBLANES, r * LANES : (r + 1) * LANES]
                     if k == blocks - 1:
-                        position = (down + k * SUBLANES - shift) // 2 * LANES + point
+                        position = ((down + k * SUBLANES - shift) // 2 * LANES).astype(jnp.float32) + point
                         value = jnp.where(position < ends[r], value, 0.0)
                     places.setdefault((r * span - shift) // SUBLANES + k, []).append(value)
             whole = [functools.reduce(lambda a, b: a + b, places[k]) for k in sorted(places)]
             size_out = per * span
-            o_ref[pl.ds(pl.multiple_of(g * size_out, 16), size_out), :] = jnp.concatenate(
+            part_ref[base, i * size_out : (i + 1) * size_out, :] = jnp.concatenate(
                 whole, axis=0
             ).astype(jnp.bfloat16)
+
+        tall = block * per * span // 2
+
+        def copy(i, half):
+            start = (2 * i + half) * tall
+            size = min(tall, rows_out * span - start)
+            return pltpu.make_async_copy(
+                part_ref.at[i, pl.ds(half * tall, size), :],
+                o_hbm.at[pl.ds(start, size), :],
+                sems.at[2 * i + half],
+            )
+
+        def step(base, carry):
+            for half in range(2):
+                for i in range(half * block // 2, (half + 1) * block // 2):
+                    one_group(base, i, base * block + i)
+                for i in range(STEPS):
+
+                    @pl.when(base == i)
+                    def _(i=i, half=half):
+                        copy(i, half).start()
+
             return carry
 
-        lax.fori_loop(0, block, body, 0, unroll=8)
+        lax.fori_loop(0, STEPS, step, 0)
+        for i in range(STEPS):
+            for half in range(2):
+                copy(i, half).wait()
 
     return pl.pallas_call(
         kernel,
-        grid=(STEPS,),
         out_shape=jax.ShapeDtypeStruct((rows_out * span, LANES), jnp.bfloat16),
-        in_specs=[
-            smem(),
-            pl.BlockSpec(fourier.shape, lambda i: (0, 0, 0)),
-            pl.BlockSpec((block,) + tables.shape[1:], lambda i: (i, 0, 0, 0)),
-        ],
-        out_specs=pl.BlockSpec((block * per * span, LANES), lambda i: (i, 0)),
+        in_specs=[vmem()] * 2,
+        out_specs=pl.BlockSpec(memory_space=pl.ANY),
         scratch_shapes=[
             pltpu.VMEM((tiles, kinds, LANES), jnp.float32),
-            pltpu.VMEM((block, 2, SUBLANES, LANES), jnp.float32),
+            pltpu.VMEM((groups, 2, SUBLANES, LANES), jnp.float32),
+            pltpu.VMEM((STEPS, block * per * span, LANES), jnp.bfloat16),
+            pltpu.SemaphoreType.DMA((2 * STEPS,)),
         ],
         compiler_params=params(16 * 1024 * 1024),
         cost_estimate=cost(8 * 10**9, 3 * 10**6),
         name="grid_values",
-    )(cycle_len, fourier, tables)
+    )(fourier, tables)
 
 
 def direct(returned, factors, panels):
@@ -710,9 +721,6 @@
     others = [across(mine, 2 * i) for i in range(1, chips)]
     panel = legendre.reshape(slots * own, lats)
     signs = parity_signs(2 * slots * 2, degrees_all)
-    first, factor, near = own_rows(wave_map, mine, panel, signs, step)
-    panels = (near, across(panel, 1))
-
     here = lats // waves
     wide = -(-here // LANES) * LANES
     tiles = wide // LANES
@@ -721,17 +729,17 @@
     groups = -(-rows_out // (per * STEPS)) * STEPS
     span = 2 * (LPAD // LANES)
     rows_here = 2 * slots * 2
+    first, factor, factors, near, tables, lens, weights, held = prepare(
+        cycle_len, gauss_w, wave_map, mine, panel, signs, span, step, waves, groups, wide
+    )
+    panels = (near, across(panel, 1))
 
     part = partial_fourier(first, factor, others, panels, slots, waves, wide)
     part = same_core(part.reshape(waves * chips, rows_here, wide))
-    tables, lens, weights, held, factors = prepare(
-        cycle_len, gauss_w, wave_map, factor, span, step, waves, groups, wide, own
-    )
     fourier, returned = quadratic(held, part, lens, weights, waves, step)
     returned = same_core(returned)
 
-    values = grid_values(cycle_len, fourier, tables, span, slot_count, rows_out, tiles)
-    returned, values = lax.optimization_barrier((returned, values))
+    values = grid_values(fourier, tables, span, slot_count, rows_out, tiles)
     values = values.reshape(rows_out, span // 2, 2, LANES)
     values = with_layout_constraint(values, Layout(major_to_minor=(0, 1, 2, 3)))
     values = values.transpose(0, 2, 1, 3)

time: 44.1 us -> 42.6 us (0.966)
  blocking collectives: 0 us -> 24 us
  waiting for transfers between devices: 13.8 us -> 1.09 us
  starting transfers between devices: 17.7 us -> 8.26 us
  Pallas kernels: 11.5 us -> 8.25 us
    all_to_all x0 -> x2, blocking collectives: none -> 24 us  [same_core(): lax.all_to_all(x, ('wave', 'lev'), 0, 0, tiled=True, axis_index_groups=gr...]
    all_to_all x2 -> x0, starting transfers between devices: 9.44 us -> none  [same_core(): lax.all_to_all(x, ('wave', 'lev'), 0, 0, tiled=True, axis_index_groups=gr...]
    all_to_all x2 -> x0, waiting for transfers between devices: 8.47 us -> none  [same_core(): lax.all_to_all(x, ('wave', 'lev'), 0, 0, tiled=True, axis_index_groups=gr...]
    ppermute x7, waiting for transfers between devices: 5.3 us -> 1.09 us  [across(): return lax.ppermute(x, 'lev', [(j, j ^ bits) for j in range(levels)])]
    pallas_call x4 -> x3, Pallas kernels: 8.75 us -> 6.16 us  [the longest x1 3.32 us: grid_values(): pl.pallas_call(kernel, out_shape=jax.ShapeDtypeStruct((rows_out * span, L...]
    pallas_call x1, Pallas kernels: 1.3 us -> 0.61 us  [partial_fourier(): pl.pallas_call(kernel, out_shape=jax.ShapeDtypeStruct((waves, chips, rows...]
  transfers between devices with their start and end apart: 9 -> 7, of which waited for: 8 -> 2; matrix products, arithmetic and copies ran while one was open for 0% -> 0% of each run, Pallas kernels for 18% -> 14%
where the time goes in v4:
time: 42.6 us; the launch traced here: 42.4 us
  blocking collectives  24 us (56%)
  starting transfers between devices  8.26 us (19%)
  Pallas kernels  8.25 us (19%)
  waiting for transfers between devices  1.09 us (3%)
  between operations  0.75 us (2%)
    all_to_all x2, blocking collectives, same_core(): lax.all_to_all(x, ('wave', 'lev'), 0, 0, tiled=True, axis_index_groups=gr...  24 us
    ppermute x7, starting transfers between devices, across(): return lax.ppermute(x, 'lev', [(j, j ^ bits) for j in range(levels)])  8.26 us
    pallas_call x1, Pallas kernels, grid_values(): pl.pallas_call(kernel, out_shape=jax.ShapeDtypeStruct((rows_out * span, L...  3.32 us
    pallas_call x1, Pallas kernels, prepare(): pl.pallas_call(kernel, out_shape=(jax.ShapeDtypeStruct((rows, degrees_all...  2.59 us
    ppermute x7, waiting for transfers between devices, across(): return lax.ppermute(x, 'lev', [(j, j ^ bits) for j in range(levels)])  1.09 us
  transfers between devices with their start and end apart: 7, of which 2 were waited for; matrix products, arithmetic and copies ran while one was open for 0% of the time, Pallas kernels for 14%

profile of v4, /device:TPU:0, one launch (start us, length us, event | category | flops | bytes accessed | tf_op | source)
XLA Modules:
  0.0 42.4 jit_solution(13809922303651098374)
XLA Ops:
  0.6 0.5 %collective-permute-start.3 = (bf16[320,1200]{1,0:T(8,128)(2,1)}, bf16[320,1200]{1,0:T(8,128)(2,1)S(1)}, u32[]{:S(2)}, u32[]{:S(2)}) collective-permute-start(bf16[320,1200]{1,0:T(8,128)(2,1)} %bitcast.20), channel_id=1, source_target_pairs={{0,1},{1,0},{2,3},{3,2},{4,5},{5,4},{6,7},{7,6},{8,9},{9,8},{10,11... | collective-permute-start | bytes 2304008 | tf_op jit(solution)/shard_map/ppermute | solution.py:714
  1.1 0.0 copy-start
  1.2 0.0 copy-start.1
  1.2 0.0 copy-start.2
  1.2 0.0 copy-start.3
  1.2 0.0 copy-start.4
  1.2 3.5 %collective-permute-start.2 = (bf16[2,2,1280]{2,1,0:T(2,128)(2,1)}, bf16[2,2,1280]{2,1,0:T(2,128)(2,1)S(1)}, u32[]{:S(2)}, u32[]{:S(2)}) collective-permute-start(bf16[2,2,1280]{2,1,0:T(2,128)(2,1)} %bitcast.23), channel_id=1, source_target_pairs={{0,6},{1,7},{2,4},{3,5},{4,2},{5,3},{6,0},{7,1},{8,14},{9,15},{10,... | collective-permute-start | bytes 30728 | tf_op jit(solution)/shard_map/ppermute | solution.py:714
  4.7 0.5 %collective-permute-start.1 = (bf16[2,2,1280]{2,1,0:T(2,128)(2,1)}, bf16[2,2,1280]{2,1,0:T(2,128)(2,1)S(1)}, u32[]{:S(2)}, u32[]{:S(2)}) collective-permute-start(bf16[2,2,1280]{2,1,0:T(2,128)(2,1)} %bitcast.24), channel_id=1, source_target_pairs={{0,4},{1,5},{2,6},{3,7},{4,0},{5,1},{6,2},{7,3},{8,12},{9,13},{10,... | collective-permute-start | bytes 30728 | tf_op jit(solution)/shard_map/ppermute | solution.py:714
  5.2 0.1 collective-permute-start
  5.4 0.0 copy-done
  5.4 0.0 copy-done.1
  5.4 0.0 copy-done.2
  5.4 0.0 copy-done.3
  5.4 0.0 copy-done.4
  5.4 2.6 %prepare.1 = (f32[8,1280]{1,0:T(8,128)S(1)}, f32[8,1280]{1,0:T(8,128)S(1)}, f32[2,8,160]{2,1,0:T(8,128)S(1)}, bf16[320,1200]{1,0:T(8,128)(2,1)S(1)}, f32[40,8,8,...) custom-call(s32[1200]{0:T(1024)S(1)} %copy-done.2, ...), custom_call_target="tpu_custom_call" | custom-call | flops 3000000000 | bytes 1000000 | tf_op jit(solution)/shard_map/prepare/pallas_call | solution.py:465
  8.0 0.0 collective-permute-done.2.refs_2_
  8.0 0.6 %collective-permute-done.1.refs_1_ = bf16[2,2,1280]{2,1,0:T(2,128)(2,1)S(1)} collective-permute-done((bf16[2,2,1280]{2,1,0:T(2,128)(2,1)}, bf16[2,2,1280]{2,1,0:T(2,128)(2,1)S(1)}, u32[]{:S(2)}, u32[]{:S(2)}) %collective-permute-start.1) | collective-permute-done | bytes 10272 | tf_op jit(solution)/shard_map/ppermute | solution.py:714
  8.6 0.5 %collective-permute-done.refs_0_ = bf16[2,2,1280]{2,1,0:T(2,128)(2,1)S(1)} collective-permute-done((bf16[2,2,1280]{2,1,0:T(2,128)(2,1)}, bf16[2,2,1280]{2,1,0:T(2,128)(2,1)S(1)}, u32[]{:S(2)}, u32[]{:S(2)}) %collective-permute-start) | collective-permute-done | bytes 10272 | tf_op jit(solution)/shard_map/ppermute | solution.py:714
  9.1 0.0 collective-permute-done.3.refs_4_.other_ref
  9.1 0.6 %partial_fourier.1 = bf16[4,4,8,384]{3,2,1,0:T(8,128)(2,1)S(1)} custom-call(f32[8,1280]{1,0:T(8,128)S(1)} %get-tuple-element.17.first_ref, f32[8,1280]{1,0:T(8,128)S(1)} %get-tuple-element.18.factor_ref, bf16[2,2,1280]{2,1,0:T(2,128)(2,1)S(1)} %collective-permute-done.refs_0_, bf16[2,2,1280]{2,1,0:T(2,128)(2,1)S(1)} %collective-permute-done.1.refs_1_, ...), custom_call_target="tpu_custom_call" | custom-call | flops 1000000000 | bytes 2000000 | tf_op jit(solution)/shard_map/partial_fourier/pallas_call | solution.py:220
  9.7 13.8 %all_to_all.10.x_ref = bf16[16,8,384]{2,1,0:T(8,128)(2,1)S(1)} all-to-all(bf16[16,8,384]{2,1,0:T(8,128)(2,1)S(1)} %bitcast.19), channel_id=1, replica_groups={{0,2,4,6,8,10,12,14,16,18,20,22,24,26,28,30},{1,3,5,7,9,11,13,15,17,19,..., dimensions={0} | all-to-all | bytes 196608 | tf_op jit(solution)/shard_map/all_to_all | solution.py:718
  23.5 0.2 quadratic.1
  23.8 10.3 %all_to_all.11 = bf16[16,8,384]{2,1,0:T(8,128)(2,1)S(1)} all-to-all(bf16[16,8,384]{2,1,0:T(8,128)(2,1)S(1)} %get-tuple-element.24), channel_id=1, replica_groups={{0,2,4,6,8,10,12,14,16,18,20,22,24,26,28,30},{1,3,5,7,9,11,13,15,17,19,..., dimensions={0} | all-to-all | bytes 196608 | tf_op jit(solution)/shard_map/all_to_all | solution.py:718
  34.0 0.8 %direct.1 = (f32[8,160]{1,0:T(8,128)S(1)}, f32[8,160]{1,0:T(8,128)S(1)}, f32[8,160]{1,0:T(8,128)S(1)}, f32[8,160]{1,0:T(8,128)S(1)}) custom-call(bf16[4,32,384]{2,1,0:T(8,128)(2,1)S(1)} %bitcast.18, f32[2,8,160]{2,1,0:T(8,128)S(1)} %get-tuple-element.25.factor_ref, bf16[320,1200]{1,0:T(8,128)(2,1)S(1)} %bitcast.22, ...), custom_call_target="tpu_custom_call" | custom-call | flops 1000000000 | bytes 2000000 | tf_op jit(solution)/shard_map/direct/pallas_call | solution.py:663
  34.8 1.0 %collective-permute-start.4 = (f32[8,160]{1,0:T(8,128)S(1)}, f32[8,160]{1,0:T(8,128)S(1)}, u32[]{:S(2)}, u32[]{:S(2)}) collective-permute-start(f32[8,160]{1,0:T(8,128)S(1)} %get-tuple-element.27), channel_id=1, source_target_pairs={{0,2},{1,3},{2,0},{3,1},{4,6},{5,7},{6,4},{7,5},{8,10},{9,11},{10,... | collective-permute-start | bytes 15368 | tf_op jit(solution)/shard_map/ppermute | solution.py:714
  35.8 0.3 collective-permute-start.5
  36.1 2.2 %collective-permute-start.6 = (f32[8,160]{1,0:T(8,128)S(1)}, f32[8,160]{1,0:T(8,128)S(1)}, u32[]{:S(2)}, u32[]{:S(2)}) collective-permute-start(f32[8,160]{1,0:T(8,128)S(1)} %get-tuple-element.29), channel_id=1, source_target_pairs={{0,6},{1,7},{2,4},{3,5},{4,2},{5,3},{6,0},{7,1},{8,14},{9,15},{10,... | collective-permute-start | bytes 15368 | tf_op jit(solution)/shard_map/ppermute | solution.py:714
  38.3 3.3 %grid_values.1 = bf16[11400,128]{1,0:T(8,128)(2,1)} custom-call(f32[128,128]{1,0:T(8,128)S(1)} %get-tuple-element.22.fourier_ref, f32[40,8,8,128]{3,2,1,0:T(8,128)S(1)} %get-tuple-element.23.table_ref), custom_call_target="tpu_custom_call" | custom-call | flops 8000000000 | bytes 3000000 | tf_op jit(solution)/shard_map/grid_values/pallas_call | solution.py:620
  41.7 0.0 collective-permute-done.4.refs_1_
  41.7 0.0 collective-permute-done.5.refs_2_
  41.7 0.0 collective-permute-done.6.refs_3_
  41.7 0.7 %join_degrees.1 = f32[2,2,1280]{2,1,0:T(2,128)} custom-call(f32[8,160]{1,0:T(8,128)S(1)} %get-tuple-element.26.refs_0_, f32[8,160]{1,0:T(8,128)S(1)} %collective-permute-done.4.refs_1_, f32[8,160]{1,0:T(8,128)S(1)} %collective-permute-done.5.refs_2_, f32[8,160]{1,0:T(8,128)S(1)} %collective-permute-done.6.refs_3_), custom_call_target="tpu_custom_call" | custom-call | tf_op jit(solution)/shard_map/join_degrees/pallas_call | solution.py:692
  (1 shorter events, 0.0 us)
Async XLA Ops:
  0.6 8.5 %collective-permute-start.3 = (bf16[320,1200]{1,0:T(8,128)(2,1)}, bf16[320,1200]{1,0:T(8,128)(2,1)S(1)}, u32[]{:S(2)}, u32[]{:S(2)}) collective-permute-start(bf16[320,1200]{1,0:T(8,128)(2,1)} %bitcast.20), channel_id=1, source_target_pairs={{0,1},{1,0},{2,3},{3,2},{4,5},{5,4},{6,7},{7,6},{8,9},{9,8},{10,11... | collective-permute-start | bytes 2304008 | tf_op jit(solution)/shard_map/ppermute | solution.py:714
  1.1 4.2 %copy-start = (bf16[2,160,1200]{2,1,0:T(8,128)(2,1)S(1)}, bf16[2,160,1200]{2,1,0:T(8,128)(2,1)}, u32[]{:S(2)}) copy-start(bf16[2,160,1200]{2,1,0:T(8,128)(2,1)} %param.6) | copy-start | bytes 2304004
  1.2 4.2 %copy-start.1 = (bf16[2,1,2,1280]{3,2,1,0:T(2,128)(2,1)S(1)}, bf16[2,1,2,1280]{3,2,1,0:T(2,128)(2,1)}, u32[]{:S(2)}) copy-start(bf16[2,1,2,1280]{3,2,1,0:T(2,128)(2,1)} %param.5) | copy-start | bytes 30724
  1.2 4.2 %copy-start.2 = (s32[1200]{0:T(1024)S(1)}, s32[1200]{0:T(1024)}, u32[]{:S(2)}) copy-start(s32[1200]{0:T(1024)} %len_row_ref.1) | copy-start | bytes 14404
  1.2 4.3 %copy-start.3 = (f32[1200]{0:T(1024)S(1)}, f32[1200]{0:T(1024)}, u32[]{:S(2)}) copy-start(f32[1200]{0:T(1024)} %weight_row_ref.1) | copy-start | bytes 14404
  1.2 4.3 %copy-start.4 = (s32[8]{0:T(128)S(1)}, s32[8]{0:T(128)}, u32[]{:S(2)}) copy-start(s32[8]{0:T(128)} %map_ref.1) | copy-start | bytes 100
  1.2 6.9 %collective-permute-start.2 = (bf16[2,2,1280]{2,1,0:T(2,128)(2,1)}, bf16[2,2,1280]{2,1,0:T(2,128)(2,1)S(1)}, u32[]{:S(2)}, u32[]{:S(2)}) collective-permute-start(bf16[2,2,1280]{2,1,0:T(2,128)(2,1)} %bitcast.23), channel_id=1, source_target_pairs={{0,6},{1,7},{2,4},{3,5},{4,2},{5,3},{6,0},{7,1},{8,14},{9,15},{10,... | collective-permute-start | bytes 30728 | tf_op jit(solution)/shard_map/ppermute | solution.py:714
  4.7 3.9 %collective-permute-start.1 = (bf16[2,2,1280]{2,1,0:T(2,128)(2,1)}, bf16[2,2,1280]{2,1,0:T(2,128)(2,1)S(1)}, u32[]{:S(2)}, u32[]{:S(2)}) collective-permute-start(bf16[2,2,1280]{2,1,0:T(2,128)(2,1)} %bitcast.24), channel_id=1, source_target_pairs={{0,4},{1,5},{2,6},{3,7},{4,0},{5,1},{6,2},{7,3},{8,12},{9,13},{10,... | collective-permute-start | bytes 30728 | tf_op jit(solution)/shard_map/ppermute | solution.py:714
  5.2 3.9 %collective-permute-start = (bf16[2,2,1280]{2,1,0:T(2,128)(2,1)}, bf16[2,2,1280]{2,1,0:T(2,128)(2,1)S(1)}, u32[]{:S(2)}, u32[]{:S(2)}) collective-permute-start(bf16[2,2,1280]{2,1,0:T(2,128)(2,1)} %bitcast.25), channel_id=1, source_target_pairs={{0,2},{1,3},{2,0},{3,1},{4,6},{5,7},{6,4},{7,5},{8,10},{9,11},{10,... | collective-permute-start | bytes 30728 | tf_op jit(solution)/shard_map/ppermute | solution.py:714
  34.8 6.9 %collective-permute-start.4 = (f32[8,160]{1,0:T(8,128)S(1)}, f32[8,160]{1,0:T(8,128)S(1)}, u32[]{:S(2)}, u32[]{:S(2)}) collective-permute-start(f32[8,160]{1,0:T(8,128)S(1)} %get-tuple-element.27), channel_id=1, source_target_pairs={{0,2},{1,3},{2,0},{3,1},{4,6},{5,7},{6,4},{7,5},{8,10},{9,11},{10,... | collective-permute-start | bytes 15368 | tf_op jit(solution)/shard_map/ppermute | solution.py:714
  35.8 5.9 %collective-permute-start.5 = (f32[8,160]{1,0:T(8,128)S(1)}, f32[8,160]{1,0:T(8,128)S(1)}, u32[]{:S(2)}, u32[]{:S(2)}) collective-permute-start(f32[8,160]{1,0:T(8,128)S(1)} %get-tuple-element.28), channel_id=1, source_target_pairs={{0,4},{1,5},{2,6},{3,7},{4,0},{5,1},{6,2},{7,3},{8,12},{9,13},{10,... | collective-permute-start | bytes 15368 | tf_op jit(solution)/shard_map/ppermute | solution.py:714
  36.1 5.6 %collective-permute-start.6 = (f32[8,160]{1,0:T(8,128)S(1)}, f32[8,160]{1,0:T(8,128)S(1)}, u32[]{:S(2)}, u32[]{:S(2)}) collective-permute-start(f32[8,160]{1,0:T(8,128)S(1)} %get-tuple-element.29), channel_id=1, source_target_pairs={{0,6},{1,7},{2,4},{3,5},{4,2},{5,3},{6,0},{7,1},{8,14},{9,15},{10,... | collective-permute-start | bytes 15368 | tf_op jit(solution)/shard_map/ppermute | solution.py:714

commit v5 on v4

--- a/solution.py
+++ b/solution.py
@@ -120,7 +120,8 @@
 
 LANES = 128
 SUBLANES = 8
-STEPS = 5
+STEPS = 2
+PIECES = 4
 VMEM = 8 * 1024 * 1024
 SINE = (6.28318516, -41.34165503, 81.60100407, -76.54978222, 39.53670553)
 
@@ -423,26 +424,26 @@
         down = lax.broadcasted_iota(jnp.int32, (SUBLANES, LANES), 0)
         turn = step * lax.broadcasted_iota(jnp.int32, (SUBLANES, LANES), 1).astype(jnp.float32)
         mine = [row == i // 2 if i % 2 == 0 else jnp.logical_and(row == i // 2, cycle == 1) for i in range(SUBLANES)]
-        after = [jnp.logical_and(row == r, cycle == 1) for r in range(per)]
+        second = down % 2 == 1
         start = at_wave() * here
 
         def body(g, carry):
             lens = [
                 len_ref[start + jnp.minimum(g * SUBLANES + i, here - 1)] for i in range(SUBLANES)
             ]
-            length = jnp.full((SUBLANES, LANES), lens[0].astype(jnp.float32), jnp.float32)
-            length_down = length
-            offset = jnp.zeros((SUBLANES, LANES), jnp.float32)
-            split, marks = offset, offset
+            length = jnp.full((SUBLANES, LANES), lens[0], jnp.int32)
+            length_down, before, before_down = length, length, length
             for i in range(1, SUBLANES):
-                value = lens[i].astype(jnp.float32)
-                length = jnp.where(mine[i], value, length)
-                length_down = jnp.where(down == i, value, length_down)
-            for r in range(per):
-                offset = jnp.where(after[r], lens[2 * r].astype(jnp.float32), offset)
-                split = jnp.where(row == r, (lens[2 * r] // LANES).astype(jnp.float32), split)
-                marks = jnp.where(down == r, (lens[2 * r] % LANES).astype(jnp.float32), marks)
-                marks = jnp.where(down == per + r, (lens[2 * r] + lens[2 * r + 1]).astype(jnp.float32), marks)
+                length = jnp.where(mine[i], lens[i], length)
+                length_down = jnp.where(down == i, lens[i], length_down)
+            for r in range(1, per):
+                before = jnp.where(row == r, lens[2 * r], before)
+                before_down = jnp.where(down // 2 == r, lens[2 * r], before_down)
+            length = length.astype(jnp.float32)
+            offset = jnp.where(cycle == 1, before, 0).astype(jnp.float32)
+            split = (before >> (LANES.bit_length() - 1)).astype(jnp.float32)
+            marks = jnp.where(second, before_down + length_down, before_down & (LANES - 1))
+            length_down = length_down.astype(jnp.float32)
             inverse = 1.0 / length
             cos, sin = circle(order * (first - offset), length, inverse)
             o_ref[g, 0] = jnp.where(imag, sin, cos)
@@ -455,10 +456,10 @@
             o_ref[g, 4] = -sin
             o_ref[g, 5] = 1.0 - 2.0 * sin * sin
             o_ref[g, 6] = -2.0 * sin * cos
-            o_ref[g, 7] = marks
+            o_ref[g, 7] = marks.astype(jnp.float32)
             return carry
 
-        lax.fori_loop(0, groups, body, 0, unroll=4)
+        lax.fori_loop(0, groups, body, 0, unroll=19)
         copy.wait()
 
     flat = jax.ShapeDtypeStruct((SUBLANES, LANES), jnp.float32)
@@ -492,7 +493,11 @@
     kinds = 4 * slot_count
     around = LANES // SUBLANES
 
-    def kernel(fourier_ref, table_ref, o_hbm, rows_ref, wave_ref, part_ref, sems):
+    total = rows_out * span
+    tail = total % (2 * SUBLANES)
+    tail_group, tail_at = divmod(total - tail, per * span)
+
+    def kernel(fourier_ref, table_ref, o_hbm, rows_ref, wave_ref, part_ref, tail_ref, sems):
         wave, _, row, cycle = lane_facts(slot_count)
         way = (1 - 2 * cycle).astype(jnp.float32)
         point = lax.broadcasted_iota(jnp.int32, (SUBLANES, LANES), 1).astype(jnp.float32)
@@ -549,7 +554,7 @@
 
             columns, ends = [], []
             for r in range(per):
-                ends.append(table_ref[g, 7, per + r : per + r + 1])
+                ends.append(table_ref[g, 7, 2 * r + 1 : 2 * r + 2])
                 cos1, sin1, cos2, sin2 = [
                     jnp.where(
                         second,
@@ -562,7 +567,7 @@
                 series = [jnp.where(down < 4, unit, jnp.where(down < 6, cos1, sin1))]
                 third = series[0] * (twice + beside)
                 series.append(jnp.where(down < 2, cos2, jnp.where(down < 4, sin2, third)))
-                here = jnp.logical_xor(point < table_ref[g, 7, r : r + 1], second)
+                here = jnp.logical_xor(point < table_ref[g, 7, 2 * r : 2 * r + 1], second)
                 for _ in range(2, size // SUBLANES):
                     series.append(twice * series[-1] - series[-2])
                 full = jnp.concatenate(series, axis=0).astype(jnp.bfloat16)
@@ -588,34 +593,45 @@
             part_ref[base, i * size_out : (i + 1) * size_out, :] = jnp.concatenate(
                 whole, axis=0
             ).astype(jnp.bfloat16)
-
-        tall = block * per * span // 2
-
-        def copy(i, half):
-            start = (2 * i + half) * tall
-            size = min(tall, rows_out * span - start)
+            if tail and i == tail_group % block:
+                tail_ref[...] = whole[tail_at // SUBLANES].astype(jnp.bfloat16)
+
+        size_out = per * span
+        cuts = [piece * block // PIECES for piece in range(PIECES + 1)]
+
+        def copy(i, piece):
+            start, end = cuts[piece] * size_out, cuts[piece + 1] * size_out
+            place = i * block * size_out
+            size = min(end, total - tail - place) - start
             return pltpu.make_async_copy(
-                part_ref.at[i, pl.ds(half * tall, size), :],
-                o_hbm.at[pl.ds(start, size), :],
-                sems.at[2 * i + half],
+                part_ref.at[i, pl.ds(start, size), :],
+                o_hbm.at[pl.ds(place + start, size), :],
+                sems.at[PIECES * i + piece],
             )
 
         def step(base, carry):
-            for half in range(2):
-                for i in range(half * block // 2, (half + 1) * block // 2):
+            for piece in range(PIECES):
+                for i in range(cuts[piece], cuts[piece + 1]):
                     one_group(base, i, base * block + i)
                 for i in range(STEPS):
 
                     @pl.when(base == i)
-                    def _(i=i, half=half):
-                        copy(i, half).start()
+                    def _(i=i, piece=piece):
+                        copy(i, piece).start()
 
             return carry
 
         lax.fori_loop(0, STEPS, step, 0)
+        if tail:
+            rest = pltpu.make_async_copy(
+                tail_ref, o_hbm.at[pl.ds(total - tail, tail), :], sems.at[PIECES * STEPS]
+            )
+            rest.start()
         for i in range(STEPS):
-            for half in range(2):
-                copy(i, half).wait()
+            for piece in range(PIECES):
+                copy(i, piece).wait()
+        if tail:
+            rest.wait()
 
     return pl.pallas_call(
         kernel,
@@ -626,7 +642,8 @@
             pltpu.VMEM((tiles, kinds, LANES), jnp.float32),
             pltpu.VMEM((groups, 2, SUBLANES, LANES), jnp.float32),
             pltpu.VMEM((STEPS, block * per * span, LANES), jnp.bfloat16),
-            pltpu.SemaphoreType.DMA((2 * STEPS,)),
+            pltpu.VMEM((SUBLANES, LANES), jnp.bfloat16),
+            pltpu.SemaphoreType.DMA((PIECES * STEPS + 1,)),
         ],
         compiler_params=params(16 * 1024 * 1024),
         cost_estimate=cost(8 * 10**9, 3 * 10**6),

time: 42.6 us -> 41.6 us (0.977)
  Pallas kernels: 8.25 us -> 6.85 us
  waiting for transfers between devices: 1.09 us -> 1.88 us
    pallas_call x1, Pallas kernels: 2.59 us -> 1.8 us  [prepare(): pl.pallas_call(kernel, out_shape=(jax.ShapeDtypeStruct((rows, degrees_all...]
    ppermute x7, waiting for transfers between devices: 1.09 us -> 1.88 us  [across(): return lax.ppermute(x, 'lev', [(j, j ^ bits) for j in range(levels)])]
    pallas_call x1, Pallas kernels: 3.32 us -> 2.72 us  [grid_values(): pl.pallas_call(kernel, out_shape=jax.ShapeDtypeStruct((rows_out * span, L...]
  transfers between devices with their start and end apart: 7 -> 7, of which waited for: 2 -> 2; matrix products, arithmetic and copies ran while one was open for 0% -> 0% of each run, Pallas kernels for 14% -> 11%
where the time goes in v5:
time: 41.6 us; the launch traced here: 41.4 us
  blocking collectives  23.6 us (57%)
  starting transfers between devices  8.26 us (20%)
  Pallas kernels  6.85 us (16%)
  waiting for transfers between devices  1.88 us (5%)
  between operations  0.75 us (2%)
    all_to_all x2, blocking collectives, same_core(): lax.all_to_all(x, ('wave', 'lev'), 0, 0, tiled=True, axis_index_groups=gr...  23.6 us
    ppermute x7, starting transfers between devices, across(): return lax.ppermute(x, 'lev', [(j, j ^ bits) for j in range(levels)])  8.26 us
    pallas_call x1, Pallas kernels, grid_values(): pl.pallas_call(kernel, out_shape=jax.ShapeDtypeStruct((rows_out * span, L...  2.72 us
    ppermute x7, waiting for transfers between devices, across(): return lax.ppermute(x, 'lev', [(j, j ^ bits) for j in range(levels)])  1.88 us
    pallas_call x1, Pallas kernels, prepare(): pl.pallas_call(kernel, out_shape=(jax.ShapeDtypeStruct((rows, degrees_all...  1.8 us
  transfers between devices with their start and end apart: 7, of which 2 were waited for; matrix products, arithmetic and copies ran while one was open for 0% of the time, Pallas kernels for 11%

profile of v5, /device:TPU:0, one launch (start us, length us, event | category | flops | bytes accessed | tf_op | source)
XLA Modules:
  0.0 41.4 jit_solution(14021036263681796122)
XLA Ops:
  0.6 0.5 %collective-permute-start.3 = (bf16[320,1200]{1,0:T(8,128)(2,1)}, bf16[320,1200]{1,0:T(8,128)(2,1)S(1)}, u32[]{:S(2)}, u32[]{:S(2)}) collective-permute-start(bf16[320,1200]{1,0:T(8,128)(2,1)} %bitcast.20), channel_id=1, source_target_pairs={{0,1},{1,0},{2,3},{3,2},{4,5},{5,4},{6,7},{7,6},{8,9},{9,8},{10,11... | collective-permute-start | bytes 2304008 | tf_op jit(solution)/shard_map/ppermute | solution.py:731
  1.1 0.0 copy-start
  1.2 0.0 copy-start.1
  1.2 0.0 copy-start.2
  1.2 0.0 copy-start.3
  1.2 0.0 copy-start.4
  1.2 3.5 %collective-permute-start.2 = (bf16[2,2,1280]{2,1,0:T(2,128)(2,1)}, bf16[2,2,1280]{2,1,0:T(2,128)(2,1)S(1)}, u32[]{:S(2)}, u32[]{:S(2)}) collective-permute-start(bf16[2,2,1280]{2,1,0:T(2,128)(2,1)} %bitcast.23), channel_id=1, source_target_pairs={{0,6},{1,7},{2,4},{3,5},{4,2},{5,3},{6,0},{7,1},{8,14},{9,15},{10,... | collective-permute-start | bytes 30728 | tf_op jit(solution)/shard_map/ppermute | solution.py:731
  4.7 0.5 %collective-permute-start.1 = (bf16[2,2,1280]{2,1,0:T(2,128)(2,1)}, bf16[2,2,1280]{2,1,0:T(2,128)(2,1)S(1)}, u32[]{:S(2)}, u32[]{:S(2)}) collective-permute-start(bf16[2,2,1280]{2,1,0:T(2,128)(2,1)} %bitcast.24), channel_id=1, source_target_pairs={{0,4},{1,5},{2,6},{3,7},{4,0},{5,1},{6,2},{7,3},{8,12},{9,13},{10,... | collective-permute-start | bytes 30728 | tf_op jit(solution)/shard_map/ppermute | solution.py:731
  5.2 0.1 collective-permute-start
  5.4 0.0 copy-done
  5.4 0.0 copy-done.1
  5.4 0.0 copy-done.2
  5.4 0.0 copy-done.3
  5.4 0.0 copy-done.4
  5.4 1.8 %prepare.1 = (f32[8,1280]{1,0:T(8,128)S(1)}, f32[8,1280]{1,0:T(8,128)S(1)}, f32[2,8,160]{2,1,0:T(8,128)S(1)}, bf16[320,1200]{1,0:T(8,128)(2,1)S(1)}, f32[38,8,8,...) custom-call(s32[1200]{0:T(1024)S(1)} %copy-done.2, ...), custom_call_target="tpu_custom_call" | custom-call | flops 3000000000 | bytes 1000000 | tf_op jit(solution)/shard_map/prepare/pallas_call | solution.py:466
  7.2 0.0 collective-permute-done.2.refs_2_
  7.2 1.4 %collective-permute-done.1.refs_1_ = bf16[2,2,1280]{2,1,0:T(2,128)(2,1)S(1)} collective-permute-done((bf16[2,2,1280]{2,1,0:T(2,128)(2,1)}, bf16[2,2,1280]{2,1,0:T(2,128)(2,1)S(1)}, u32[]{:S(2)}, u32[]{:S(2)}) %collective-permute-start.1) | collective-permute-done | bytes 10272 | tf_op jit(solution)/shard_map/ppermute | solution.py:731
  8.6 0.5 %collective-permute-done.refs_0_ = bf16[2,2,1280]{2,1,0:T(2,128)(2,1)S(1)} collective-permute-done((bf16[2,2,1280]{2,1,0:T(2,128)(2,1)}, bf16[2,2,1280]{2,1,0:T(2,128)(2,1)S(1)}, u32[]{:S(2)}, u32[]{:S(2)}) %collective-permute-start) | collective-permute-done | bytes 10272 | tf_op jit(solution)/shard_map/ppermute | solution.py:731
  9.1 0.0 collective-permute-done.3.refs_4_.other_ref
  9.1 0.6 %partial_fourier.1 = bf16[4,4,8,384]{3,2,1,0:T(8,128)(2,1)S(1)} custom-call(f32[8,1280]{1,0:T(8,128)S(1)} %get-tuple-element.17.first_ref, f32[8,1280]{1,0:T(8,128)S(1)} %get-tuple-element.18.factor_ref, bf16[2,2,1280]{2,1,0:T(2,128)(2,1)S(1)} %collective-permute-done.refs_0_, bf16[2,2,1280]{2,1,0:T(2,128)(2,1)S(1)} %collective-permute-done.1.refs_1_, ...), custom_call_target="tpu_custom_call" | custom-call | flops 1000000000 | bytes 2000000 | tf_op jit(solution)/shard_map/partial_fourier/pallas_call | solution.py:221
  9.7 13.4 %all_to_all.10.x_ref = bf16[16,8,384]{2,1,0:T(8,128)(2,1)S(1)} all-to-all(bf16[16,8,384]{2,1,0:T(8,128)(2,1)S(1)} %bitcast.19), channel_id=1, replica_groups={{0,2,4,6,8,10,12,14,16,18,20,22,24,26,28,30},{1,3,5,7,9,11,13,15,17,19,..., dimensions={0} | all-to-all | bytes 196608 | tf_op jit(solution)/shard_map/all_to_all | solution.py:735
  23.1 0.2 quadratic.1
  23.4 10.3 %all_to_all.11 = bf16[16,8,384]{2,1,0:T(8,128)(2,1)S(1)} all-to-all(bf16[16,8,384]{2,1,0:T(8,128)(2,1)S(1)} %get-tuple-element.24), channel_id=1, replica_groups={{0,2,4,6,8,10,12,14,16,18,20,22,24,26,28,30},{1,3,5,7,9,11,13,15,17,19,..., dimensions={0} | all-to-all | bytes 196608 | tf_op jit(solution)/shard_map/all_to_all | solution.py:735
  33.6 0.8 %direct.1 = (f32[8,160]{1,0:T(8,128)S(1)}, f32[8,160]{1,0:T(8,128)S(1)}, f32[8,160]{1,0:T(8,128)S(1)}, f32[8,160]{1,0:T(8,128)S(1)}) custom-call(bf16[4,32,384]{2,1,0:T(8,128)(2,1)S(1)} %bitcast.18, f32[2,8,160]{2,1,0:T(8,128)S(1)} %get-tuple-element.25.factor_ref, bf16[320,1200]{1,0:T(8,128)(2,1)S(1)} %bitcast.22, ...), custom_call_target="tpu_custom_call" | custom-call | flops 1000000000 | bytes 2000000 | tf_op jit(solution)/shard_map/direct/pallas_call | solution.py:680
  34.4 1.0 %collective-permute-start.4 = (f32[8,160]{1,0:T(8,128)S(1)}, f32[8,160]{1,0:T(8,128)S(1)}, u32[]{:S(2)}, u32[]{:S(2)}) collective-permute-start(f32[8,160]{1,0:T(8,128)S(1)} %get-tuple-element.27), channel_id=1, source_target_pairs={{0,2},{1,3},{2,0},{3,1},{4,6},{5,7},{6,4},{7,5},{8,10},{9,11},{10,... | collective-permute-start | bytes 15368 | tf_op jit(solution)/shard_map/ppermute | solution.py:731
  35.4 0.3 collective-permute-start.5
  35.7 2.2 %collective-permute-start.6 = (f32[8,160]{1,0:T(8,128)S(1)}, f32[8,160]{1,0:T(8,128)S(1)}, u32[]{:S(2)}, u32[]{:S(2)}) collective-permute-start(f32[8,160]{1,0:T(8,128)S(1)} %get-tuple-element.29), channel_id=1, source_target_pairs={{0,6},{1,7},{2,4},{3,5},{4,2},{5,3},{6,0},{7,1},{8,14},{9,15},{10,... | collective-permute-start | bytes 15368 | tf_op jit(solution)/shard_map/ppermute | solution.py:731
  37.9 2.7 %grid_values.1 = bf16[11400,128]{1,0:T(8,128)(2,1)} custom-call(f32[128,128]{1,0:T(8,128)S(1)} %get-tuple-element.22.fourier_ref, f32[38,8,8,128]{3,2,1,0:T(8,128)S(1)} %get-tuple-element.23.table_ref), custom_call_target="tpu_custom_call" | custom-call | flops 8000000000 | bytes 3000000 | tf_op jit(solution)/shard_map/grid_values/pallas_call | solution.py:636
  40.7 0.0 collective-permute-done.4.refs_1_
  40.7 0.0 collective-permute-done.5.refs_2_
  40.7 0.0 collective-permute-done.6.refs_3_
  40.7 0.7 %join_degrees.1 = f32[2,2,1280]{2,1,0:T(2,128)} custom-call(f32[8,160]{1,0:T(8,128)S(1)} %get-tuple-element.26.refs_0_, f32[8,160]{1,0:T(8,128)S(1)} %collective-permute-done.4.refs_1_, f32[8,160]{1,0:T(8,128)S(1)} %collective-permute-done.5.refs_2_, f32[8,160]{1,0:T(8,128)S(1)} %collective-permute-done.6.refs_3_), custom_call_target="tpu_custom_call" | custom-call | tf_op jit(solution)/shard_map/join_degrees/pallas_call | solution.py:709
  (1 shorter events, 0.0 us)
Async XLA Ops:
  0.6 8.5 %collective-permute-start.3 = (bf16[320,1200]{1,0:T(8,128)(2,1)}, bf16[320,1200]{1,0:T(8,128)(2,1)S(1)}, u32[]{:S(2)}, u32[]{:S(2)}) collective-permute-start(bf16[320,1200]{1,0:T(8,128)(2,1)} %bitcast.20), channel_id=1, source_target_pairs={{0,1},{1,0},{2,3},{3,2},{4,5},{5,4},{6,7},{7,6},{8,9},{9,8},{10,11... | collective-permute-start | bytes 2304008 | tf_op jit(solution)/shard_map/ppermute | solution.py:731
  1.1 4.2 %copy-start = (bf16[2,160,1200]{2,1,0:T(8,128)(2,1)S(1)}, bf16[2,160,1200]{2,1,0:T(8,128)(2,1)}, u32[]{:S(2)}) copy-start(bf16[2,160,1200]{2,1,0:T(8,128)(2,1)} %param.6) | copy-start | bytes 2304004
  1.2 4.2 %copy-start.1 = (bf16[2,1,2,1280]{3,2,1,0:T(2,128)(2,1)S(1)}, bf16[2,1,2,1280]{3,2,1,0:T(2,128)(2,1)}, u32[]{:S(2)}) copy-start(bf16[2,1,2,1280]{3,2,1,0:T(2,128)(2,1)} %param.5) | copy-start | bytes 30724
  1.2 4.2 %copy-start.2 = (s32[1200]{0:T(1024)S(1)}, s32[1200]{0:T(1024)}, u32[]{:S(2)}) copy-start(s32[1200]{0:T(1024)} %len_row_ref.1) | copy-start | bytes 14404
  1.2 4.3 %copy-start.3 = (f32[1200]{0:T(1024)S(1)}, f32[1200]{0:T(1024)}, u32[]{:S(2)}) copy-start(f32[1200]{0:T(1024)} %weight_row_ref.1) | copy-start | bytes 14404
  1.2 4.3 %copy-start.4 = (s32[8]{0:T(128)S(1)}, s32[8]{0:T(128)}, u32[]{:S(2)}) copy-start(s32[8]{0:T(128)} %map_ref.1) | copy-start | bytes 100
  1.2 6.1 %collective-permute-start.2 = (bf16[2,2,1280]{2,1,0:T(2,128)(2,1)}, bf16[2,2,1280]{2,1,0:T(2,128)(2,1)S(1)}, u32[]{:S(2)}, u32[]{:S(2)}) collective-permute-start(bf16[2,2,1280]{2,1,0:T(2,128)(2,1)} %bitcast.23), channel_id=1, source_target_pairs={{0,6},{1,7},{2,4},{3,5},{4,2},{5,3},{6,0},{7,1},{8,14},{9,15},{10,... | collective-permute-start | bytes 30728 | tf_op jit(solution)/shard_map/ppermute | solution.py:731
  4.7 3.9 %collective-permute-start.1 = (bf16[2,2,1280]{2,1,0:T(2,128)(2,1)}, bf16[2,2,1280]{2,1,0:T(2,128)(2,1)S(1)}, u32[]{:S(2)}, u32[]{:S(2)}) collective-permute-start(bf16[2,2,1280]{2,1,0:T(2,128)(2,1)} %bitcast.24), channel_id=1, source_target_pairs={{0,4},{1,5},{2,6},{3,7},{4,0},{5,1},{6,2},{7,3},{8,12},{9,13},{10,... | collective-permute-start | bytes 30728 | tf_op jit(solution)/shard_map/ppermute | solution.py:731
  5.2 3.9 %collective-permute-start = (bf16[2,2,1280]{2,1,0:T(2,128)(2,1)}, bf16[2,2,1280]{2,1,0:T(2,128)(2,1)S(1)}, u32[]{:S(2)}, u32[]{:S(2)}) collective-permute-start(bf16[2,2,1280]{2,1,0:T(2,128)(2,1)} %bitcast.25), channel_id=1, source_target_pairs={{0,2},{1,3},{2,0},{3,1},{4,6},{5,7},{6,4},{7,5},{8,10},{9,11},{10,... | collective-permute-start | bytes 30728 | tf_op jit(solution)/shard_map/ppermute | solution.py:731
  34.4 6.3 %collective-permute-start.4 = (f32[8,160]{1,0:T(8,128)S(1)}, f32[8,160]{1,0:T(8,128)S(1)}, u32[]{:S(2)}, u32[]{:S(2)}) collective-permute-start(f32[8,160]{1,0:T(8,128)S(1)} %get-tuple-element.27), channel_id=1, source_target_pairs={{0,2},{1,3},{2,0},{3,1},{4,6},{5,7},{6,4},{7,5},{8,10},{9,11},{10,... | collective-permute-start | bytes 15368 | tf_op jit(solution)/shard_map/ppermute | solution.py:731
  35.4 5.3 %collective-permute-start.5 = (f32[8,160]{1,0:T(8,128)S(1)}, f32[8,160]{1,0:T(8,128)S(1)}, u32[]{:S(2)}, u32[]{:S(2)}) collective-permute-start(f32[8,160]{1,0:T(8,128)S(1)} %get-tuple-element.28), channel_id=1, source_target_pairs={{0,4},{1,5},{2,6},{3,7},{4,0},{5,1},{6,2},{7,3},{8,12},{9,13},{10,... | collective-permute-start | bytes 15368 | tf_op jit(solution)/shard_map/ppermute | solution.py:731
  35.7 5.0 %collective-permute-start.6 = (f32[8,160]{1,0:T(8,128)S(1)}, f32[8,160]{1,0:T(8,128)S(1)}, u32[]{:S(2)}, u32[]{:S(2)}) collective-permute-start(f32[8,160]{1,0:T(8,128)S(1)} %get-tuple-element.29), channel_id=1, source_target_pairs={{0,6},{1,7},{2,4},{3,5},{4,2},{5,3},{6,0},{7,1},{8,14},{9,15},{10,... | collective-permute-start | bytes 15368 | tf_op jit(solution)/shard_map/ppermute | solution.py:731

commit v6 on v5

--- a/solution.py
+++ b/solution.py
@@ -155,6 +155,10 @@
     return lax.axis_index("lev")
 
 
+def from_middle(count):
+    return sorted(range(count), key=lambda i: (abs(2 * i - count + 1), -i))
+
+
 def smem():
     return pl.BlockSpec(memory_space=pltpu.SMEM)
 
@@ -210,13 +214,14 @@
         total = jnp.dot(left_ref[0], panel_refs[0][...], preferred_element_type=jnp.float32)
         total += jnp.dot(left_ref[1], panel_refs[1][...], preferred_element_type=jnp.float32)
         chip = at_level() // 2
+        places = [from_middle(waves).index(j) for j in range(waves)]
         fill = jnp.zeros((rows, wide - here), jnp.float32)
         for i in range(chips):
             mine = total[i * rows : (i + 1) * rows]
             for j in range(waves):
                 value = mine[:, j * here : (j + 1) * here]
                 value = jnp.concatenate([value, fill], axis=1)
-                o_ref[j, chip ^ i] = value.astype(jnp.bfloat16)
+                o_ref[places[j], chip ^ i] = value.astype(jnp.bfloat16)
 
     return pl.pallas_call(
         kernel,
@@ -242,10 +247,10 @@
     def kernel(held_ref, x_ref, len_ref, weight_ref, g_ref, o_ref, z_ref, r_ref, s_ref):
         half = rows // 2
         z_ref[...] = jnp.zeros(z_ref.shape, jnp.float32)
-        for i in range(waves):
-            total = x_ref[i * levels].astype(jnp.float32)
+        for place, i in enumerate(from_middle(waves)):
+            total = x_ref[place * levels].astype(jnp.float32)
             for j in range(1, levels):
-                total = total + x_ref[i * levels + j].astype(jnp.float32)
+                total = total + x_ref[place * levels + j].astype(jnp.float32)
             total = total.astype(jnp.bfloat16).astype(jnp.float32)
             for h in range(2):
                 for t in range(tiles):
@@ -317,7 +322,7 @@
             at = i * 2 * SUBLANES
             r_ref[at : at + SUBLANES, :] = re
             r_ref[at + SUBLANES : at + 2 * SUBLANES, :] = im
-        for i in range(waves):
+        for place, i in enumerate(from_middle(waves)):
             for h in range(2):
                 for t in range(tiles):
                     start = i * half * SUBLANES + h * (SUBLANES // 2) + t
@@ -326,7 +331,7 @@
                     ]
             packed = s_ref[...].astype(jnp.bfloat16)
             for j in range(levels):
-                o_ref[i * levels + j] = packed
+                o_ref[place * levels + j] = packed
 
     return pl.pallas_call(
         kernel,
@@ -660,8 +665,8 @@
 
     def kernel(x_ref, factor_ref, own_ref, other_ref, *refs):
         o_refs, left_ref, all_ref = refs[:chips], refs[chips], refs[chips + 1]
-        for j in range(waves):
-            left_ref[:, j * here : (j + 1) * here] = x_ref[j, :, 0:here].astype(jnp.float32)
+        for place, j in enumerate(from_middle(waves)):
+            left_ref[:, j * here : (j + 1) * here] = x_ref[place, :, 0:here].astype(jnp.float32)
         left = left_ref[...].astype(jnp.bfloat16)
         shape = (chips, half, own)
         slot_of = lax.broadcasted_iota(jnp.int32, shape, 1) // 2
@@ -731,7 +736,10 @@
         return lax.ppermute(x, "lev", [(j, j ^ bits) for j in range(levels)])
 
     def same_core(x):
-        groups = [[j for j in range(waves * levels) if j % 2 == core] for core in range(2)]
+        groups = [
+            [wave * levels + 2 * chip + core for wave in from_middle(waves) for chip in range(chips)]
+            for core in range(2)
+        ]
         return lax.all_to_all(x, ("wave", "lev"), 0, 0, tiled=True, axis_index_groups=groups)
 
     mine = spec.reshape(slots, 2, degrees_all)

time: 41.6 us -> 39.4 us (0.947)
  blocking collectives: 23.6 us -> 21.4 us
    all_to_all x2, blocking collectives: 23.6 us -> 21.4 us  [same_core(): lax.all_to_all(x, ('wave', 'lev'), 0, 0, tiled=True, axis_index_groups=gr...]
  transfers between devices with their start and end apart: 7 -> 7, of which waited for: 2 -> 2; matrix products, arithmetic and copies ran while one was open for 0% -> 0% of each run, Pallas kernels for 11% -> 12%
where the time goes in v6:
time: 39.4 us; the launch traced here: 39.2 us
  blocking collectives  21.4 us (54%)
  starting transfers between devices  8.26 us (21%)
  Pallas kernels  6.86 us (17%)
  waiting for transfers between devices  1.88 us (5%)
  between operations  0.75 us (2%)
    all_to_all x2, blocking collectives, same_core(): lax.all_to_all(x, ('wave', 'lev'), 0, 0, tiled=True, axis_index_groups=gr...  21.4 us
    ppermute x7, starting transfers between devices, across(): return lax.ppermute(x, 'lev', [(j, j ^ bits) for j in range(levels)])  8.26 us
    pallas_call x1, Pallas kernels, grid_values(): pl.pallas_call(kernel, out_shape=jax.ShapeDtypeStruct((rows_out * span, L...  2.72 us
    ppermute x7, waiting for transfers between devices, across(): return lax.ppermute(x, 'lev', [(j, j ^ bits) for j in range(levels)])  1.88 us
    pallas_call x1, Pallas kernels, prepare(): pl.pallas_call(kernel, out_shape=(jax.ShapeDtypeStruct((rows, degrees_all...  1.8 us
  transfers between devices with their start and end apart: 7, of which 2 were waited for; matrix products, arithmetic and copies ran while one was open for 0% of the time, Pallas kernels for 12%

profile of v6, /device:TPU:0, one launch (start us, length us, event | category | flops | bytes accessed | tf_op | source)
XLA Modules:
  0.0 39.2 jit_solution(18213485982109555052)
XLA Ops:
  0.6 0.5 %collective-permute-start.3 = (bf16[320,1200]{1,0:T(8,128)(2,1)}, bf16[320,1200]{1,0:T(8,128)(2,1)S(1)}, u32[]{:S(2)}, u32[]{:S(2)}) collective-permute-start(bf16[320,1200]{1,0:T(8,128)(2,1)} %bitcast.20), channel_id=1, source_target_pairs={{0,1},{1,0},{2,3},{3,2},{4,5},{5,4},{6,7},{7,6},{8,9},{9,8},{10,11... | collective-permute-start | bytes 2304008 | tf_op jit(solution)/shard_map/ppermute | solution.py:736
  1.1 0.0 copy-start
  1.2 0.0 copy-start.1
  1.2 0.0 copy-start.2
  1.2 0.0 copy-start.3
  1.2 0.0 copy-start.4
  1.2 3.5 %collective-permute-start.2 = (bf16[2,2,1280]{2,1,0:T(2,128)(2,1)}, bf16[2,2,1280]{2,1,0:T(2,128)(2,1)S(1)}, u32[]{:S(2)}, u32[]{:S(2)}) collective-permute-start(bf16[2,2,1280]{2,1,0:T(2,128)(2,1)} %bitcast.23), channel_id=1, source_target_pairs={{0,6},{1,7},{2,4},{3,5},{4,2},{5,3},{6,0},{7,1},{8,14},{9,15},{10,... | collective-permute-start | bytes 30728 | tf_op jit(solution)/shard_map/ppermute | solution.py:736
  4.7 0.5 %collective-permute-start.1 = (bf16[2,2,1280]{2,1,0:T(2,128)(2,1)}, bf16[2,2,1280]{2,1,0:T(2,128)(2,1)S(1)}, u32[]{:S(2)}, u32[]{:S(2)}) collective-permute-start(bf16[2,2,1280]{2,1,0:T(2,128)(2,1)} %bitcast.24), channel_id=1, source_target_pairs={{0,4},{1,5},{2,6},{3,7},{4,0},{5,1},{6,2},{7,3},{8,12},{9,13},{10,... | collective-permute-start | bytes 30728 | tf_op jit(solution)/shard_map/ppermute | solution.py:736
  5.2 0.1 collective-permute-start
  5.4 0.0 copy-done
  5.4 0.0 copy-done.1
  5.4 0.0 copy-done.2
  5.4 0.0 copy-done.3
  5.4 0.0 copy-done.4
  5.4 1.8 %prepare.1 = (f32[8,1280]{1,0:T(8,128)S(1)}, f32[8,1280]{1,0:T(8,128)S(1)}, f32[2,8,160]{2,1,0:T(8,128)S(1)}, bf16[320,1200]{1,0:T(8,128)(2,1)S(1)}, f32[38,8,8,...) custom-call(s32[1200]{0:T(1024)S(1)} %copy-done.2, ...), custom_call_target="tpu_custom_call" | custom-call | flops 3000000000 | bytes 1000000 | tf_op jit(solution)/shard_map/prepare/pallas_call | solution.py:471
  7.2 0.0 collective-permute-done.2.refs_2_
  7.2 1.4 %collective-permute-done.1.refs_1_ = bf16[2,2,1280]{2,1,0:T(2,128)(2,1)S(1)} collective-permute-done((bf16[2,2,1280]{2,1,0:T(2,128)(2,1)}, bf16[2,2,1280]{2,1,0:T(2,128)(2,1)S(1)}, u32[]{:S(2)}, u32[]{:S(2)}) %collective-permute-start.1) | collective-permute-done | bytes 10272 | tf_op jit(solution)/shard_map/ppermute | solution.py:736
  8.6 0.5 %collective-permute-done.refs_0_ = bf16[2,2,1280]{2,1,0:T(2,128)(2,1)S(1)} collective-permute-done((bf16[2,2,1280]{2,1,0:T(2,128)(2,1)}, bf16[2,2,1280]{2,1,0:T(2,128)(2,1)S(1)}, u32[]{:S(2)}, u32[]{:S(2)}) %collective-permute-start) | collective-permute-done | bytes 10272 | tf_op jit(solution)/shard_map/ppermute | solution.py:736
  9.1 0.0 collective-permute-done.3.refs_4_.other_ref
  9.1 0.6 %partial_fourier.1 = bf16[4,4,8,384]{3,2,1,0:T(8,128)(2,1)S(1)} custom-call(f32[8,1280]{1,0:T(8,128)S(1)} %get-tuple-element.17.first_ref, f32[8,1280]{1,0:T(8,128)S(1)} %get-tuple-element.18.factor_ref, bf16[2,2,1280]{2,1,0:T(2,128)(2,1)S(1)} %collective-permute-done.refs_0_, bf16[2,2,1280]{2,1,0:T(2,128)(2,1)S(1)} %collective-permute-done.1.refs_1_, ...), custom_call_target="tpu_custom_call" | custom-call | flops 1000000000 | bytes 2000000 | tf_op jit(solution)/shard_map/partial_fourier/pallas_call | solution.py:226
  9.7 11.6 %all_to_all.10.x_ref = bf16[16,8,384]{2,1,0:T(8,128)(2,1)S(1)} all-to-all(bf16[16,8,384]{2,1,0:T(8,128)(2,1)S(1)} %bitcast.19), channel_id=1, replica_groups={{16,18,20,22,8,10,12,14,24,26,28,30,0,2,4,6},{17,19,21,23,9,11,13,15,25..., dimensions={0} | all-to-all | bytes 196608 | tf_op jit(solution)/shard_map/all_to_all | solution.py:743
  21.3 0.3 quadratic.1
  21.6 9.8 %all_to_all.11 = bf16[16,8,384]{2,1,0:T(8,128)(2,1)S(1)} all-to-all(bf16[16,8,384]{2,1,0:T(8,128)(2,1)S(1)} %get-tuple-element.24), channel_id=1, replica_groups={{16,18,20,22,8,10,12,14,24,26,28,30,0,2,4,6},{17,19,21,23,9,11,13,15,25..., dimensions={0} | all-to-all | bytes 196608 | tf_op jit(solution)/shard_map/all_to_all | solution.py:743
  31.4 0.8 %direct.1 = (f32[8,160]{1,0:T(8,128)S(1)}, f32[8,160]{1,0:T(8,128)S(1)}, f32[8,160]{1,0:T(8,128)S(1)}, f32[8,160]{1,0:T(8,128)S(1)}) custom-call(bf16[4,32,384]{2,1,0:T(8,128)(2,1)S(1)} %bitcast.18, f32[2,8,160]{2,1,0:T(8,128)S(1)} %get-tuple-element.25.factor_ref, bf16[320,1200]{1,0:T(8,128)(2,1)S(1)} %bitcast.22, ...), custom_call_target="tpu_custom_call" | custom-call | flops 1000000000 | bytes 2000000 | tf_op jit(solution)/shard_map/direct/pallas_call | solution.py:685
  32.1 1.0 %collective-permute-start.4 = (f32[8,160]{1,0:T(8,128)S(1)}, f32[8,160]{1,0:T(8,128)S(1)}, u32[]{:S(2)}, u32[]{:S(2)}) collective-permute-start(f32[8,160]{1,0:T(8,128)S(1)} %get-tuple-element.27), channel_id=1, source_target_pairs={{0,2},{1,3},{2,0},{3,1},{4,6},{5,7},{6,4},{7,5},{8,10},{9,11},{10,... | collective-permute-start | bytes 15368 | tf_op jit(solution)/shard_map/ppermute | solution.py:736
  33.2 0.3 collective-permute-start.5
  33.5 2.2 %collective-permute-start.6 = (f32[8,160]{1,0:T(8,128)S(1)}, f32[8,160]{1,0:T(8,128)S(1)}, u32[]{:S(2)}, u32[]{:S(2)}) collective-permute-start(f32[8,160]{1,0:T(8,128)S(1)} %get-tuple-element.29), channel_id=1, source_target_pairs={{0,6},{1,7},{2,4},{3,5},{4,2},{5,3},{6,0},{7,1},{8,14},{9,15},{10,... | collective-permute-start | bytes 15368 | tf_op jit(solution)/shard_map/ppermute | solution.py:736
  35.7 2.7 %grid_values.1 = bf16[11400,128]{1,0:T(8,128)(2,1)} custom-call(f32[128,128]{1,0:T(8,128)S(1)} %get-tuple-element.22.fourier_ref, f32[38,8,8,128]{3,2,1,0:T(8,128)S(1)} %get-tuple-element.23.table_ref), custom_call_target="tpu_custom_call" | custom-call | flops 8000000000 | bytes 3000000 | tf_op jit(solution)/shard_map/grid_values/pallas_call | solution.py:641
  38.4 0.0 collective-permute-done.4.refs_1_
  38.4 0.0 collective-permute-done.5.refs_2_
  38.5 0.0 collective-permute-done.6.refs_3_
  38.5 0.7 %join_degrees.1 = f32[2,2,1280]{2,1,0:T(2,128)} custom-call(f32[8,160]{1,0:T(8,128)S(1)} %get-tuple-element.26.refs_0_, f32[8,160]{1,0:T(8,128)S(1)} %collective-permute-done.4.refs_1_, f32[8,160]{1,0:T(8,128)S(1)} %collective-permute-done.5.refs_2_, f32[8,160]{1,0:T(8,128)S(1)} %collective-permute-done.6.refs_3_), custom_call_target="tpu_custom_call" | custom-call | tf_op jit(solution)/shard_map/join_degrees/pallas_call | solution.py:714
  (1 shorter events, 0.0 us)
Async XLA Ops:
  0.6 8.5 %collective-permute-start.3 = (bf16[320,1200]{1,0:T(8,128)(2,1)}, bf16[320,1200]{1,0:T(8,128)(2,1)S(1)}, u32[]{:S(2)}, u32[]{:S(2)}) collective-permute-start(bf16[320,1200]{1,0:T(8,128)(2,1)} %bitcast.20), channel_id=1, source_target_pairs={{0,1},{1,0},{2,3},{3,2},{4,5},{5,4},{6,7},{7,6},{8,9},{9,8},{10,11... | collective-permute-start | bytes 2304008 | tf_op jit(solution)/shard_map/ppermute | solution.py:736
  1.1 4.2 %copy-start = (bf16[2,160,1200]{2,1,0:T(8,128)(2,1)S(1)}, bf16[2,160,1200]{2,1,0:T(8,128)(2,1)}, u32[]{:S(2)}) copy-start(bf16[2,160,1200]{2,1,0:T(8,128)(2,1)} %param.6) | copy-start | bytes 2304004
  1.2 4.2 %copy-start.1 = (bf16[2,1,2,1280]{3,2,1,0:T(2,128)(2,1)S(1)}, bf16[2,1,2,1280]{3,2,1,0:T(2,128)(2,1)}, u32[]{:S(2)}) copy-start(bf16[2,1,2,1280]{3,2,1,0:T(2,128)(2,1)} %param.5) | copy-start | bytes 30724
  1.2 4.2 %copy-start.2 = (s32[1200]{0:T(1024)S(1)}, s32[1200]{0:T(1024)}, u32[]{:S(2)}) copy-start(s32[1200]{0:T(1024)} %len_row_ref.1) | copy-start | bytes 14404
  1.2 4.3 %copy-start.3 = (f32[1200]{0:T(1024)S(1)}, f32[1200]{0:T(1024)}, u32[]{:S(2)}) copy-start(f32[1200]{0:T(1024)} %weight_row_ref.1) | copy-start | bytes 14404
  1.2 4.3 %copy-start.4 = (s32[8]{0:T(128)S(1)}, s32[8]{0:T(128)}, u32[]{:S(2)}) copy-start(s32[8]{0:T(128)} %map_ref.1) | copy-start | bytes 100
  1.2 6.1 %collective-permute-start.2 = (bf16[2,2,1280]{2,1,0:T(2,128)(2,1)}, bf16[2,2,1280]{2,1,0:T(2,128)(2,1)S(1)}, u32[]{:S(2)}, u32[]{:S(2)}) collective-permute-start(bf16[2,2,1280]{2,1,0:T(2,128)(2,1)} %bitcast.23), channel_id=1, source_target_pairs={{0,6},{1,7},{2,4},{3,5},{4,2},{5,3},{6,0},{7,1},{8,14},{9,15},{10,... | collective-permute-start | bytes 30728 | tf_op jit(solution)/shard_map/ppermute | solution.py:736
  4.7 3.9 %collective-permute-start.1 = (bf16[2,2,1280]{2,1,0:T(2,128)(2,1)}, bf16[2,2,1280]{2,1,0:T(2,128)(2,1)S(1)}, u32[]{:S(2)}, u32[]{:S(2)}) collective-permute-start(bf16[2,2,1280]{2,1,0:T(2,128)(2,1)} %bitcast.24), channel_id=1, source_target_pairs={{0,4},{1,5},{2,6},{3,7},{4,0},{5,1},{6,2},{7,3},{8,12},{9,13},{10,... | collective-permute-start | bytes 30728 | tf_op jit(solution)/shard_map/ppermute | solution.py:736
  5.2 3.9 %collective-permute-start = (bf16[2,2,1280]{2,1,0:T(2,128)(2,1)}, bf16[2,2,1280]{2,1,0:T(2,128)(2,1)S(1)}, u32[]{:S(2)}, u32[]{:S(2)}) collective-permute-start(bf16[2,2,1280]{2,1,0:T(2,128)(2,1)} %bitcast.25), channel_id=1, source_target_pairs={{0,2},{1,3},{2,0},{3,1},{4,6},{5,7},{6,4},{7,5},{8,10},{9,11},{10,... | collective-permute-start | bytes 30728 | tf_op jit(solution)/shard_map/ppermute | solution.py:736
  32.1 6.3 %collective-permute-start.4 = (f32[8,160]{1,0:T(8,128)S(1)}, f32[8,160]{1,0:T(8,128)S(1)}, u32[]{:S(2)}, u32[]{:S(2)}) collective-permute-start(f32[8,160]{1,0:T(8,128)S(1)} %get-tuple-element.27), channel_id=1, source_target_pairs={{0,2},{1,3},{2,0},{3,1},{4,6},{5,7},{6,4},{7,5},{8,10},{9,11},{10,... | collective-permute-start | bytes 15368 | tf_op jit(solution)/shard_map/ppermute | solution.py:736
  33.2 5.3 %collective-permute-start.5 = (f32[8,160]{1,0:T(8,128)S(1)}, f32[8,160]{1,0:T(8,128)S(1)}, u32[]{:S(2)}, u32[]{:S(2)}) collective-permute-start(f32[8,160]{1,0:T(8,128)S(1)} %get-tuple-element.28), channel_id=1, source_target_pairs={{0,4},{1,5},{2,6},{3,7},{4,0},{5,1},{6,2},{7,3},{8,12},{9,13},{10,... | collective-permute-start | bytes 15368 | tf_op jit(solution)/shard_map/ppermute | solution.py:736
  33.5 5.0 %collective-permute-start.6 = (f32[8,160]{1,0:T(8,128)S(1)}, f32[8,160]{1,0:T(8,128)S(1)}, u32[]{:S(2)}, u32[]{:S(2)}) collective-permute-start(f32[8,160]{1,0:T(8,128)S(1)} %get-tuple-element.29), channel_id=1, source_target_pairs={{0,6},{1,7},{2,4},{3,5},{4,2},{5,3},{6,0},{7,1},{8,14},{9,15},{10,... | collective-permute-start | bytes 15368 | tf_op jit(solution)/shard_map/ppermute | solution.py:736

commit v7 on v6

--- a/solution.py
+++ b/solution.py
@@ -159,6 +159,10 @@
     return sorted(range(count), key=lambda i: (abs(2 * i - count + 1), -i))
 
 
+def turned(chips):
+    return chips // 2
+
+
 def smem():
     return pl.BlockSpec(memory_space=pltpu.SMEM)
 
@@ -221,7 +225,7 @@
             for j in range(waves):
                 value = mine[:, j * here : (j + 1) * here]
                 value = jnp.concatenate([value, fill], axis=1)
-                o_ref[places[j], chip ^ i] = value.astype(jnp.bfloat16)
+                o_ref[places[j], chip ^ i ^ turned(chips)] = value.astype(jnp.bfloat16)
 
     return pl.pallas_call(
         kernel,
@@ -680,7 +684,7 @@
                 result = jnp.where(slot_of == s, mine[:, :half] + mine[:, half:], result)
             all_ref[:, e * half : (e + 1) * half, :] = result
         for i in range(chips):
-            o_refs[i][...] = all_ref[(at_level() // 2) ^ i]
+            o_refs[i][...] = all_ref[(at_level() // 2) ^ i ^ turned(chips)]
 
     return pl.pallas_call(
         kernel,
@@ -737,7 +741,11 @@
 
     def same_core(x):
         groups = [
-            [wave * levels + 2 * chip + core for wave in from_middle(waves) for chip in range(chips)]
+            [
+                wave * levels + 2 * (chip ^ turned(chips)) + core
+                for wave in from_middle(waves)
+                for chip in range(chips)
+            ]
             for core in range(2)
         ]
         return lax.all_to_all(x, ("wave", "lev"), 0, 0, tiled=True, axis_index_groups=groups)

time: 39.4 us -> 39.2 us (level)
  blocking collectives: 21.4 us -> 20.6 us
  waiting for transfers between devices: 1.88 us -> 2.48 us
    all_to_all x2, blocking collectives: 21.4 us -> 20.6 us  [same_core(): lax.all_to_all(x, ('wave', 'lev'), 0, 0, tiled=True, axis_index_groups=gr...]
    ppermute x7, waiting for transfers between devices: 1.88 us -> 2.48 us  [across(): return lax.ppermute(x, 'lev', [(j, j ^ bits) for j in range(levels)])]
  transfers between devices with their start and end apart: 7 -> 7, of which waited for: 2 -> 3; matrix products, arithmetic and copies ran while one was open for 0% -> 0% of each run, Pallas kernels for 12% -> 12%
where the time goes in v7:
time: 39.2 us; the launch traced here: 39 us
  blocking collectives  20.6 us (53%)
  starting transfers between devices  8.26 us (21%)
  Pallas kernels  6.86 us (18%)
  waiting for transfers between devices  2.48 us (6%)
  between operations  0.74 us (2%)
    all_to_all x2, blocking collectives, same_core(): lax.all_to_all(x, ('wave', 'lev'), 0, 0, tiled=True, axis_index_groups=gr...  20.6 us
    ppermute x7, starting transfers between devices, across(): return lax.ppermute(x, 'lev', [(j, j ^ bits) for j in range(levels)])  8.26 us
    pallas_call x1, Pallas kernels, grid_values(): pl.pallas_call(kernel, out_shape=jax.ShapeDtypeStruct((rows_out * span, L...  2.72 us
    ppermute x7, waiting for transfers between devices, across(): return lax.ppermute(x, 'lev', [(j, j ^ bits) for j in range(levels)])  2.48 us
    pallas_call x1, Pallas kernels, prepare(): pl.pallas_call(kernel, out_shape=(jax.ShapeDtypeStruct((rows, degrees_all...  1.8 us
  transfers between devices with their start and end apart: 7, of which 3 were waited for; matrix products, arithmetic and copies ran while one was open for 0% of the time, Pallas kernels for 12%

profile of v7, /device:TPU:0, one launch (start us, length us, event | category | flops | bytes accessed | tf_op | source)
XLA Modules:
  0.0 39.0 jit_solution(5134179527908648471)
XLA Ops:
  0.6 0.5 %collective-permute-start.3 = (bf16[320,1200]{1,0:T(8,128)(2,1)}, bf16[320,1200]{1,0:T(8,128)(2,1)S(1)}, u32[]{:S(2)}, u32[]{:S(2)}) collective-permute-start(bf16[320,1200]{1,0:T(8,128)(2,1)} %bitcast.20), channel_id=1, source_target_pairs={{0,1},{1,0},{2,3},{3,2},{4,5},{5,4},{6,7},{7,6},{8,9},{9,8},{10,11... | collective-permute-start | bytes 2304008 | tf_op jit(solution)/shard_map/ppermute | solution.py:740
  1.1 0.0 copy-start
  1.2 0.0 copy-start.1
  1.2 0.0 copy-start.2
  1.2 0.0 copy-start.3
  1.2 0.0 copy-start.4
  1.2 3.5 %collective-permute-start.2 = (bf16[2,2,1280]{2,1,0:T(2,128)(2,1)}, bf16[2,2,1280]{2,1,0:T(2,128)(2,1)S(1)}, u32[]{:S(2)}, u32[]{:S(2)}) collective-permute-start(bf16[2,2,1280]{2,1,0:T(2,128)(2,1)} %bitcast.23), channel_id=1, source_target_pairs={{0,6},{1,7},{2,4},{3,5},{4,2},{5,3},{6,0},{7,1},{8,14},{9,15},{10,... | collective-permute-start | bytes 30728 | tf_op jit(solution)/shard_map/ppermute | solution.py:740
  4.7 0.5 %collective-permute-start.1 = (bf16[2,2,1280]{2,1,0:T(2,128)(2,1)}, bf16[2,2,1280]{2,1,0:T(2,128)(2,1)S(1)}, u32[]{:S(2)}, u32[]{:S(2)}) collective-permute-start(bf16[2,2,1280]{2,1,0:T(2,128)(2,1)} %bitcast.24), channel_id=1, source_target_pairs={{0,4},{1,5},{2,6},{3,7},{4,0},{5,1},{6,2},{7,3},{8,12},{9,13},{10,... | collective-permute-start | bytes 30728 | tf_op jit(solution)/shard_map/ppermute | solution.py:740
  5.2 0.1 collective-permute-start
  5.4 0.0 copy-done
  5.4 0.0 copy-done.1
  5.4 0.0 copy-done.2
  5.4 0.0 copy-done.3
  5.4 0.0 copy-done.4
  5.4 1.8 %prepare.1 = (f32[8,1280]{1,0:T(8,128)S(1)}, f32[8,1280]{1,0:T(8,128)S(1)}, f32[2,8,160]{2,1,0:T(8,128)S(1)}, bf16[320,1200]{1,0:T(8,128)(2,1)S(1)}, f32[38,8,8,...) custom-call(s32[1200]{0:T(1024)S(1)} %copy-done.2, ...), custom_call_target="tpu_custom_call" | custom-call | flops 3000000000 | bytes 1000000 | tf_op jit(solution)/shard_map/prepare/pallas_call | solution.py:475
  7.2 0.0 collective-permute-done.2.refs_2_
  7.2 1.4 %collective-permute-done.1.refs_1_ = bf16[2,2,1280]{2,1,0:T(2,128)(2,1)S(1)} collective-permute-done((bf16[2,2,1280]{2,1,0:T(2,128)(2,1)}, bf16[2,2,1280]{2,1,0:T(2,128)(2,1)S(1)}, u32[]{:S(2)}, u32[]{:S(2)}) %collective-permute-start.1) | collective-permute-done | bytes 10272 | tf_op jit(solution)/shard_map/ppermute | solution.py:740
  8.6 0.5 %collective-permute-done.refs_0_ = bf16[2,2,1280]{2,1,0:T(2,128)(2,1)S(1)} collective-permute-done((bf16[2,2,1280]{2,1,0:T(2,128)(2,1)}, bf16[2,2,1280]{2,1,0:T(2,128)(2,1)S(1)}, u32[]{:S(2)}, u32[]{:S(2)}) %collective-permute-start) | collective-permute-done | bytes 10272 | tf_op jit(solution)/shard_map/ppermute | solution.py:740
  9.1 0.0 collective-permute-done.3.refs_4_.other_ref
  9.1 0.6 %partial_fourier.1 = bf16[4,4,8,384]{3,2,1,0:T(8,128)(2,1)S(1)} custom-call(f32[8,1280]{1,0:T(8,128)S(1)} %get-tuple-element.17.first_ref, f32[8,1280]{1,0:T(8,128)S(1)} %get-tuple-element.18.factor_ref, bf16[2,2,1280]{2,1,0:T(2,128)(2,1)S(1)} %collective-permute-done.refs_0_, bf16[2,2,1280]{2,1,0:T(2,128)(2,1)S(1)} %collective-permute-done.1.refs_1_, ...), custom_call_target="tpu_custom_call" | custom-call | flops 1000000000 | bytes 2000000 | tf_op jit(solution)/shard_map/partial_fourier/pallas_call | solution.py:230
  9.7 10.8 %all_to_all.10.x_ref = bf16[16,8,384]{2,1,0:T(8,128)(2,1)S(1)} all-to-all(bf16[16,8,384]{2,1,0:T(8,128)(2,1)S(1)} %bitcast.19), channel_id=1, replica_groups={{20,22,16,18,12,14,8,10,28,30,24,26,4,6,0,2},{21,23,17,19,13,15,9,11,29..., dimensions={0} | all-to-all | bytes 196608 | tf_op jit(solution)/shard_map/all_to_all | solution.py:751
  20.6 0.3 quadratic.1
  20.8 9.8 %all_to_all.11 = bf16[16,8,384]{2,1,0:T(8,128)(2,1)S(1)} all-to-all(bf16[16,8,384]{2,1,0:T(8,128)(2,1)S(1)} %get-tuple-element.24), channel_id=1, replica_groups={{20,22,16,18,12,14,8,10,28,30,24,26,4,6,0,2},{21,23,17,19,13,15,9,11,29..., dimensions={0} | all-to-all | bytes 196608 | tf_op jit(solution)/shard_map/all_to_all | solution.py:751
  30.6 0.8 %direct.1 = (f32[8,160]{1,0:T(8,128)S(1)}, f32[8,160]{1,0:T(8,128)S(1)}, f32[8,160]{1,0:T(8,128)S(1)}, f32[8,160]{1,0:T(8,128)S(1)}) custom-call(bf16[4,32,384]{2,1,0:T(8,128)(2,1)S(1)} %bitcast.18, f32[2,8,160]{2,1,0:T(8,128)S(1)} %get-tuple-element.25.factor_ref, bf16[320,1200]{1,0:T(8,128)(2,1)S(1)} %bitcast.22, ...), custom_call_target="tpu_custom_call" | custom-call | flops 1000000000 | bytes 2000000 | tf_op jit(solution)/shard_map/direct/pallas_call | solution.py:689
  31.4 0.6 %collective-permute-start.4 = (f32[8,160]{1,0:T(8,128)S(1)}, f32[8,160]{1,0:T(8,128)S(1)}, u32[]{:S(2)}, u32[]{:S(2)}) collective-permute-start(f32[8,160]{1,0:T(8,128)S(1)} %get-tuple-element.27), channel_id=1, source_target_pairs={{0,2},{1,3},{2,0},{3,1},{4,6},{5,7},{6,4},{7,5},{8,10},{9,11},{10,... | collective-permute-start | bytes 15368 | tf_op jit(solution)/shard_map/ppermute | solution.py:740
  32.0 1.7 %collective-permute-start.5 = (f32[8,160]{1,0:T(8,128)S(1)}, f32[8,160]{1,0:T(8,128)S(1)}, u32[]{:S(2)}, u32[]{:S(2)}) collective-permute-start(f32[8,160]{1,0:T(8,128)S(1)} %get-tuple-element.28), channel_id=1, source_target_pairs={{0,4},{1,5},{2,6},{3,7},{4,0},{5,1},{6,2},{7,3},{8,12},{9,13},{10,... | collective-permute-start | bytes 15368 | tf_op jit(solution)/shard_map/ppermute | solution.py:740
  33.7 1.2 %collective-permute-start.6 = (f32[8,160]{1,0:T(8,128)S(1)}, f32[8,160]{1,0:T(8,128)S(1)}, u32[]{:S(2)}, u32[]{:S(2)}) collective-permute-start(f32[8,160]{1,0:T(8,128)S(1)} %get-tuple-element.29), channel_id=1, source_target_pairs={{0,6},{1,7},{2,4},{3,5},{4,2},{5,3},{6,0},{7,1},{8,14},{9,15},{10,... | collective-permute-start | bytes 15368 | tf_op jit(solution)/shard_map/ppermute | solution.py:740
  34.9 2.7 %grid_values.1 = bf16[11400,128]{1,0:T(8,128)(2,1)} custom-call(f32[128,128]{1,0:T(8,128)S(1)} %get-tuple-element.22.fourier_ref, f32[38,8,8,128]{3,2,1,0:T(8,128)S(1)} %get-tuple-element.23.table_ref), custom_call_target="tpu_custom_call" | custom-call | flops 8000000000 | bytes 3000000 | tf_op jit(solution)/shard_map/grid_values/pallas_call | solution.py:645
  37.7 0.0 collective-permute-done.4.refs_1_
  37.7 0.0 collective-permute-done.5.refs_2_
  37.7 0.6 %collective-permute-done.6.refs_3_ = f32[8,160]{1,0:T(8,128)S(1)} collective-permute-done((f32[8,160]{1,0:T(8,128)S(1)}, f32[8,160]{1,0:T(8,128)S(1)}, u32[]{:S(2)}, u32[]{:S(2)}) %collective-permute-start.6) | collective-permute-done | bytes 5152 | tf_op jit(solution)/shard_map/ppermute | solution.py:740
  38.3 0.7 %join_degrees.1 = f32[2,2,1280]{2,1,0:T(2,128)} custom-call(f32[8,160]{1,0:T(8,128)S(1)} %get-tuple-element.26.refs_0_, f32[8,160]{1,0:T(8,128)S(1)} %collective-permute-done.4.refs_1_, f32[8,160]{1,0:T(8,128)S(1)} %collective-permute-done.5.refs_2_, f32[8,160]{1,0:T(8,128)S(1)} %collective-permute-done.6.refs_3_), custom_call_target="tpu_custom_call" | custom-call | tf_op jit(solution)/shard_map/join_degrees/pallas_call | solution.py:718
  (1 shorter events, 0.0 us)
Async XLA Ops:
  0.6 8.5 %collective-permute-start.3 = (bf16[320,1200]{1,0:T(8,128)(2,1)}, bf16[320,1200]{1,0:T(8,128)(2,1)S(1)}, u32[]{:S(2)}, u32[]{:S(2)}) collective-permute-start(bf16[320,1200]{1,0:T(8,128)(2,1)} %bitcast.20), channel_id=1, source_target_pairs={{0,1},{1,0},{2,3},{3,2},{4,5},{5,4},{6,7},{7,6},{8,9},{9,8},{10,11... | collective-permute-start | bytes 2304008 | tf_op jit(solution)/shard_map/ppermute | solution.py:740
  1.1 4.2 %copy-start = (bf16[2,160,1200]{2,1,0:T(8,128)(2,1)S(1)}, bf16[2,160,1200]{2,1,0:T(8,128)(2,1)}, u32[]{:S(2)}) copy-start(bf16[2,160,1200]{2,1,0:T(8,128)(2,1)} %param.6) | copy-start | bytes 2304004
  1.2 4.2 %copy-start.1 = (bf16[2,1,2,1280]{3,2,1,0:T(2,128)(2,1)S(1)}, bf16[2,1,2,1280]{3,2,1,0:T(2,128)(2,1)}, u32[]{:S(2)}) copy-start(bf16[2,1,2,1280]{3,2,1,0:T(2,128)(2,1)} %param.5) | copy-start | bytes 30724
  1.2 4.2 %copy-start.2 = (s32[1200]{0:T(1024)S(1)}, s32[1200]{0:T(1024)}, u32[]{:S(2)}) copy-start(s32[1200]{0:T(1024)} %len_row_ref.1) | copy-start | bytes 14404
  1.2 4.3 %copy-start.3 = (f32[1200]{0:T(1024)S(1)}, f32[1200]{0:T(1024)}, u32[]{:S(2)}) copy-start(f32[1200]{0:T(1024)} %weight_row_ref.1) | copy-start | bytes 14404
  1.2 4.3 %copy-start.4 = (s32[8]{0:T(128)S(1)}, s32[8]{0:T(128)}, u32[]{:S(2)}) copy-start(s32[8]{0:T(128)} %map_ref.1) | copy-start | bytes 100
  1.2 6.1 %collective-permute-start.2 = (bf16[2,2,1280]{2,1,0:T(2,128)(2,1)}, bf16[2,2,1280]{2,1,0:T(2,128)(2,1)S(1)}, u32[]{:S(2)}, u32[]{:S(2)}) collective-permute-start(bf16[2,2,1280]{2,1,0:T(2,128)(2,1)} %bitcast.23), channel_id=1, source_target_pairs={{0,6},{1,7},{2,4},{3,5},{4,2},{5,3},{6,0},{7,1},{8,14},{9,15},{10,... | collective-permute-start | bytes 30728 | tf_op jit(solution)/shard_map/ppermute | solution.py:740
  4.7 3.9 %collective-permute-start.1 = (bf16[2,2,1280]{2,1,0:T(2,128)(2,1)}, bf16[2,2,1280]{2,1,0:T(2,128)(2,1)S(1)}, u32[]{:S(2)}, u32[]{:S(2)}) collective-permute-start(bf16[2,2,1280]{2,1,0:T(2,128)(2,1)} %bitcast.24), channel_id=1, source_target_pairs={{0,4},{1,5},{2,6},{3,7},{4,0},{5,1},{6,2},{7,3},{8,12},{9,13},{10,... | collective-permute-start | bytes 30728 | tf_op jit(solution)/shard_map/ppermute | solution.py:740
  5.2 3.9 %collective-permute-start = (bf16[2,2,1280]{2,1,0:T(2,128)(2,1)}, bf16[2,2,1280]{2,1,0:T(2,128)(2,1)S(1)}, u32[]{:S(2)}, u32[]{:S(2)}) collective-permute-start(bf16[2,2,1280]{2,1,0:T(2,128)(2,1)} %bitcast.25), channel_id=1, source_target_pairs={{0,2},{1,3},{2,0},{3,1},{4,6},{5,7},{6,4},{7,5},{8,10},{9,11},{10,... | collective-permute-start | bytes 30728 | tf_op jit(solution)/shard_map/ppermute | solution.py:740
  31.4 6.3 %collective-permute-start.4 = (f32[8,160]{1,0:T(8,128)S(1)}, f32[8,160]{1,0:T(8,128)S(1)}, u32[]{:S(2)}, u32[]{:S(2)}) collective-permute-start(f32[8,160]{1,0:T(8,128)S(1)} %get-tuple-element.27), channel_id=1, source_target_pairs={{0,2},{1,3},{2,0},{3,1},{4,6},{5,7},{6,4},{7,5},{8,10},{9,11},{10,... | collective-permute-start | bytes 15368 | tf_op jit(solution)/shard_map/ppermute | solution.py:740
  32.0 5.7 %collective-permute-start.5 = (f32[8,160]{1,0:T(8,128)S(1)}, f32[8,160]{1,0:T(8,128)S(1)}, u32[]{:S(2)}, u32[]{:S(2)}) collective-permute-start(f32[8,160]{1,0:T(8,128)S(1)} %get-tuple-element.28), channel_id=1, source_target_pairs={{0,4},{1,5},{2,6},{3,7},{4,0},{5,1},{6,2},{7,3},{8,12},{9,13},{10,... | collective-permute-start | bytes 15368 | tf_op jit(solution)/shard_map/ppermute | solution.py:740
  33.7 4.5 %collective-permute-start.6 = (f32[8,160]{1,0:T(8,128)S(1)}, f32[8,160]{1,0:T(8,128)S(1)}, u32[]{:S(2)}, u32[]{:S(2)}) collective-permute-start(f32[8,160]{1,0:T(8,128)S(1)} %get-tuple-element.29), channel_id=1, source_target_pairs={{0,6},{1,7},{2,4},{3,5},{4,2},{5,3},{6,0},{7,1},{8,14},{9,15},{10,... | collective-permute-start | bytes 15368 | tf_op jit(solution)/shard_map/ppermute | solution.py:740

commit v8 on v7

--- a/solution.py
+++ b/solution.py
@@ -188,7 +188,7 @@
     )()
 
 
-def partial_fourier(first, factor, others, panels, slots, waves, wide):
+def partial_fourier(first, factor, others, panels, slots, waves):
     chips = len(others) + 1
     rows, degrees_all = first.shape
     parts = rows // (2 * slots)
@@ -219,17 +219,28 @@
         total += jnp.dot(left_ref[1], panel_refs[1][...], preferred_element_type=jnp.float32)
         chip = at_level() // 2
         places = [from_middle(waves).index(j) for j in range(waves)]
-        fill = jnp.zeros((rows, wide - here), jnp.float32)
+        half, full = rows // 2, here // LANES
+        fill = jnp.zeros((half, LANES // 2 - here % LANES), jnp.float32)
         for i in range(chips):
-            mine = total[i * rows : (i + 1) * rows]
             for j in range(waves):
-                value = mine[:, j * here : (j + 1) * here]
-                value = jnp.concatenate([value, fill], axis=1)
-                o_ref[places[j], chip ^ i ^ turned(chips)] = value.astype(jnp.bfloat16)
+                tiles = []
+                for t in range(full + 1):
+                    start = j * here + t * LANES
+                    both = [
+                        total[i * rows + h * half : i * rows + (h + 1) * half, start : min(start + LANES, (j + 1) * here)]
+                        for h in range(2)
+                    ]
+                    if t == full:
+                        both = [jnp.concatenate([both[0], fill, both[1], fill], axis=1)]
+                    tiles += both
+                for k, tile in enumerate(tiles):
+                    o_ref[places[j], chip ^ i ^ turned(chips), k] = tile.astype(jnp.bfloat16)
 
     return pl.pallas_call(
         kernel,
-        out_shape=jax.ShapeDtypeStruct((waves, chips, rows, wide), jnp.bfloat16),
+        out_shape=jax.ShapeDtypeStruct(
+            (waves, chips, 2 * (here // LANES) + 1, rows // 2, LANES), jnp.bfloat16
+        ),
         in_specs=[vmem()] * (chips + 3),
         out_specs=vmem(),
         scratch_shapes=[pltpu.VMEM((2, chips * rows, depth), jnp.bfloat16)],
@@ -240,28 +251,29 @@
 
 
 def quadratic(held, parts_sum, lens, weights, waves, step):
-    sources, rows, wide = parts_sum.shape
+    sources, packs, half, _ = parts_sum.shape
     slot_count = held.shape[0]
     levels = sources // waves
     slots = slot_count // waves
-    tiles = wide // LANES
+    full = packs // 2
     top = 2 * (slot_count - 1)
     shape = (SUBLANES, LANES)
 
-    def kernel(held_ref, x_ref, len_ref, weight_ref, g_ref, o_ref, z_ref, r_ref, s_ref):
-        half = rows // 2
+    def kernel(held_ref, x_ref, len_ref, weight_ref, g_ref, o_ref, z_ref, r_ref):
         z_ref[...] = jnp.zeros(z_ref.shape, jnp.float32)
         for place, i in enumerate(from_middle(waves)):
             total = x_ref[place * levels].astype(jnp.float32)
             for j in range(1, levels):
                 total = total + x_ref[place * levels + j].astype(jnp.float32)
             total = total.astype(jnp.bfloat16).astype(jnp.float32)
-            for h in range(2):
-                for t in range(tiles):
+            for t in range(full + 1):
+                for h in range(2):
                     at = i * half * SUBLANES + h * (SUBLANES // 2) + t
-                    z_ref[pl.ds(at, half, stride=SUBLANES), :] = total[
-                        h * half : (h + 1) * half, t * LANES : (t + 1) * LANES
-                    ]
+                    if t < full:
+                        value = total[2 * t + h]
+                    else:
+                        value = pltpu.roll(total[2 * t], LANES // 2, 1) if h else total[2 * t]
+                    z_ref[pl.ds(at, half, stride=SUBLANES), :] = value
         lens_here = len_ref[...]
         kept = [
             jnp.where(lens_here > 2.0 * step * w, 1.0, 0.0) for w in range(slot_count)
@@ -327,28 +339,29 @@
             r_ref[at : at + SUBLANES, :] = re
             r_ref[at + SUBLANES : at + 2 * SUBLANES, :] = im
         for place, i in enumerate(from_middle(waves)):
-            for h in range(2):
-                for t in range(tiles):
-                    start = i * half * SUBLANES + h * (SUBLANES // 2) + t
-                    s_ref[h * half : (h + 1) * half, t * LANES : (t + 1) * LANES] = r_ref[
-                        pl.ds(start, half, stride=SUBLANES), :
-                    ]
-            packed = s_ref[...].astype(jnp.bfloat16)
-            for j in range(levels):
-                o_ref[place * levels + j] = packed
+            for t in range(full + 1):
+                both = [
+                    r_ref[pl.ds(i * half * SUBLANES + h * (SUBLANES // 2) + t, half, stride=SUBLANES), :]
+                    for h in range(2)
+                ]
+                if t == full:
+                    both = [both[0] + pltpu.roll(both[1], LANES // 2, 1)]
+                for h, value in enumerate(both):
+                    packed = value.astype(jnp.bfloat16)
+                    for j in range(levels):
+                        o_ref[place * levels + j, 2 * t + h] = packed
 
     return pl.pallas_call(
         kernel,
         out_shape=(
             jax.ShapeDtypeStruct((2 * slot_count * SUBLANES, LANES), jnp.float32),
-            jax.ShapeDtypeStruct((sources, rows, wide), jnp.bfloat16),
+            jax.ShapeDtypeStruct(parts_sum.shape, jnp.bfloat16),
         ),
         in_specs=[vmem()] * 4,
         out_specs=(vmem(), vmem()),
         scratch_shapes=[
             pltpu.VMEM((2 * slot_count * SUBLANES, LANES), jnp.float32),
             pltpu.VMEM((2 * slot_count * SUBLANES, LANES), jnp.float32),
-            pltpu.VMEM((rows, wide), jnp.float32),
         ],
         compiler_params=params(),
         name="quadratic",
@@ -661,16 +674,27 @@
 
 
 def direct(returned, factors, panels):
-    waves, tall, _ = returned.shape
+    waves, chips, packs, half, _ = returned.shape
     depth, lats = panels[0].shape
     own, here = factors.shape[2], lats // waves
-    slots, half = depth // own, factors.shape[1] // 2
-    chips = tall // (2 * half)
+    slots, full = depth // own, packs // 2
+    tall = chips * 2 * half
 
     def kernel(x_ref, factor_ref, own_ref, other_ref, *refs):
-        o_refs, left_ref, all_ref = refs[:chips], refs[chips], refs[chips + 1]
+        o_refs, left_ref, all_ref, wide_ref = refs[:chips], refs[chips], refs[chips + 1], refs[chips + 2]
         for place, j in enumerate(from_middle(waves)):
-            left_ref[:, j * here : (j + 1) * here] = x_ref[place, :, 0:here].astype(jnp.float32)
+            for i in range(chips):
+                for t in range(full + 1):
+                    for h in range(2):
+                        if t < full:
+                            value = x_ref[place, i, 2 * t + h].astype(jnp.float32)
+                        elif h == 0:
+                            value = x_ref[place, i, 2 * t].astype(jnp.float32)
+                        else:
+                            value = pltpu.roll(value, LANES // 2, 1)
+                        at = (2 * i + h) * half
+                        wide_ref[j, at : at + half, t * LANES : (t + 1) * LANES] = value
+            left_ref[:, j * here : (j + 1) * here] = wide_ref[j, :, 0:here]
         left = left_ref[...].astype(jnp.bfloat16)
         shape = (chips, half, own)
         slot_of = lax.broadcasted_iota(jnp.int32, shape, 1) // 2
@@ -694,6 +718,7 @@
         scratch_shapes=[
             pltpu.VMEM((tall, lats), jnp.float32),
             pltpu.VMEM((chips, 2 * half, own), jnp.float32),
+            pltpu.VMEM((waves, tall, (full + 1) * LANES), jnp.float32),
         ],
         compiler_params=params(),
         cost_estimate=cost(10**9, 2 * 10**6),
@@ -761,14 +786,13 @@
     rows_out = here // 2
     groups = -(-rows_out // (per * STEPS)) * STEPS
     span = 2 * (LPAD // LANES)
-    rows_here = 2 * slots * 2
     first, factor, factors, near, tables, lens, weights, held = prepare(
         cycle_len, gauss_w, wave_map, mine, panel, signs, span, step, waves, groups, wide
     )
     panels = (near, across(panel, 1))
 
-    part = partial_fourier(first, factor, others, panels, slots, waves, wide)
-    part = same_core(part.reshape(waves * chips, rows_here, wide))
+    part = partial_fourier(first, factor, others, panels, slots, waves)
+    part = same_core(part.reshape((waves * chips,) + part.shape[2:]))
     fourier, returned = quadratic(held, part, lens, weights, waves, step)
     returned = same_core(returned)
 
@@ -781,7 +805,7 @@
     values = with_layout_constraint(values, Layout(major_to_minor=(0, 1, 2)))
     grid = values.transpose(1, 0, 2).reshape(2, rows_out, 1, LPAD)
 
-    returned = returned.reshape(waves, chips * rows_here, wide)
+    returned = returned.reshape((waves, chips) + returned.shape[1:])
     pieces = direct(returned, factors, (panel, panels[1]))
     pieces = [pieces[0]] + [across(pieces[i], 2 * i) for i in range(1, chips)]
     spec_out = join_degrees(pieces, slots).reshape(slots, 1, 2, degrees_all)
@@ -796,6 +820,7 @@
         and spec.shape[1] == 1
         and 4 * spec.shape[0] == SUBLANES
         and levels > 1
+        and 0 < legendre.shape[2] * spec.shape[0] // slot_count % LANES <= LANES // 2
         and levels & (levels - 1) == 0
     )
     if fits:

time: 39.2 us -> 39.1 us (level)
  no operation moved by 1% of the time
where the time goes in v8:
time: 39.1 us; the launch traced here: 38.9 us
  blocking collectives  20.4 us (52%)
  starting transfers between devices  8.26 us (21%)
  Pallas kernels  7.02 us (18%)
  waiting for transfers between devices  2.44 us (6%)
  between operations  0.74 us (2%)
    all_to_all x2, blocking collectives, same_core(): lax.all_to_all(x, ('wave', 'lev'), 0, 0, tiled=True, axis_index_groups=gr...  20.4 us
    ppermute x7, starting transfers between devices, across(): return lax.ppermute(x, 'lev', [(j, j ^ bits) for j in range(levels)])  8.26 us
    pallas_call x1, Pallas kernels, grid_values(): pl.pallas_call(kernel, out_shape=jax.ShapeDtypeStruct((rows_out * span, L...  2.72 us
    ppermute x7, waiting for transfers between devices, across(): return lax.ppermute(x, 'lev', [(j, j ^ bits) for j in range(levels)])  2.44 us
    pallas_call x1, Pallas kernels, prepare(): pl.pallas_call(kernel, out_shape=(jax.ShapeDtypeStruct((rows, degrees_all...  1.8 us
    pallas_call x1, Pallas kernels, direct(): pl.pallas_call(kernel, out_shape=(jax.ShapeDtypeStruct((2 * half, own), j...  0.83 us
  transfers between devices with their start and end apart: 7, of which 3 were waited for; matrix products, arithmetic and copies ran while one was open for 0% of the time, Pallas kernels for 12%

profile of v8, /device:TPU:0, one launch (start us, length us, event | category | flops | bytes accessed | tf_op | source)
XLA Modules:
  0.0 38.9 jit_solution(12399683982939160336)
XLA Ops:
  0.6 0.5 %collective-permute-start.3 = (bf16[320,1200]{1,0:T(8,128)(2,1)}, bf16[320,1200]{1,0:T(8,128)(2,1)S(1)}, u32[]{:S(2)}, u32[]{:S(2)}) collective-permute-start(bf16[320,1200]{1,0:T(8,128)(2,1)} %bitcast.20), channel_id=1, source_target_pairs={{0,1},{1,0},{2,3},{3,2},{4,5},{5,4},{6,7},{7,6},{8,9},{9,8},{10,11... | collective-permute-start | bytes 2304008 | tf_op jit(solution)/shard_map/ppermute | solution.py:765
  1.1 0.0 copy-start
  1.2 0.0 copy-start.1
  1.2 0.0 copy-start.2
  1.2 0.0 copy-start.3
  1.2 0.0 copy-start.4
  1.2 3.5 %collective-permute-start.2 = (bf16[2,2,1280]{2,1,0:T(2,128)(2,1)}, bf16[2,2,1280]{2,1,0:T(2,128)(2,1)S(1)}, u32[]{:S(2)}, u32[]{:S(2)}) collective-permute-start(bf16[2,2,1280]{2,1,0:T(2,128)(2,1)} %bitcast.23), channel_id=1, source_target_pairs={{0,6},{1,7},{2,4},{3,5},{4,2},{5,3},{6,0},{7,1},{8,14},{9,15},{10,... | collective-permute-start | bytes 30728 | tf_op jit(solution)/shard_map/ppermute | solution.py:765
  4.7 0.5 %collective-permute-start.1 = (bf16[2,2,1280]{2,1,0:T(2,128)(2,1)}, bf16[2,2,1280]{2,1,0:T(2,128)(2,1)S(1)}, u32[]{:S(2)}, u32[]{:S(2)}) collective-permute-start(bf16[2,2,1280]{2,1,0:T(2,128)(2,1)} %bitcast.24), channel_id=1, source_target_pairs={{0,4},{1,5},{2,6},{3,7},{4,0},{5,1},{6,2},{7,3},{8,12},{9,13},{10,... | collective-permute-start | bytes 30728 | tf_op jit(solution)/shard_map/ppermute | solution.py:765
  5.2 0.1 collective-permute-start
  5.4 0.0 copy-done
  5.4 0.0 copy-done.1
  5.4 0.0 copy-done.2
  5.4 0.0 copy-done.3
  5.4 0.0 copy-done.4
  5.4 1.8 %prepare.1 = (f32[8,1280]{1,0:T(8,128)S(1)}, f32[8,1280]{1,0:T(8,128)S(1)}, f32[2,8,160]{2,1,0:T(8,128)S(1)}, bf16[320,1200]{1,0:T(8,128)(2,1)S(1)}, f32[38,8,8,...) custom-call(s32[1200]{0:T(1024)S(1)} %copy-done.2, ...), custom_call_target="tpu_custom_call" | custom-call | flops 3000000000 | bytes 1000000 | tf_op jit(solution)/shard_map/prepare/pallas_call | solution.py:488
  7.2 0.0 collective-permute-done.2.refs_2_
  7.2 1.4 %collective-permute-done.1.refs_1_ = bf16[2,2,1280]{2,1,0:T(2,128)(2,1)S(1)} collective-permute-done((bf16[2,2,1280]{2,1,0:T(2,128)(2,1)}, bf16[2,2,1280]{2,1,0:T(2,128)(2,1)S(1)}, u32[]{:S(2)}, u32[]{:S(2)}) %collective-permute-start.1) | collective-permute-done | bytes 10272 | tf_op jit(solution)/shard_map/ppermute | solution.py:765
  8.6 0.5 %collective-permute-done.refs_0_ = bf16[2,2,1280]{2,1,0:T(2,128)(2,1)S(1)} collective-permute-done((bf16[2,2,1280]{2,1,0:T(2,128)(2,1)}, bf16[2,2,1280]{2,1,0:T(2,128)(2,1)S(1)}, u32[]{:S(2)}, u32[]{:S(2)}) %collective-permute-start) | collective-permute-done | bytes 10272 | tf_op jit(solution)/shard_map/ppermute | solution.py:765
  9.1 0.0 collective-permute-done.3.refs_4_.other_ref
  9.1 0.6 %partial_fourier.1 = bf16[4,4,5,4,128]{4,3,2,1,0:T(4,128)(2,1)S(1)} custom-call(f32[8,1280]{1,0:T(8,128)S(1)} %get-tuple-element.17.first_ref, f32[8,1280]{1,0:T(8,128)S(1)} %get-tuple-element.18.factor_ref, bf16[2,2,1280]{2,1,0:T(2,128)(2,1)S(1)} %collective-permute-done.refs_0_, bf16[2,2,1280]{2,1,0:T(2,128)(2,1)S(1)} %collective-permute-done.1.refs_1_, ...), custom_call_target="tpu_custom_call" | custom-call | flops 1000000000 | bytes 2000000 | tf_op jit(solution)/shard_map/partial_fourier/pallas_call | solution.py:239
  9.8 10.7 %all_to_all.10.x_ref = bf16[16,5,4,128]{3,2,1,0:T(4,128)(2,1)S(1)} all-to-all(bf16[16,5,4,128]{3,2,1,0:T(4,128)(2,1)S(1)} %bitcast.19), channel_id=1, replica_groups={{20,22,16,18,12,14,8,10,28,30,24,26,4,6,0,2},{21,23,17,19,13,15,9,11,29..., dimensions={0} | all-to-all | bytes 163840 | tf_op jit(solution)/shard_map/all_to_all | solution.py:776
  20.5 0.3 quadratic.1
  20.8 9.7 %all_to_all.11 = bf16[16,5,4,128]{3,2,1,0:T(4,128)(2,1)S(1)} all-to-all(bf16[16,5,4,128]{3,2,1,0:T(4,128)(2,1)S(1)} %get-tuple-element.24), channel_id=1, replica_groups={{20,22,16,18,12,14,8,10,28,30,24,26,4,6,0,2},{21,23,17,19,13,15,9,11,29..., dimensions={0} | all-to-all | bytes 163840 | tf_op jit(solution)/shard_map/all_to_all | solution.py:776
  30.5 0.8 %direct.1 = (f32[8,160]{1,0:T(8,128)S(1)}, f32[8,160]{1,0:T(8,128)S(1)}, f32[8,160]{1,0:T(8,128)S(1)}, f32[8,160]{1,0:T(8,128)S(1)}) custom-call(bf16[4,4,5,4,128]{4,3,2,1,0:T(4,128)(2,1)S(1)} %bitcast.18, f32[2,8,160]{2,1,0:T(8,128)S(1)} %get-tuple-element.25.factor_ref, bf16[320,1200]{1,0:T(8,128)(2,1)S(1)} %bitcast.22, ...), custom_call_target="tpu_custom_call" | custom-call | flops 1000000000 | bytes 2000000 | tf_op jit(solution)/shard_map/direct/pallas_call | solution.py:713
  31.3 0.6 %collective-permute-start.4 = (f32[8,160]{1,0:T(8,128)S(1)}, f32[8,160]{1,0:T(8,128)S(1)}, u32[]{:S(2)}, u32[]{:S(2)}) collective-permute-start(f32[8,160]{1,0:T(8,128)S(1)} %get-tuple-element.27), channel_id=1, source_target_pairs={{0,2},{1,3},{2,0},{3,1},{4,6},{5,7},{6,4},{7,5},{8,10},{9,11},{10,... | collective-permute-start | bytes 15368 | tf_op jit(solution)/shard_map/ppermute | solution.py:765
  31.9 1.7 %collective-permute-start.5 = (f32[8,160]{1,0:T(8,128)S(1)}, f32[8,160]{1,0:T(8,128)S(1)}, u32[]{:S(2)}, u32[]{:S(2)}) collective-permute-start(f32[8,160]{1,0:T(8,128)S(1)} %get-tuple-element.28), channel_id=1, source_target_pairs={{0,4},{1,5},{2,6},{3,7},{4,0},{5,1},{6,2},{7,3},{8,12},{9,13},{10,... | collective-permute-start | bytes 15368 | tf_op jit(solution)/shard_map/ppermute | solution.py:765
  33.6 1.2 %collective-permute-start.6 = (f32[8,160]{1,0:T(8,128)S(1)}, f32[8,160]{1,0:T(8,128)S(1)}, u32[]{:S(2)}, u32[]{:S(2)}) collective-permute-start(f32[8,160]{1,0:T(8,128)S(1)} %get-tuple-element.29), channel_id=1, source_target_pairs={{0,6},{1,7},{2,4},{3,5},{4,2},{5,3},{6,0},{7,1},{8,14},{9,15},{10,... | collective-permute-start | bytes 15368 | tf_op jit(solution)/shard_map/ppermute | solution.py:765
  34.9 2.7 %grid_values.1 = bf16[11400,128]{1,0:T(8,128)(2,1)} custom-call(f32[128,128]{1,0:T(8,128)S(1)} %get-tuple-element.22.fourier_ref, f32[38,8,8,128]{3,2,1,0:T(8,128)S(1)} %get-tuple-element.23.table_ref), custom_call_target="tpu_custom_call" | custom-call | flops 8000000000 | bytes 3000000 | tf_op jit(solution)/shard_map/grid_values/pallas_call | solution.py:658
  37.6 0.0 collective-permute-done.4.refs_1_
  37.6 0.0 collective-permute-done.5.refs_2_
  37.6 0.6 %collective-permute-done.6.refs_3_ = f32[8,160]{1,0:T(8,128)S(1)} collective-permute-done((f32[8,160]{1,0:T(8,128)S(1)}, f32[8,160]{1,0:T(8,128)S(1)}, u32[]{:S(2)}, u32[]{:S(2)}) %collective-permute-start.6) | collective-permute-done | bytes 5152 | tf_op jit(solution)/shard_map/ppermute | solution.py:765
  38.2 0.7 %join_degrees.1 = f32[2,2,1280]{2,1,0:T(2,128)} custom-call(f32[8,160]{1,0:T(8,128)S(1)} %get-tuple-element.26.refs_0_, f32[8,160]{1,0:T(8,128)S(1)} %collective-permute-done.4.refs_1_, f32[8,160]{1,0:T(8,128)S(1)} %collective-permute-done.5.refs_2_, f32[8,160]{1,0:T(8,128)S(1)} %collective-permute-done.6.refs_3_), custom_call_target="tpu_custom_call" | custom-call | tf_op jit(solution)/shard_map/join_degrees/pallas_call | solution.py:743
  (1 shorter events, 0.0 us)
Async XLA Ops:
  0.6 8.5 %collective-permute-start.3 = (bf16[320,1200]{1,0:T(8,128)(2,1)}, bf16[320,1200]{1,0:T(8,128)(2,1)S(1)}, u32[]{:S(2)}, u32[]{:S(2)}) collective-permute-start(bf16[320,1200]{1,0:T(8,128)(2,1)} %bitcast.20), channel_id=1, source_target_pairs={{0,1},{1,0},{2,3},{3,2},{4,5},{5,4},{6,7},{7,6},{8,9},{9,8},{10,11... | collective-permute-start | bytes 2304008 | tf_op jit(solution)/shard_map/ppermute | solution.py:765
  1.1 4.2 %copy-start = (bf16[2,160,1200]{2,1,0:T(8,128)(2,1)S(1)}, bf16[2,160,1200]{2,1,0:T(8,128)(2,1)}, u32[]{:S(2)}) copy-start(bf16[2,160,1200]{2,1,0:T(8,128)(2,1)} %param.6) | copy-start | bytes 2304004
  1.2 4.2 %copy-start.1 = (bf16[2,1,2,1280]{3,2,1,0:T(2,128)(2,1)S(1)}, bf16[2,1,2,1280]{3,2,1,0:T(2,128)(2,1)}, u32[]{:S(2)}) copy-start(bf16[2,1,2,1280]{3,2,1,0:T(2,128)(2,1)} %param.5) | copy-start | bytes 30724
  1.2 4.2 %copy-start.2 = (s32[1200]{0:T(1024)S(1)}, s32[1200]{0:T(1024)}, u32[]{:S(2)}) copy-start(s32[1200]{0:T(1024)} %len_row_ref.1) | copy-start | bytes 14404
  1.2 4.3 %copy-start.3 = (f32[1200]{0:T(1024)S(1)}, f32[1200]{0:T(1024)}, u32[]{:S(2)}) copy-start(f32[1200]{0:T(1024)} %weight_row_ref.1) | copy-start | bytes 14404
  1.2 4.3 %copy-start.4 = (s32[8]{0:T(128)S(1)}, s32[8]{0:T(128)}, u32[]{:S(2)}) copy-start(s32[8]{0:T(128)} %map_ref.1) | copy-start | bytes 100
  1.2 6.1 %collective-permute-start.2 = (bf16[2,2,1280]{2,1,0:T(2,128)(2,1)}, bf16[2,2,1280]{2,1,0:T(2,128)(2,1)S(1)}, u32[]{:S(2)}, u32[]{:S(2)}) collective-permute-start(bf16[2,2,1280]{2,1,0:T(2,128)(2,1)} %bitcast.23), channel_id=1, source_target_pairs={{0,6},{1,7},{2,4},{3,5},{4,2},{5,3},{6,0},{7,1},{8,14},{9,15},{10,... | collective-permute-start | bytes 30728 | tf_op jit(solution)/shard_map/ppermute | solution.py:765
  4.7 3.9 %collective-permute-start.1 = (bf16[2,2,1280]{2,1,0:T(2,128)(2,1)}, bf16[2,2,1280]{2,1,0:T(2,128)(2,1)S(1)}, u32[]{:S(2)}, u32[]{:S(2)}) collective-permute-start(bf16[2,2,1280]{2,1,0:T(2,128)(2,1)} %bitcast.24), channel_id=1, source_target_pairs={{0,4},{1,5},{2,6},{3,7},{4,0},{5,1},{6,2},{7,3},{8,12},{9,13},{10,... | collective-permute-start | bytes 30728 | tf_op jit(solution)/shard_map/ppermute | solution.py:765
  5.2 3.9 %collective-permute-start = (bf16[2,2,1280]{2,1,0:T(2,128)(2,1)}, bf16[2,2,1280]{2,1,0:T(2,128)(2,1)S(1)}, u32[]{:S(2)}, u32[]{:S(2)}) collective-permute-start(bf16[2,2,1280]{2,1,0:T(2,128)(2,1)} %bitcast.25), channel_id=1, source_target_pairs={{0,2},{1,3},{2,0},{3,1},{4,6},{5,7},{6,4},{7,5},{8,10},{9,11},{10,... | collective-permute-start | bytes 30728 | tf_op jit(solution)/shard_map/ppermute | solution.py:765
  31.3 6.3 %collective-permute-start.4 = (f32[8,160]{1,0:T(8,128)S(1)}, f32[8,160]{1,0:T(8,128)S(1)}, u32[]{:S(2)}, u32[]{:S(2)}) collective-permute-start(f32[8,160]{1,0:T(8,128)S(1)} %get-tuple-element.27), channel_id=1, source_target_pairs={{0,2},{1,3},{2,0},{3,1},{4,6},{5,7},{6,4},{7,5},{8,10},{9,11},{10,... | collective-permute-start | bytes 15368 | tf_op jit(solution)/shard_map/ppermute | solution.py:765
  31.9 5.7 %collective-permute-start.5 = (f32[8,160]{1,0:T(8,128)S(1)}, f32[8,160]{1,0:T(8,128)S(1)}, u32[]{:S(2)}, u32[]{:S(2)}) collective-permute-start(f32[8,160]{1,0:T(8,128)S(1)} %get-tuple-element.28), channel_id=1, source_target_pairs={{0,4},{1,5},{2,6},{3,7},{4,0},{5,1},{6,2},{7,3},{8,12},{9,13},{10,... | collective-permute-start | bytes 15368 | tf_op jit(solution)/shard_map/ppermute | solution.py:765
  33.6 4.5 %collective-permute-start.6 = (f32[8,160]{1,0:T(8,128)S(1)}, f32[8,160]{1,0:T(8,128)S(1)}, u32[]{:S(2)}, u32[]{:S(2)}) collective-permute-start(f32[8,160]{1,0:T(8,128)S(1)} %get-tuple-element.29), channel_id=1, source_target_pairs={{0,6},{1,7},{2,4},{3,5},{4,2},{5,3},{6,0},{7,1},{8,14},{9,15},{10,... | collective-permute-start | bytes 15368 | tf_op jit(solution)/shard_map/ppermute | solution.py:765
